TPU v7x, 256 devices: a whole 4x4x8 slice. The times are simulated.
256 devices in a mesh: normal: 2 (over x_lo), surf: 128 (over z, y, x_hi, core).
Axes of the slice: x: 4 (x_hi: 2, x_lo: 2; x = x_hi * 2 + x_lo), y: 4, z: 8, core: 2. Of those that a mesh axis runs over, the one named last changes fastest.
Arguments:
- populations: bfloat16 [256, 32, 16384], P(None, 'normal', 'surf'), may hold values from 0.1 to 60, as said below
- absorb_table: bfloat16 [128, 256], replicated, may hold values from 2.9e-06 to 0.0031, as said below
- emit_table: bfloat16 [128, 256], replicated, may hold values from 2.9e-06 to 0.0031, as said below
- energy: float32 [128, 32, 16384], P(None, 'normal', 'surf'), may hold values from 0.2 to 1.5
- wall_source: float32 [128], replicated, may hold values from 0.5 to 2
- neighbours: int32 [16384, 4], P('surf'), may hold values from -1 to 16383, as said below
- wall_type: int32 [16384], P('surf'), may hold values from 0 to 2
Outputs:
- energy_out: float32 [128, 32, 16384], P(None, 'normal', 'surf')
Inputs may be any that keep to these rules, and one draw needn't show every extreme that they name: `neighbours`: every entry that is not -1 is another surface cell within 32 positions of the cell itself; some entry lies exactly 32 away. `populations`: populations are positive. `absorb_table`: entries are positive. `emit_table`: entries are positive.
All inputs are finite; a program needn't handle non-finite values.
Results may differ from a plain program's by a relative error of at most 0.0003.
Values sent between devices are 32-bit elements; how exact they have to be, the bound alone decides.
No kernel may reach another device: no remote copies, remote signals or barrier semaphores. Data moves between devices by JAX's collectives and lax.ppermute only.
A program may use at most 64 MiB of HBM per device.

v0:
```python
import jax
import jax.numpy as jnp
from jax import lax
from jax.sharding import PartitionSpec as P

ITERS = 2
HALO = 32


SURF_WEIGHT = 0.02


def with_halo(block, sides, width):
    for axis, dim in sides:
        count = lax.axis_size(axis)
        forward = [(i, i + 1) for i in range(count - 1)]
        backward = [(target, source) for source, target in forward]
        low = lax.ppermute(
            lax.slice_in_dim(block, block.shape[dim] - width, None, axis=dim), axis, forward
        )
        high = lax.ppermute(lax.slice_in_dim(block, 0, width, axis=dim), axis, backward)
        block = jnp.concatenate([low, block, high], axis=dim)
    return block


def passed_along(block, axis, distance):
    devices = range(lax.axis_size(axis))
    route = [(i - distance, i) for i in devices if i - distance in devices]
    return lax.ppermute(block, axis, route)


def face_value(left, right):
    return 2.0 / (3.0 * (left + right))


def eliminate(lower_rows, diag_rows, upper_rows):
    pivots = []
    carried = []
    for position in range(len(diag_rows)):
        if position == 0:
            denominator = diag_rows[0]
        else:
            denominator = diag_rows[position] - lower_rows[position] * carried[position - 1]
        pivot = 1.0 / denominator
        pivots.append(pivot)
        carried.append(upper_rows[position] * pivot)
    return (pivots, carried)


def substitute(lower_rows, pivots, carried, values):
    forward = []
    for position in range(len(pivots)):
        if position == 0:
            forward.append(values[0] * pivots[0])
        else:
            forward.append(
                (values[position] - lower_rows[position] * forward[position - 1]) * pivots[position]
            )
    solved = [forward[-1]]
    for position in range(len(pivots) - 2, -1, -1):
        solved.insert(0, forward[position] - carried[position] * solved[0])
    return solved


def body(populations, absorb_table, emit_table, energy, wall_source, neighbours, wall_type):
    level_count, row_count, cell_count = populations.shape
    group_count = absorb_table.shape[0]
    flat = populations.reshape(level_count, row_count * cell_count)
    kappa = jnp.dot(absorb_table, flat, preferred_element_type=jnp.float32).reshape(
        group_count, row_count, cell_count
    )
    emission = jnp.dot(emit_table, flat, preferred_element_type=jnp.float32).reshape(
        group_count, row_count, cell_count
    )
    depth = lax.axis_size("normal")
    level_index = lax.axis_index("normal")
    first_block = level_index == 0
    last_block = level_index == depth - 1
    row_ids = lax.broadcasted_iota(jnp.int32, (1, row_count, 1), 1)
    wall_row = first_block & (row_ids == 0)
    outer_row = last_block & (row_ids == row_count - 1)
    rimmed = with_halo(kappa, (("normal", 1),), 1)
    faces = face_value(rimmed[:, :-1, :], rimmed[:, 1:, :])
    lower = jnp.where(wall_row, 0.0, -faces[:, :-1, :])
    upper = jnp.where(outer_row, 0.0, -faces[:, 1:, :])
    wide = with_halo(jnp.stack([kappa, energy]), (("surf", 3),), HALO)
    offset = lax.axis_index("surf") * cell_count - HALO
    valid = neighbours >= 0
    places = jnp.where(valid, neighbours - offset, 0)
    couples = []
    for slot in range(4):
        nearby = jnp.take(wide[0], places[:, slot], axis=2)
        couples.append(jnp.where(valid[:, slot], SURF_WEIGHT * face_value(kappa, nearby), 0.0))
    wall_weight = jnp.where(wall_type == 0, 0.5, jnp.where(wall_type == 1, 0.25, 0.0)).astype(
        jnp.float32
    )
    boundary = jnp.where(wall_row, wall_weight[None, None, :], 0.0) + jnp.where(outer_row, 0.5, 0.0)
    diag = kappa - lower - upper + (couples[0] + couples[1] + couples[2] + couples[3]) + boundary
    wall_rhs = jnp.where(wall_row, wall_weight[None, None, :] * wall_source[:, None, None], 0.0)
    lower_rows = [lower[:, position, :] for position in range(row_count)]
    diag_rows = [diag[:, position, :] for position in range(row_count)]
    upper_rows = [upper[:, position, :] for position in range(row_count)]
    inner = row_count - 1
    pivots, carried = eliminate(lower_rows[:inner], diag_rows[:inner], upper_rows[:inner])
    alpha = substitute(lower_rows, pivots, carried, [-lower_rows[0]] + [0.0] * (inner - 1))
    beta = substitute(lower_rows, pivots, carried, [0.0] * (inner - 1) + [-upper_rows[inner - 1]])
    coupling_next = passed_along(jnp.stack([alpha[0], beta[0]]), "normal", -1)
    end_lower = lower_rows[inner]
    end_upper = upper_rows[inner]
    reduced_lower = end_lower * alpha[inner - 1]
    reduced_diag = diag_rows[inner] + end_lower * beta[inner - 1] + end_upper * coupling_next[0]
    reduced_upper = end_upper * coupling_next[1]
    multipliers = []
    segment_lower, segment_diag, segment_upper = (reduced_lower, reduced_diag, reduced_upper)
    distance = 1
    while distance < depth:
        packed = jnp.stack([segment_lower, segment_diag, segment_upper])
        below = passed_along(packed, "normal", distance)
        above = passed_along(packed, "normal", -distance)
        has_below = level_index >= distance
        has_above = level_index < depth - distance
        low_factor = segment_lower / jnp.where(has_below, below[1], 1.0)
        high_factor = segment_upper / jnp.where(has_above, above[1], 1.0)
        segment_diag = segment_diag - below[2] * low_factor - above[0] * high_factor
        segment_lower = -below[0] * low_factor
        segment_upper = -above[2] * high_factor
        multipliers.append((distance, low_factor, high_factor))
        distance = distance * 2
    current = energy
    energy_wide = wide[1]
    for step in range(ITERS):
        if step > 0:
            energy_wide = with_halo(current, (("surf", 2),), HALO)
        gathered = (
            couples[0] * jnp.take(energy_wide, places[:, 0], axis=2)
            + couples[1] * jnp.take(energy_wide, places[:, 1], axis=2)
            + couples[2] * jnp.take(energy_wide, places[:, 2], axis=2)
            + couples[3] * jnp.take(energy_wide, places[:, 3], axis=2)
        )
        rhs = emission + gathered + wall_rhs
        rhs_rows = [rhs[:, position, :] for position in range(row_count)]
        particular = substitute(lower_rows, pivots, carried, rhs_rows[:inner])
        value_next = passed_along(particular[0], "normal", -1)
        reduced_rhs = rhs_rows[inner] - end_lower * particular[inner - 1] - end_upper * value_next
        segment_rhs = reduced_rhs
        distance, low_factor, high_factor = multipliers[0]
        below_rhs = passed_along(segment_rhs, "normal", distance)
        above_rhs = passed_along(segment_rhs, "normal", -distance)
        segment_rhs = segment_rhs - below_rhs * low_factor - above_rhs * high_factor
        own_last = segment_rhs / segment_diag
        previous = passed_along(own_last, "normal", 1)
        new_rows = [
            particular[position] + alpha[position] * previous + beta[position] * own_last
            for position in range(inner)
        ]
        current = jnp.stack(new_rows + [own_last], axis=1)
    return current


def solution(mesh):
    return jax.shard_map(
        body,
        mesh=mesh,
        in_specs=(
            P(None, "normal", "surf"),
            P(),
            P(),
            P(None, "normal", "surf"),
            P(),
            P("surf", None),
            P("surf"),
        ),
        out_specs=P(None, "normal", "surf"),
        check_vma=False,
    )
```

profile of v0, /device:TPU:128, one launch (start us, length us, event | category | flops | bytes accessed | tf_op | source)
XLA Modules:
  0.0 171.6 jit_solution(2782537313716826184)
XLA Ops:
  0.0 1.6 fusion.2
  2.0 1.3 collective-permute-start.3
  3.3 4.5 %collective-permute-start.2 = (f32[128,1,128]{0,2,1:T(8,128)S(1)}, f32[128,1,128]{0,2,1:T(8,128)S(1)}, u32[]{:S(2)}, u32[]{:S(2)}) collective-permute-start(f32[128,1,128]{0,2,1:T(8,128)S(1)} %get-tuple-element.160), channel_id=1, source_target_pairs={{0,128},{1,129},{2,130},{3,131},{4,132},{5,133},{6,134},{7,135},{8... | collective-permute-start | bytes 196616 | tf_op jit(solution)/shard_map/ppermute | solution.py:18
  8.0 0.7 copy.14
  8.7 1.8 %copy.13 = f32[128,16,128]{0,1,2:T(8,128)S(1)} copy(f32[128,16,128]{2,1,0:T(8,128)} %param.12) | data formatting | bytes 2097152 | tf_op args[3]
  10.6 1.1 pad_maximum_fusion.3
  11.7 1.9 %collective-permute-start = (f32[2,128,16,32]{1,2,3,0:T(8,128)}, f32[2,128,16,32]{1,2,3,0:T(8,128)}, u32[]{:S(2)}, u32[]{:S(2)}) collective-permute-start(f32[2,128,16,32]{1,2,3,0:T(8,128)} %get-tuple-element.153), channel_id=1, source_target_pairs={{0,1},{1,2},{2,3},{3,4},{4,5},{5,6},{6,7},{7,8},{8,9},{9,10},{10,1... | collective-permute-start | bytes 1572872 | tf_op jit(solution)/shard_map/ppermute | solution.py:18
  13.6 9.4 %collective-permute-start.1 = (f32[2,128,16,32]{1,2,3,0:T(8,128)}, f32[2,128,16,32]{1,2,3,0:T(8,128)}, u32[]{:S(2)}, u32[]{:S(2)}) collective-permute-start(f32[2,128,16,32]{1,2,3,0:T(8,128)} %get-tuple-element.154), channel_id=1, source_target_pairs={{1,0},{2,1},{3,2},{4,3},{5,4},{6,5},{7,6},{8,7},{9,8},{10,9},{11,1... | collective-permute-start | bytes 1572872 | tf_op jit(solution)/shard_map/ppermute | solution.py:21
  25.4 2.5 %copy.99 = bf16[32,8,16,128]{3,1,2,0:T(8,128)(2,1)} copy(bf16[32,8,16,128]{3,2,1,0:T(8,128)(2,1)} %bitcast.1639) | data formatting | bytes 2097152
  27.9 2.3 %copy.11 = bf16[2048,256]{1,0:T(8,128)(2,1)} copy(bf16[2048,256]{0,1:T(8,128)(2,1)} %bitcast.1641) | data formatting | bytes 2097152 | tf_op jit(solution)/shard_map/dot_general | solution.py:72
  30.2 0.7 broadcast_multiply_fusion
  30.9 1.3 pad_clamp_fusion
  32.2 1.2 fusion.1
  33.4 1.4 pad_maximum_fusion
  35.0 1.8 %gather_fusion.6 = f32[128,128,16]{1,2,0:T(8,128)} fusion(f32[128,16,192]{0,1,2:T(8,128)S(1)} %get-tuple-element.151, s32[1024]{0:T(1024)} %get-tuple-element.173), kind=kCustom, calls=%fused_computation.6.clone | custom fusion | bytes 2097664 | tf_op jit(solution)/shard_map/jit(_take)/gather | solution.py:92
  36.8 1.9 %gather_fusion.4 = f32[128,128,16]{1,2,0:T(8,128)} fusion(f32[128,16,192]{0,1,2:T(8,128)S(1)} %get-tuple-element.151, s32[1024]{0:T(1024)} %get-tuple-element.174), kind=kCustom, calls=%fused_computation.4.clone | custom fusion | bytes 2097664 | tf_op jit(solution)/shard_map/jit(_take)/gather | solution.py:92
  38.7 1.8 %gather_fusion.7 = f32[128,128,16]{1,2,0:T(8,128)} fusion(f32[128,16,192]{0,1,2:T(8,128)S(1)} %get-tuple-element.152, s32[1024]{0:T(1024)} %get-tuple-element.173), kind=kCustom, calls=%fused_computation.7.clone | custom fusion | bytes 2097664 | tf_op jit(solution)/shard_map/jit(_take)/gather | solution.py:138
  40.5 1.9 %gather_fusion.5 = f32[128,128,16]{1,2,0:T(8,128)} fusion(f32[128,16,192]{0,1,2:T(8,128)S(1)} %get-tuple-element.152, s32[1024]{0:T(1024)} %get-tuple-element.174), kind=kCustom, calls=%fused_computation.5.clone | custom fusion | bytes 2097664 | tf_op jit(solution)/shard_map/jit(_take)/gather | solution.py:137
  42.4 2.0 %gather_fusion.2 = f32[128,128,16]{1,2,0:T(8,128)} fusion(f32[128,16,192]{0,1,2:T(8,128)S(1)} %get-tuple-element.151, s32[1024]{0:T(1024)} %get-tuple-element.175), kind=kCustom, calls=%fused_computation.2.clone | custom fusion | bytes 2097664 | tf_op jit(solution)/shard_map/jit(_take)/gather | solution.py:92
  44.4 1.9 %gather_fusion.3 = f32[128,128,16]{1,2,0:T(8,128)} fusion(f32[128,16,192]{0,1,2:T(8,128)S(1)} %get-tuple-element.152, s32[1024]{0:T(1024)} %get-tuple-element.175), kind=kCustom, calls=%fused_computation.3.clone | custom fusion | bytes 2097664 | tf_op jit(solution)/shard_map/jit(_take)/gather | solution.py:136
  46.2 1.8 %gather_fusion = f32[128,128,16]{1,2,0:T(8,128)} fusion(f32[128,16,192]{0,1,2:T(8,128)S(1)} %get-tuple-element.151, s32[1024]{0:T(1024)S(1)} %get-tuple-element.176), kind=kCustom, calls=%fused_computation.clone | custom fusion | bytes 2097664 | tf_op jit(solution)/shard_map/jit(_take)/gather | solution.py:92
  48.1 1.7 %gather_fusion.1 = f32[128,128,16]{1,2,0:T(8,128)} fusion(f32[128,16,192]{0,1,2:T(8,128)S(1)} %get-tuple-element.152, s32[1024]{0:T(1024)S(1)} %get-tuple-element.176), kind=kCustom, calls=%fused_computation.1.clone | custom fusion | bytes 2097664 | tf_op jit(solution)/shard_map/jit(_take)/gather | solution.py:135
  49.9 4.7 %add_add_fusion = (f32[128,16,128]{0,2,1:T(8,128)S(1)}, f32[128,16,128]{0,2,1:T(8,128)S(1)}, f32[128,16,128]{0,2,1:T(8,128)S(1)}) fusion(f32[128,16,128]{0,2,1:T(8,128)S(1)} %bitcast.1632, f32[16,128]{1,0:T(8,128)S(1)} %select_add_fusion.2, f32[128,128,16]{1,2,0:T(8,128)} %gather_fusion, pred[128]{0:T(512)(128)(4,1)S(1)} %copy-done.144, ...), kind=kLoop, calls=%fused_computation.76 | loop fusion | flops 9175040 | bytes 10495008 | tf_op jit(solution)/shard_map/add | solution.py:98
  55.8 1.6 collective-permute-start.6
  58.9 4.6 %select_add_fusion.1 = (f32[128,16,128]{0,2,1:T(8,128)S(1)}, f32[128,16,128]{0,2,1:T(8,128)}) fusion(f32[128,128,16]{1,2,0:T(8,128)S(1)} %copy-done.52, f32[128,128,16]{1,2,0:T(8,128)S(1)} %copy-done.53, f32[128,128,16]{1,2,0:T(8,128)S(1)} %copy-done.54, f32[128,128,16]{1,2,0:T(8,128)S(1)} %copy-done.55, f32[128,128]{0,1:T(8,128)S(1)} %broadcast_multiply_fusion, ...), kind=kOutput, calls=%fused_computation.17 | convolution fusion | flops 144179200 | bytes 12715024 | tf_op jit(solution)/shard_map/dot_general | solution.py:72
  63.5 1.0 fusion.78
  64.6 1.0 fusion.244
  65.7 1.3 collective-permute-start.4
  67.1 0.7 pad_maximum_fusion.4
  67.8 1.3 collective-permute-start.9
  69.1 5.9 %collective-permute-start.7 = (f32[3,128,128]{1,2,0:T(8,128)}, f32[3,128,128]{1,2,0:T(8,128)}, u32[]{:S(2)}, u32[]{:S(2)}) collective-permute-start(f32[3,128,128]{1,2,0:T(8,128)} %pad_maximum_fusion.4), channel_id=1, source_target_pairs={{0,128},{1,129},{2,130},{3,131},{4,132},{5,133},{6,134},{7,135},{8... | collective-permute-start | bytes 589832 | tf_op jit(solution)/shard_map/ppermute | solution.py:29
  75.0 0.7 fusion.71
  75.6 1.3 collective-permute-start.8
  76.9 5.8 %collective-permute-start.5 = (f32[128,128]{0,1:T(8,128)}, f32[128,128]{0,1:T(8,128)}, u32[]{:S(2)}, u32[]{:S(2)}) collective-permute-start(f32[128,128]{0,1:T(8,128)} %fusion.71), channel_id=1, source_target_pairs={{0,128},{1,129},{2,130},{3,131},{4,132},{5,133},{6,134},{7,135},{8... | collective-permute-start | bytes 196616 | tf_op jit(solution)/shard_map/ppermute | solution.py:29
  82.7 1.6 collective-permute-done.5
  84.5 2.6 %subtract_divide_fusion.1 = (f32[128,128]{0,1:T(8,128)S(1)}, f32[128,128]{0,1:T(8,128)}, f32[128,128]{0,1:T(8,128)S(1)}, f32[128,128]{0,1:T(8,128)S(1)}, f32[128...) fusion(f32[128,128]{0,1:T(8,128)} %collective-permute-done.8, ...), kind=kLoop, calls=%fused_computation.588 | loop fusion | flops 1736704 | bytes 4128770 | tf_op jit(solution)/shard_map/div | solution.py:150
  87.1 4.3 %collective-permute-start.10 = (f32[128,128]{0,1:T(8,128)S(1)}, f32[128,128]{0,1:T(8,128)S(1)}, u32[]{:S(2)}, u32[]{:S(2)}) collective-permute-start(f32[128,128]{0,1:T(8,128)S(1)} %get-tuple-element.54), channel_id=1, source_target_pairs={{0,128},{1,129},{2,130},{3,131},{4,132},{5,133},{6,134},{7,135},{8... | collective-permute-start | bytes 196616 | tf_op jit(solution)/shard_map/ppermute | solution.py:29
  91.4 1.9 %collective-permute-done.10 = f32[128,128]{0,1:T(8,128)S(1)} collective-permute-done((f32[128,128]{0,1:T(8,128)S(1)}, f32[128,128]{0,1:T(8,128)S(1)}, u32[]{:S(2)}, u32[]{:S(2)}) %collective-permute-start.10) | collective-permute-done | bytes 65568 | tf_op jit(solution)/shard_map/ppermute | solution.py:29
  93.4 1.2 constant_dynamic-update-slice_fusion.15
  95.2 0.7 copy-done.100
  97.0 1.9 %collective-permute-start.11 = (f32[128,16,32]{0,2,1:T(8,128)S(1)}, f32[128,16,32]{0,2,1:T(8,128)S(1)}, u32[]{:S(2)}, u32[]{:S(2)}) collective-permute-start(f32[128,16,32]{0,2,1:T(8,128)S(1)} %get-tuple-element.157), channel_id=1, source_target_pairs={{0,1},{1,2},{2,3},{3,4},{4,5},{5,6},{6,7},{7,8},{8,9},{9,10},{10,1... | collective-permute-start | bytes 786440 | tf_op jit(solution)/shard_map/ppermute | solution.py:18
  99.0 9.4 %collective-permute-start.12 = (f32[128,16,32]{0,2,1:T(8,128)S(1)}, f32[128,16,32]{0,2,1:T(8,128)S(1)}, u32[]{:S(2)}, u32[]{:S(2)}) collective-permute-start(f32[128,16,32]{0,2,1:T(8,128)S(1)} %get-tuple-element.158), channel_id=1, source_target_pairs={{1,0},{2,1},{3,2},{4,3},{5,4},{6,5},{7,6},{8,7},{9,8},{10,9},{11,1... | collective-permute-start | bytes 786440 | tf_op jit(solution)/shard_map/ppermute | solution.py:21
  108.3 2.2 %collective-permute-done.11 = f32[128,16,32]{0,2,1:T(8,128)S(1)} collective-permute-done((f32[128,16,32]{0,2,1:T(8,128)S(1)}, f32[128,16,32]{0,2,1:T(8,128)S(1)}, u32[]{:S(2)}, u32[]{:S(2)}) %collective-permute-start.11) | collective-permute-done | bytes 262176 | tf_op jit(solution)/shard_map/ppermute | solution.py:18
  110.6 1.7 collective-permute-done.12
  112.3 2.1 %copy.23 = f32[128,16,192]{0,1,2:T(8,128)} copy(f32[128,16,192]{0,2,1:T(8,128)S(1)} %pad_maximum_fusion.1) | data formatting | bytes 3145728 | tf_op jit(solution)/shard_map/concatenate | solution.py:22
  114.4 3.2 %gather_fusion.11 = f32[128,128,16]{1,2,0:T(8,128)} fusion(f32[128,16,192]{0,1,2:T(8,128)} %copy.23, s32[1024]{0:T(1024)} %get-tuple-element.173), kind=kCustom, calls=%fused_computation.11.clone | custom fusion | bytes 2097664 | tf_op jit(solution)/shard_map/jit(_take)/gather | solution.py:138
  117.6 3.2 %gather_fusion.10 = f32[128,128,16]{1,2,0:T(8,128)} fusion(f32[128,16,192]{0,1,2:T(8,128)} %copy.23, s32[1024]{0:T(1024)} %get-tuple-element.174), kind=kCustom, calls=%fused_computation.10.clone | custom fusion | bytes 2097664 | tf_op jit(solution)/shard_map/jit(_take)/gather | solution.py:137
  120.7 3.2 %gather_fusion.9 = f32[128,128,16]{1,2,0:T(8,128)} fusion(f32[128,16,192]{0,1,2:T(8,128)} %copy.23, s32[1024]{0:T(1024)} %get-tuple-element.175), kind=kCustom, calls=%fused_computation.9.clone | custom fusion | bytes 2097664 | tf_op jit(solution)/shard_map/jit(_take)/gather | solution.py:136
  123.9 3.0 %gather_fusion.8 = f32[128,128,16]{1,2,0:T(8,128)} fusion(f32[128,16,192]{0,1,2:T(8,128)} %copy.23, s32[1024]{0:T(1024)S(1)} %get-tuple-element.176), kind=kCustom, calls=%fused_computation.8.clone | custom fusion | bytes 2097664 | tf_op jit(solution)/shard_map/jit(_take)/gather | solution.py:135
  127.1 7.3 %select_add_fusion = f32[128,16,128]{0,2,1:T(8,128)S(1)} fusion(f32[128,16,128]{0,2,1:T(8,128)} %get-tuple-element.172, f32[128,128,16]{1,2,0:T(8,128)} %gather_fusion.11, f32[128,128,16]{1,2,0:T(8,128)} %gather_fusion.10, f32[128,128,16]{1,2,0:T(8,128)} %gather_fusion.9, f32[128,128,16]{1,2,0:T(8,128)} %gather_fusion.8, f32[128,128]{0,1:T(8,128)} %copy-done.141, ...), kind=kLoop, calls=%fused_computation.16 | loop fusion | flops 9961472 | bytes 11600912 | tf_op jit(solution)/shard_map/add | solution.py:140
  134.6 1.2 fusion.38
  136.0 1.1 fusion.245
  137.1 1.4 collective-permute-start.13
  138.6 4.9 %collective-permute-done.13 = f32[128,128]{0,1:T(8,128)S(1)} collective-permute-done((f32[128,128]{0,1:T(8,128)S(1)}, f32[128,128]{0,1:T(8,128)S(1)}, u32[]{:S(2)}, u32[]{:S(2)}) %collective-permute-start.13) | collective-permute-done | bytes 65568 | tf_op jit(solution)/shard_map/ppermute | solution.py:29
  143.5 1.4 collective-permute-start.15
  144.9 4.5 %collective-permute-start.14 = (f32[128,128]{0,1:T(8,128)S(1)}, f32[128,128]{0,1:T(8,128)S(1)}, u32[]{:S(2)}, u32[]{:S(2)}) collective-permute-start(f32[128,128]{0,1:T(8,128)S(1)} %fusion.32), channel_id=1, source_target_pairs={{0,128},{1,129},{2,130},{3,131},{4,132},{5,133},{6,134},{7,135},{8... | collective-permute-start | bytes 196616 | tf_op jit(solution)/shard_map/ppermute | solution.py:29
  149.8 1.6 collective-permute-done.14
  151.4 4.4 %collective-permute-start.16 = (f32[128,128]{0,1:T(8,128)S(1)}, f32[128,128]{0,1:T(8,128)S(1)}, u32[]{:S(2)}, u32[]{:S(2)}) collective-permute-start(f32[128,128]{0,1:T(8,128)S(1)} %subtract_divide_fusion), channel_id=1, source_target_pairs={{0,128},{1,129},{2,130},{3,131},{4,132},{5,133},{6,134},{7,135},{8... | collective-permute-start | bytes 196616 | tf_op jit(solution)/shard_map/ppermute | solution.py:29
  155.8 1.9 %collective-permute-done.16 = f32[128,128]{0,1:T(8,128)S(1)} collective-permute-done((f32[128,128]{0,1:T(8,128)S(1)}, f32[128,128]{0,1:T(8,128)S(1)}, u32[]{:S(2)}, u32[]{:S(2)}) %collective-permute-start.16) | collective-permute-done | bytes 65568 | tf_op jit(solution)/shard_map/ppermute | solution.py:29
  157.7 1.5 constant_dynamic-update-slice_fusion.31
  160.5 0.6 constant_dynamic-update-slice_fusion.28
  161.2 0.6 constant_dynamic-update-slice_fusion.27
  165.8 0.7 constant_dynamic-update-slice_fusion.20
  169.0 2.6 %copy.31 = f32[128,16,128]{2,1,0:T(8,128)} copy(f32[128,16,128]{0,2,1:T(8,128)} %constant_dynamic-update-slice_fusion.16) | data formatting | bytes 2097152 | tf_op jit(solution)/shard_map/stack | solution.py:156
  (372 shorter events, 15.3 us)
Async XLA Ops:
  0.0 57.4 %copy-start = (bf16[128,256]{1,0:T(8,128)(2,1)S(1)}, bf16[128,256]{1,0:T(8,128)(2,1)}, u32[]{:S(2)}) copy-start(bf16[128,256]{1,0:T(8,128)(2,1)} %param.11) | copy-start | bytes 196612
  2.0 30.2 %copy-start.1 = (f32[128,2048]{0,1:T(8,128)}, f32[128,2048]{0,1:T(8,128)S(1)}, u32[]{:S(2)}) copy-start(f32[128,2048]{0,1:T(8,128)S(1)} %copy.12) | copy-start | bytes 3145732
  2.0 30.2 %collective-permute-start.3 = (f32[128,1,128]{0,2,1:T(8,128)S(1)}, f32[128,1,128]{0,2,1:T(8,128)S(1)}, u32[]{:S(2)}, u32[]{:S(2)}) collective-permute-start(f32[128,1,128]{0,2,1:T(8,128)S(1)} %get-tuple-element.159), channel_id=1, source_target_pairs={{128,0},{129,1},{130,2},{131,3},{132,4},{133,5},{134,6},{135,7},{1... | collective-permute-start | bytes 196616 | tf_op jit(solution)/shard_map/ppermute | solution.py:21
  3.3 28.9 %collective-permute-start.2 = (f32[128,1,128]{0,2,1:T(8,128)S(1)}, f32[128,1,128]{0,2,1:T(8,128)S(1)}, u32[]{:S(2)}, u32[]{:S(2)}) collective-permute-start(f32[128,1,128]{0,2,1:T(8,128)S(1)} %get-tuple-element.160), channel_id=1, source_target_pairs={{0,128},{1,129},{2,130},{3,131},{4,132},{5,133},{6,134},{7,135},{8... | collective-permute-start | bytes 196616 | tf_op jit(solution)/shard_map/ppermute | solution.py:18
  10.6 12.4 %copy-start.156 = (s32[128]{0:T(128)S(1)}, s32[128]{0:T(128)}, u32[]{:S(2)}) copy-start(s32[128]{0:T(128)} %param.15) | copy-start | bytes 1540
  10.6 12.4 %copy-start.143 = (s32[128,4]{0,1:T(4,128)S(1)}, s32[128,4]{0,1:T(4,128)}, u32[]{:S(2)}) copy-start(s32[128,4]{0,1:T(4,128)} %param.14) | copy-start | bytes 6148
  11.7 21.7 %collective-permute-start = (f32[2,128,16,32]{1,2,3,0:T(8,128)}, f32[2,128,16,32]{1,2,3,0:T(8,128)}, u32[]{:S(2)}, u32[]{:S(2)}) collective-permute-start(f32[2,128,16,32]{1,2,3,0:T(8,128)} %get-tuple-element.153), channel_id=1, source_target_pairs={{0,1},{1,2},{2,3},{3,4},{4,5},{5,6},{6,7},{7,8},{8,9},{9,10},{10,1... | collective-permute-start | bytes 1572872 | tf_op jit(solution)/shard_map/ppermute | solution.py:18
  13.6 19.8 %collective-permute-start.1 = (f32[2,128,16,32]{1,2,3,0:T(8,128)}, f32[2,128,16,32]{1,2,3,0:T(8,128)}, u32[]{:S(2)}, u32[]{:S(2)}) collective-permute-start(f32[2,128,16,32]{1,2,3,0:T(8,128)} %get-tuple-element.154), channel_id=1, source_target_pairs={{1,0},{2,1},{3,2},{4,3},{5,4},{6,5},{7,6},{8,7},{9,8},{10,9},{11,1... | collective-permute-start | bytes 1572872 | tf_op jit(solution)/shard_map/ppermute | solution.py:21
  30.9 26.5 %copy-start.141 = (f32[128,128]{0,1:T(8,128)}, f32[128,128]{0,1:T(8,128)S(1)}, u32[]{:S(2)}) copy-start(f32[128,128]{0,1:T(8,128)S(1)} %broadcast_multiply_fusion) | copy-start | bytes 196612
  54.6 12.4 %copy-start.3 = (f32[128,16,128]{0,2,1:T(8,128)}, f32[128,16,128]{0,2,1:T(8,128)S(1)}, u32[]{:S(2)}) copy-start(f32[128,16,128]{0,2,1:T(8,128)S(1)} %get-tuple-element.140) | copy-start | bytes 3145732
  55.8 11.2 %collective-permute-start.6 = (f32[2,128,128]{1,2,0:T(8,128)S(1)}, f32[2,128,128]{1,2,0:T(8,128)S(1)}, u32[]{:S(2)}, u32[]{:S(2)}) collective-permute-start(f32[2,128,128]{1,2,0:T(8,128)S(1)} %pad_maximum_fusion.5), channel_id=1, source_target_pairs={{128,0},{129,1},{130,2},{131,3},{132,4},{133,5},{134,6},{135,7},{1... | collective-permute-start | bytes 393224 | tf_op jit(solution)/shard_map/ppermute | solution.py:29
  65.7 9.9 %copy-start.57 = (f32[128,128]{0,1:T(8,128)}, f32[128,128]{0,1:T(8,128)S(1)}, u32[]{:S(2)}) copy-start(f32[128,128]{0,1:T(8,128)S(1)} %get-tuple-element.81) | copy-start | bytes 196612
  65.7 11.2 %copy-start.139 = (f32[128,128]{0,1:T(8,128)}, f32[128,128]{0,1:T(8,128)S(1)}, u32[]{:S(2)}) copy-start(f32[128,128]{0,1:T(8,128)S(1)} %get-tuple-element.74) | copy-start | bytes 196612
  65.7 9.2 %collective-permute-start.4 = (f32[128,128]{0,1:T(8,128)S(1)}, f32[128,128]{0,1:T(8,128)S(1)}, u32[]{:S(2)}, u32[]{:S(2)}) collective-permute-start(f32[128,128]{0,1:T(8,128)S(1)} %get-tuple-element.74), channel_id=1, source_target_pairs={{128,0},{129,1},{130,2},{131,3},{132,4},{133,5},{134,6},{135,7},{1... | collective-permute-start | bytes 196616 | tf_op jit(solution)/shard_map/ppermute | solution.py:29
  67.0 9.9 %copy-start.135 = (f32[2,128,128]{1,2,0:T(8,128)}, f32[2,128,128]{1,2,0:T(8,128)S(1)}, u32[]{:S(2)}) copy-start(f32[2,128,128]{1,2,0:T(8,128)S(1)} %collective-permute-done.6) | copy-start | bytes 393220
  67.8 16.5 %collective-permute-start.9 = (f32[3,128,128]{1,2,0:T(8,128)}, f32[3,128,128]{1,2,0:T(8,128)}, u32[]{:S(2)}, u32[]{:S(2)}) collective-permute-start(f32[3,128,128]{1,2,0:T(8,128)} %pad_maximum_fusion.4), channel_id=1, source_target_pairs={{128,0},{129,1},{130,2},{131,3},{132,4},{133,5},{134,6},{135,7},{1... | collective-permute-start | bytes 589832 | tf_op jit(solution)/shard_map/ppermute | solution.py:29
  69.1 15.2 %collective-permute-start.7 = (f32[3,128,128]{1,2,0:T(8,128)}, f32[3,128,128]{1,2,0:T(8,128)}, u32[]{:S(2)}, u32[]{:S(2)}) collective-permute-start(f32[3,128,128]{1,2,0:T(8,128)} %pad_maximum_fusion.4), channel_id=1, source_target_pairs={{0,128},{1,129},{2,130},{3,131},{4,132},{5,133},{6,134},{7,135},{8... | collective-permute-start | bytes 589832 | tf_op jit(solution)/shard_map/ppermute | solution.py:29
  75.6 7.1 %collective-permute-start.8 = (f32[128,128]{0,1:T(8,128)}, f32[128,128]{0,1:T(8,128)}, u32[]{:S(2)}, u32[]{:S(2)}) collective-permute-start(f32[128,128]{0,1:T(8,128)} %fusion.71), channel_id=1, source_target_pairs={{128,0},{129,1},{130,2},{131,3},{132,4},{133,5},{134,6},{135,7},{1... | collective-permute-start | bytes 196616 | tf_op jit(solution)/shard_map/ppermute | solution.py:29
  76.9 7.3 %collective-permute-start.5 = (f32[128,128]{0,1:T(8,128)}, f32[128,128]{0,1:T(8,128)}, u32[]{:S(2)}, u32[]{:S(2)}) collective-permute-start(f32[128,128]{0,1:T(8,128)} %fusion.71), channel_id=1, source_target_pairs={{0,128},{1,129},{2,130},{3,131},{4,132},{5,133},{6,134},{7,135},{8... | collective-permute-start | bytes 196616 | tf_op jit(solution)/shard_map/ppermute | solution.py:29
  84.3 8.9 %copy-start.9 = (f32[128,128]{0,1:T(8,128)S(1)}, f32[128,128]{0,1:T(8,128)}, u32[]{:S(2)}) copy-start(f32[128,128]{0,1:T(8,128)} %copy-done.8) | copy-start | bytes 196612
  84.3 8.9 %copy-start.12 = (f32[128,1,128]{0,2,1:T(8,128)S(1)}, f32[128,1,128]{0,2,1:T(8,128)}, u32[]{:S(2)}) copy-start(f32[128,1,128]{0,2,1:T(8,128)} %copy-done.11) | copy-start | bytes 196612
  84.3 8.9 %copy-start.15 = (f32[128,128]{0,1:T(8,128)S(1)}, f32[128,128]{0,1:T(8,128)}, u32[]{:S(2)}) copy-start(f32[128,128]{0,1:T(8,128)} %copy-done.14) | copy-start | bytes 196612
  84.3 8.9 %copy-start.17 = (f32[128,128]{0,1:T(8,128)S(1)}, f32[128,128]{0,1:T(8,128)}, u32[]{:S(2)}) copy-start(f32[128,128]{0,1:T(8,128)} %get-tuple-element.84) | copy-start | bytes 196612
  84.3 8.9 %copy-start.19 = (f32[128,128]{0,1:T(8,128)S(1)}, f32[128,128]{0,1:T(8,128)}, u32[]{:S(2)}) copy-start(f32[128,128]{0,1:T(8,128)} %get-tuple-element.103) | copy-start | bytes 196612
  84.3 8.9 %copy-start.21 = (f32[128,128]{0,1:T(8,128)S(1)}, f32[128,128]{0,1:T(8,128)}, u32[]{:S(2)}) copy-start(f32[128,128]{0,1:T(8,128)} %get-tuple-element.107) | copy-start | bytes 196612
  84.4 8.9 %copy-start.23 = (f32[128,128]{0,1:T(8,128)S(1)}, f32[128,128]{0,1:T(8,128)}, u32[]{:S(2)}) copy-start(f32[128,128]{0,1:T(8,128)} %get-tuple-element.111) | copy-start | bytes 196612
  84.4 8.9 %copy-start.25 = (f32[128,128]{0,1:T(8,128)S(1)}, f32[128,128]{0,1:T(8,128)}, u32[]{:S(2)}) copy-start(f32[128,128]{0,1:T(8,128)} %get-tuple-element.115) | copy-start | bytes 196612
  84.4 8.9 %copy-start.27 = (f32[128,128]{0,1:T(8,128)S(1)}, f32[128,128]{0,1:T(8,128)}, u32[]{:S(2)}) copy-start(f32[128,128]{0,1:T(8,128)} %get-tuple-element.119) | copy-start | bytes 196612
  84.4 8.9 %copy-start.30 = (f32[128,128]{0,1:T(8,128)S(1)}, f32[128,128]{0,1:T(8,128)}, u32[]{:S(2)}) copy-start(f32[128,128]{0,1:T(8,128)} %copy-done.29) | copy-start | bytes 196612
  84.4 8.9 %copy-start.33 = (f32[128,128]{0,1:T(8,128)S(1)}, f32[128,128]{0,1:T(8,128)}, u32[]{:S(2)}) copy-start(f32[128,128]{0,1:T(8,128)} %copy-done.32) | copy-start | bytes 196612
  84.4 8.9 %copy-start.36 = (f32[128,128]{0,1:T(8,128)S(1)}, f32[128,128]{0,1:T(8,128)}, u32[]{:S(2)}) copy-start(f32[128,128]{0,1:T(8,128)} %copy-done.35) | copy-start | bytes 196612
  84.4 8.9 %copy-start.39 = (f32[128,128]{0,1:T(8,128)S(1)}, f32[128,128]{0,1:T(8,128)}, u32[]{:S(2)}) copy-start(f32[128,128]{0,1:T(8,128)} %copy-done.38) | copy-start | bytes 196612
  84.4 8.9 %copy-start.42 = (f32[128,128]{0,1:T(8,128)S(1)}, f32[128,128]{0,1:T(8,128)}, u32[]{:S(2)}) copy-start(f32[128,128]{0,1:T(8,128)} %copy-done.41) | copy-start | bytes 196612
  84.4 8.9 %copy-start.67 = (f32[128,128]{0,1:T(8,128)S(1)}, f32[128,128]{0,1:T(8,128)}, u32[]{:S(2)}) copy-start(f32[128,128]{0,1:T(8,128)} %get-tuple-element.86) | copy-start | bytes 196612
  84.4 8.9 %copy-start.140 = (f32[128,128]{0,1:T(8,128)S(1)}, f32[128,128]{0,1:T(8,128)}, u32[]{:S(2)}) copy-start(f32[128,128]{0,1:T(8,128)} %copy-done.139) | copy-start | bytes 196612
  87.1 9.9 %copy-start.44 = (f32[128,128]{0,1:T(8,128)}, f32[128,128]{0,1:T(8,128)S(1)}, u32[]{:S(2)}) copy-start(f32[128,128]{0,1:T(8,128)S(1)} %get-tuple-element.56) | copy-start | bytes 196612
  87.1 9.9 %copy-start.46 = (f32[128,128]{0,1:T(8,128)}, f32[128,128]{0,1:T(8,128)S(1)}, u32[]{:S(2)}) copy-start(f32[128,128]{0,1:T(8,128)S(1)} %get-tuple-element.65) | copy-start | bytes 196612
  87.1 6.2 %collective-permute-start.10 = (f32[128,128]{0,1:T(8,128)S(1)}, f32[128,128]{0,1:T(8,128)S(1)}, u32[]{:S(2)}, u32[]{:S(2)}) collective-permute-start(f32[128,128]{0,1:T(8,128)S(1)} %get-tuple-element.54), channel_id=1, source_target_pairs={{0,128},{1,129},{2,130},{3,131},{4,132},{5,133},{6,134},{7,135},{8... | collective-permute-start | bytes 196616 | tf_op jit(solution)/shard_map/ppermute | solution.py:29
  97.0 13.5 %collective-permute-start.11 = (f32[128,16,32]{0,2,1:T(8,128)S(1)}, f32[128,16,32]{0,2,1:T(8,128)S(1)}, u32[]{:S(2)}, u32[]{:S(2)}) collective-permute-start(f32[128,16,32]{0,2,1:T(8,128)S(1)} %get-tuple-element.157), channel_id=1, source_target_pairs={{0,1},{1,2},{2,3},{3,4},{4,5},{5,6},{6,7},{7,8},{8,9},{9,10},{10,1... | collective-permute-start | bytes 786440 | tf_op jit(solution)/shard_map/ppermute | solution.py:18
  99.0 13.2 %collective-permute-start.12 = (f32[128,16,32]{0,2,1:T(8,128)S(1)}, f32[128,16,32]{0,2,1:T(8,128)S(1)}, u32[]{:S(2)}, u32[]{:S(2)}) collective-permute-start(f32[128,16,32]{0,2,1:T(8,128)S(1)} %get-tuple-element.158), channel_id=1, source_target_pairs={{1,0},{2,1},{3,2},{4,3},{5,4},{6,5},{7,6},{8,7},{9,8},{10,9},{11,1... | collective-permute-start | bytes 786440 | tf_op jit(solution)/shard_map/ppermute | solution.py:21
  127.0 7.4 %copy-start.22 = (f32[128,128]{0,1:T(8,128)S(1)}, f32[128,128]{0,1:T(8,128)}, u32[]{:S(2)}) copy-start(f32[128,128]{0,1:T(8,128)} %get-tuple-element.107) | copy-start | bytes 196612
  127.0 7.4 %copy-start.24 = (f32[128,128]{0,1:T(8,128)S(1)}, f32[128,128]{0,1:T(8,128)}, u32[]{:S(2)}) copy-start(f32[128,128]{0,1:T(8,128)} %get-tuple-element.111) | copy-start | bytes 196612
  135.9 15.4 %copy-start.136 = (f32[128,128]{0,1:T(8,128)S(1)}, f32[128,128]{0,1:T(8,128)}, u32[]{:S(2)}) copy-start(f32[128,128]{0,1:T(8,128)} %get-tuple-element.55) | copy-start | bytes 196612
  135.9 15.4 %copy-start.137 = (f32[128,128]{0,1:T(8,128)S(1)}, f32[128,128]{0,1:T(8,128)}, u32[]{:S(2)}) copy-start(f32[128,128]{0,1:T(8,128)} %get-tuple-element.64) | copy-start | bytes 196612
  135.9 15.4 %copy-start.138 = (f32[128,128]{0,1:T(8,128)S(1)}, f32[128,128]{0,1:T(8,128)}, u32[]{:S(2)}) copy-start(f32[128,128]{0,1:T(8,128)} %get-tuple-element.73) | copy-start | bytes 196612
  135.9 21.8 %copy-start.13 = (f32[128,1,128]{0,2,1:T(8,128)S(1)}, f32[128,1,128]{0,2,1:T(8,128)}, u32[]{:S(2)}) copy-start(f32[128,1,128]{0,2,1:T(8,128)} %copy-done.11) | copy-start | bytes 196612
  135.9 21.8 %copy-start.49 = (f32[128,128]{0,1:T(8,128)S(1)}, f32[128,128]{0,1:T(8,128)}, u32[]{:S(2)}) copy-start(f32[128,128]{0,1:T(8,128)} %copy-done.48) | copy-start | bytes 196612
  135.9 21.8 %copy-start.51 = (f32[128,128]{0,1:T(8,128)S(1)}, f32[128,128]{0,1:T(8,128)}, u32[]{:S(2)}) copy-start(f32[128,128]{0,1:T(8,128)} %copy-done.50) | copy-start | bytes 196612
  137.1 22.8 %copy-start.90 = (f32[128,128]{0,1:T(8,128)S(1)}, f32[128,128]{0,1:T(8,128)}, u32[]{:S(2)}) copy-start(f32[128,128]{0,1:T(8,128)} %copy-done.89) | copy-start | bytes 196612
  137.1 22.8 %copy-start.92 = (f32[128,128]{0,1:T(8,128)S(1)}, f32[128,128]{0,1:T(8,128)}, u32[]{:S(2)}) copy-start(f32[128,128]{0,1:T(8,128)} %copy-done.91) | copy-start | bytes 196612
  137.1 23.4 %copy-start.126 = (f32[128,128]{0,1:T(8,128)S(1)}, f32[128,128]{0,1:T(8,128)}, u32[]{:S(2)}) copy-start(f32[128,128]{0,1:T(8,128)} %copy-done.125) | copy-start | bytes 196612
  137.1 23.4 %copy-start.128 = (f32[128,128]{0,1:T(8,128)S(1)}, f32[128,128]{0,1:T(8,128)}, u32[]{:S(2)}) copy-start(f32[128,128]{0,1:T(8,128)} %copy-done.127) | copy-start | bytes 196612
  137.1 24.1 %copy-start.86 = (f32[128,128]{0,1:T(8,128)S(1)}, f32[128,128]{0,1:T(8,128)}, u32[]{:S(2)}) copy-start(f32[128,128]{0,1:T(8,128)} %copy-done.85) | copy-start | bytes 196612
  137.1 24.0 %copy-start.88 = (f32[128,128]{0,1:T(8,128)S(1)}, f32[128,128]{0,1:T(8,128)}, u32[]{:S(2)}) copy-start(f32[128,128]{0,1:T(8,128)} %copy-done.87) | copy-start | bytes 196612
  137.1 6.3 %collective-permute-start.13 = (f32[128,128]{0,1:T(8,128)S(1)}, f32[128,128]{0,1:T(8,128)S(1)}, u32[]{:S(2)}, u32[]{:S(2)}) collective-permute-start(f32[128,128]{0,1:T(8,128)S(1)} %get-tuple-element.6), channel_id=1, source_target_pairs={{128,0},{129,1},{130,2},{131,3},{132,4},{133,5},{134,6},{135,7},{1... | collective-permute-start | bytes 196616 | tf_op jit(solution)/shard_map/ppermute | solution.py:29
  143.4 18.4 %copy-start.122 = (f32[128,128]{0,1:T(8,128)S(1)}, f32[128,128]{0,1:T(8,128)}, u32[]{:S(2)}) copy-start(f32[128,128]{0,1:T(8,128)} %copy-done.121) | copy-start | bytes 196612
  143.4 18.4 %copy-start.124 = (f32[128,128]{0,1:T(8,128)S(1)}, f32[128,128]{0,1:T(8,128)}, u32[]{:S(2)}) copy-start(f32[128,128]{0,1:T(8,128)} %copy-done.123) | copy-start | bytes 196612
  143.5 6.3 %collective-permute-start.15 = (f32[128,128]{0,1:T(8,128)S(1)}, f32[128,128]{0,1:T(8,128)S(1)}, u32[]{:S(2)}, u32[]{:S(2)}) collective-permute-start(f32[128,128]{0,1:T(8,128)S(1)} %fusion.32), channel_id=1, source_target_pairs={{128,0},{129,1},{130,2},{131,3},{132,4},{133,5},{134,6},{135,7},{1... | collective-permute-start | bytes 196616 | tf_op jit(solution)/shard_map/ppermute | solution.py:29
  144.9 6.4 %collective-permute-start.14 = (f32[128,128]{0,1:T(8,128)S(1)}, f32[128,128]{0,1:T(8,128)S(1)}, u32[]{:S(2)}, u32[]{:S(2)}) collective-permute-start(f32[128,128]{0,1:T(8,128)S(1)} %fusion.32), channel_id=1, source_target_pairs={{0,128},{1,129},{2,130},{3,131},{4,132},{5,133},{6,134},{7,135},{8... | collective-permute-start | bytes 196616 | tf_op jit(solution)/shard_map/ppermute | solution.py:29
  151.4 11.1 %copy-start.82 = (f32[128,128]{0,1:T(8,128)S(1)}, f32[128,128]{0,1:T(8,128)}, u32[]{:S(2)}) copy-start(f32[128,128]{0,1:T(8,128)} %copy-done.81) | copy-start | bytes 196612
  151.4 11.1 %copy-start.84 = (f32[128,128]{0,1:T(8,128)S(1)}, f32[128,128]{0,1:T(8,128)}, u32[]{:S(2)}) copy-start(f32[128,128]{0,1:T(8,128)} %copy-done.83) | copy-start | bytes 196612
  151.4 11.8 %copy-start.118 = (f32[128,128]{0,1:T(8,128)S(1)}, f32[128,128]{0,1:T(8,128)}, u32[]{:S(2)}) copy-start(f32[128,128]{0,1:T(8,128)} %copy-done.117) | copy-start | bytes 196612
  151.4 11.8 %copy-start.120 = (f32[128,128]{0,1:T(8,128)S(1)}, f32[128,128]{0,1:T(8,128)}, u32[]{:S(2)}) copy-start(f32[128,128]{0,1:T(8,128)} %copy-done.119) | copy-start | bytes 196612
  151.4 6.3 %collective-permute-start.16 = (f32[128,128]{0,1:T(8,128)S(1)}, f32[128,128]{0,1:T(8,128)S(1)}, u32[]{:S(2)}, u32[]{:S(2)}) collective-permute-start(f32[128,128]{0,1:T(8,128)S(1)} %subtract_divide_fusion), channel_id=1, source_target_pairs={{0,128},{1,129},{2,130},{3,131},{4,132},{5,133},{6,134},{7,135},{8... | collective-permute-start | bytes 196616 | tf_op jit(solution)/shard_map/ppermute | solution.py:29
  (110 other events, 281.7 us)
where the time goes:
time: 174 us; the launch traced here: 172 us
  starting transfers between devices  61.5 us (35%)
  local copies, waits for them, and re-layouts  44.5 us (26%)
  other arithmetic  41.1 us (24%)
  waiting for transfers between devices  16 us (9%)
  matrix products  6.21 us (4%)
  between operations  2.26 us (1%)
    ppermute x11, starting transfers between devices, passed_along(): return lax.ppermute(block, axis, route)  33.1 us
    ppermute x3, starting transfers between devices, with_halo(): lax.ppermute(lax.slice_in_dim(block, 0, width, axis=dim), axis, backward)  20 us
    ppermute x11, waiting for transfers between devices, passed_along(): return lax.ppermute(block, axis, route)  12.1 us
    unnamed x30, other arithmetic  12.1 us
    ppermute x3, starting transfers between devices, with_halo(): lax.ppermute(lax.slice_in_dim(block, block.shape[dim] - width, None, axis...  8.38 us
    unnamed x317, local copies, waits for them, and re-layouts  7.71 us
    gather x4, local copies, waits for them, and re-layouts, body(): nearby = jnp.take(wide[0], places[:, slot], axis=2)  7.44 us
    add x1, other arithmetic, body(): rhs = emission + gathered + wall_rhs  7.32 us
  transfers between devices with their start and end apart: 17, of which 8 were waited for; matrix products, arithmetic and copies ran while one was open for 13% of the time, Pallas kernels for 0%

commit v1 on v0

v1 whole, which is shorter than its diff:
```python
import jax
import jax.numpy as jnp
from jax import lax
from jax.experimental import pallas as pl
from jax.experimental.pallas import tpu as pltpu
from jax.sharding import PartitionSpec as P

HALO = 32
LANES = 128
SURF_WEIGHT = 0.02
FACE = 2.0 / 3.0
LIMIT = 32 * 1024 * 1024


def inverse(value):
    guess = pl.reciprocal(value, approx=True)
    return guess * (2.0 - value * guess)


def lane_ids(rows):
    return lax.broadcasted_iota(jnp.int32, (rows, LANES), 1)


def gather(value, lanes):
    return jnp.take_along_axis(value, lanes, axis=1, mode="promise_in_bounds")


def row_of(position, count):
    block = lax.axis_index("normal")
    return position + block * (count - 1 - 2 * position)


def pack_sides(planes, forward_ref, backward_ref, lead):
    groups = planes[0].shape[0]
    slot = lane_ids(groups) // HALO
    for part in range(len(planes) // 4):
        four = planes[4 * part : 4 * part + 4]
        ahead, back = [], []
        for k in range(4):
            turn = (HALO * (k + 1)) % LANES
            ahead.append(pltpu.roll(four[k], turn, 1) if turn else four[k])
            turn = HALO * (k ^ 1)
            back.append(pltpu.roll(four[k], turn, 1) if turn else four[k])
        forward = jnp.where(slot == 0, ahead[0], jnp.where(slot == 1, ahead[1], jnp.where(slot == 2, ahead[2], ahead[3])))
        backward = jnp.where(slot == 0, back[1], jnp.where(slot == 1, back[0], jnp.where(slot == 2, back[3], back[2])))
        forward_ref[lead + (part,)] = forward
        backward_ref[lead + (part,)] = backward


def local_places(neighbours_ref):
    offset = lax.axis_index("surf") * LANES
    found = neighbours_ref[...]
    return found >= 0, found - offset


def own_tables(neighbours_ref, rows):
    valid, local = local_places(neighbours_ref)
    inside = valid & (local >= 0) & (local < LANES)
    lanes = jnp.where(inside, local, 0)
    weight = jnp.where(inside, SURF_WEIGHT * FACE, 0.0)
    return [
        (
            jnp.broadcast_to(lanes[s : s + 1], (rows, LANES)),
            jnp.broadcast_to(weight[s : s + 1], (rows, LANES)),
        )
        for s in range(4)
    ]


def halo_tables(neighbours_ref, rows):
    valid, local = local_places(neighbours_ref)
    low = valid & (local < 0)
    high = valid & (local >= LANES)
    weight = jnp.where(low | high, SURF_WEIGHT * FACE, 0.0)
    tables = []
    for s in range(4):
        lanes = []
        for k in range(4):
            place = jnp.where(low, local + HALO * (k + 1), jnp.where(high, local - LANES + HALO * (k ^ 1), 0))
            lanes.append(jnp.broadcast_to(place[s : s + 1], (rows, LANES)))
        tables.append((lanes, jnp.broadcast_to(weight[s : s + 1], (rows, LANES))))
    return tables


def halo_pair(low, high):
    even = (lane_ids(low.shape[0]) // HALO) % 2 == 0
    return jnp.where(even, low, high), jnp.where(even, high, low)


def absorb_kernel(pops_ref, absorb_ref, emit_ref, energy_ref, source_ref, wall_ref, kappa_ref, emission_ref, forward_ref, backward_ref, edge_ref):
    rows, groups, cells = kappa_ref.shape
    tables = jnp.concatenate([absorb_ref[...], emit_ref[...]], axis=0)
    levels = jnp.swapaxes(pops_ref[...], 0, 1)
    for pair in range(rows // 2):
        both = jnp.concatenate([levels[2 * pair], levels[2 * pair + 1]], axis=1)
        product = jnp.dot(tables, both, preferred_element_type=jnp.float32)
        for k in range(2):
            row = row_of(2 * pair + k, rows)
            kappa_ref[row] = product[:groups, k * cells : (k + 1) * cells]
            emission_ref[row] = product[groups:, k * cells : (k + 1) * cells]

    @pl.when(lax.axis_index("normal") == 0)
    def _():
        kind = wall_ref[...]
        weight = jnp.where(kind == 0, 0.5, jnp.where(kind == 1, 0.25, 0.0))
        source = jnp.broadcast_to(source_ref[...], (groups, groups)).T
        emission_ref[0] = emission_ref[0] + source * weight

    pack_sides([kappa_ref[r] for r in range(rows)], forward_ref, backward_ref, (0,))
    pack_sides(
        [energy_ref[pl.ds(row_of(r, rows), groups, stride=rows), :] for r in range(rows)], forward_ref, backward_ref, (1,)
    )
    edge_ref[...] = kappa_ref[rows - 1]


def own_kernel(kappa_ref, emission_ref, energy_ref, neighbours_ref, wall_ref, base_ref, rhs_ref, face_ref, couple_ref):
    rows, groups, cells = kappa_ref.shape
    chunk = 32
    tables = own_tables(neighbours_ref, chunk)
    kind = wall_ref[...]
    weight = jnp.where(kind == 0, 0.5, jnp.where(kind == 1, 0.25, 0.0))
    boundary = jnp.where(lax.axis_index("normal") == 0, weight, 0.5)

    @pl.loop(0, rows)
    def _(r):
        end = jnp.where(r == 0, boundary, 0.0)
        before = jnp.maximum(r - 1, 0)
        source = row_of(r, rows)
        for part in range(groups // chunk):
            here = pl.ds(part * chunk, chunk)
            kappa = kappa_ref[r, here, :]
            energy = energy_ref[pl.ds(part * chunk * rows + source, chunk, stride=rows), :]
            total = kappa + end
            rhs = emission_ref[r, here, :]
            for s in range(4):
                lanes, factor = tables[s]
                couple = factor * inverse(kappa + gather(kappa, lanes))
                couple_ref[s, r, here, :] = couple
                total = total + couple
                rhs = rhs + couple * gather(energy, lanes)
            base_ref[r, here, :] = total
            rhs_ref[r, here, :] = rhs
            face_ref[r, here, :] = FACE * inverse(kappa_ref[before, here, :] + kappa)


def first_kernel(kappa_ref, base_ref, rhs_ref, face_ref, low_ref, high_ref, neighbours_ref, other_edge_ref, couple_ref, pivot_ref, carried_ref, solved_ref, ends_ref):
    rows, groups, cells = kappa_ref.shape
    chunk = 32
    tables = halo_tables(neighbours_ref, chunk)

    @pl.loop(0, groups // chunk)
    def _(part):
        here = pl.ds(pl.multiple_of(part * chunk, chunk), chunk)
        schur = None
        carried = None
        solved = None
        for r in range(rows):
            quad, k = divmod(r, 4)
            if k == 0:
                halo_kappa = halo_pair(low_ref[0, quad, here, :], high_ref[0, quad, here, :])
                halo_energy = halo_pair(low_ref[1, quad, here, :], high_ref[1, quad, here, :])
            kappa = kappa_ref[r, here, :]
            base = base_ref[r, here, :]
            rhs = rhs_ref[r, here, :]
            for s in range(4):
                lanes, factor = tables[s]
                couple = factor * inverse(kappa + gather(halo_kappa[k % 2], lanes[k]))
                couple_ref[s, r, here, :] = couple
                base = base + couple
                rhs = rhs + couple * gather(halo_energy[k % 2], lanes[k])
            if r > 0:
                face = face_ref[r, here, :]
                base = base + schur * carried
                rhs = rhs + face * solved
            schur = base
            if r == rows - 1:
                ends_ref[0, here, :] = schur
                ends_ref[1, here, :] = rhs
            else:
                after = face_ref[r + 1, here, :]
                pivot = inverse(schur + after)
                carried = after * pivot
                solved = rhs * pivot
                pivot_ref[r, here, :] = pivot
                carried_ref[r, here, :] = carried
                solved_ref[r, here, :] = solved


def meet_kernel(ends_ref, other_ref, edge_ref, other_edge_ref, carried_ref, solved_ref, current_ref, forward_ref, backward_ref, mix_ref):
    rows, groups, cells = current_ref.shape
    face = FACE * inverse(edge_ref[...] + other_edge_ref[...])
    own, other = ends_ref[0], other_ref[0]
    scale = inverse(own * other + face * (own + other))
    near = (other + face) * scale
    far = face * scale
    mix_ref[0] = near
    mix_ref[1] = far
    value = near * ends_ref[1] + far * other_ref[1]
    current_ref[rows - 1] = value
    planes = [value]
    for r in range(rows - 2, -1, -1):
        value = solved_ref[r] + carried_ref[r] * value
        current_ref[r] = value
    pack_sides([current_ref[r] for r in range(rows)], forward_ref, backward_ref, ())


def own_again_kernel(current_ref, emission_ref, couple_ref, neighbours_ref, rhs_ref):
    rows, groups, cells = current_ref.shape
    chunk = 32
    tables = own_tables(neighbours_ref, chunk)

    @pl.loop(0, rows)
    def _(r):
        for part in range(groups // chunk):
            here = pl.ds(part * chunk, chunk)
            current = current_ref[r, here, :]
            rhs = emission_ref[r, here, :]
            for s in range(4):
                rhs = rhs + couple_ref[s, r, here, :] * gather(current, tables[s][0])
            rhs_ref[r, here, :] = rhs


def again_kernel(rhs_ref, low_ref, high_ref, couple_ref, neighbours_ref, pivot_ref, face_ref, solved_ref, end_ref):
    rows, groups, cells = rhs_ref.shape
    chunk = 32
    tables = halo_tables(neighbours_ref, chunk)

    @pl.loop(0, groups // chunk)
    def _(part):
        here = pl.ds(pl.multiple_of(part * chunk, chunk), chunk)
        solved = None
        for r in range(rows):
            quad, k = divmod(r, 4)
            if k == 0:
                halo = halo_pair(low_ref[quad, here, :], high_ref[quad, here, :])
            rhs = rhs_ref[r, here, :]
            for s in range(4):
                rhs = rhs + couple_ref[s, r, here, :] * gather(halo[k % 2], tables[s][0][k])
            if r > 0:
                rhs = rhs + face_ref[r, here, :] * solved
            if r == rows - 1:
                end_ref[here, :] = rhs
            else:
                solved = rhs * pivot_ref[r, here, :]
                solved_ref[r, here, :] = solved


def last_kernel(end_ref, other_ref, mix_ref, carried_ref, solved_ref, out_ref):
    rows = carried_ref.shape[0]
    groups = end_ref.shape[0]
    value = mix_ref[0] * end_ref[...] + mix_ref[1] * other_ref[...]
    out_ref[pl.ds(row_of(rows - 1, rows), groups, stride=rows), :] = value
    for r in range(rows - 2, -1, -1):
        value = solved_ref[r] + carried_ref[r] * value
        out_ref[pl.ds(row_of(r, rows), groups, stride=rows), :] = value


def call(kernel, outs, *args):
    space = pl.BlockSpec(memory_space=pltpu.VMEM)
    return pl.pallas_call(
        kernel,
        out_shape=[jax.ShapeDtypeStruct(shape, jnp.float32) for shape in outs],
        in_specs=[space] * len(args),
        out_specs=[space] * len(outs),
        compiler_params=pltpu.CompilerParams(vmem_limit_bytes=LIMIT),
    )(*args)


def body(populations, absorb_table, emit_table, energy, wall_source, neighbours, wall_type):
    levels, rows, cells = populations.shape
    groups = absorb_table.shape[0]
    whole = (rows, groups, cells)
    plane = (groups, cells)
    packed = (rows // 4, groups, cells)
    count = lax.axis_size("surf")
    ahead = [(i, (i + 1) % count) for i in range(count)]
    back = [(target, source) for source, target in ahead]
    swap = [(0, 1), (1, 0)]
    lines = energy.reshape(groups * rows, cells)
    places = neighbours.T
    walls = wall_type.reshape(1, cells)
    sources = wall_source.reshape(1, groups)

    kappa, emission, forward, backward, edge = call(
        absorb_kernel,
        [whole, whole, (2,) + packed, (2,) + packed, plane],
        populations, absorb_table, emit_table, lines, sources, walls,
    )
    low = lax.ppermute(forward, "surf", ahead)
    high = lax.ppermute(backward, "surf", back)
    other_edge = lax.ppermute(edge, "normal", swap)
    base, rhs, face, own_couple = call(
        own_kernel, [whole, whole, whole, (4,) + whole], kappa, emission, lines, places, walls
    )
    halo_couple, pivot, carried, solved, ends = call(
        first_kernel,
        [(4,) + whole, whole, whole, whole, (2,) + plane],
        kappa, base, rhs, face, low, high, places, other_edge,
    )
    other_ends = lax.ppermute(ends, "normal", swap)
    current, forward, backward, mix = call(
        meet_kernel, [whole, packed, packed, (2,) + plane], ends, other_ends, edge, other_edge, carried, solved
    )
    low = lax.ppermute(forward, "surf", ahead)
    high = lax.ppermute(backward, "surf", back)
    (rhs,) = call(own_again_kernel, [whole], current, emission, own_couple, places)
    solved, end = call(again_kernel, [whole, plane], rhs, low, high, halo_couple, places, pivot, face)
    other_end = lax.ppermute(end, "normal", swap)
    (out,) = call(last_kernel, [(groups * rows, cells)], end, other_end, mix, carried, solved)
    return out.reshape(groups, rows, cells)


def solution(mesh):
    return jax.shard_map(
        body,
        mesh=mesh,
        in_specs=(
            P(None, "normal", "surf"),
            P(),
            P(),
            P(None, "normal", "surf"),
            P(),
            P("surf", None),
            P("surf"),
        ),
        out_specs=P(None, "normal", "surf"),
        check_vma=False,
    )
```

time: 174 us -> 55.8 us (0.32)
  the two profiles are of different devices: /device:TPU:128 before, /device:TPU:127 now
where the time goes in v1:
time: 55.8 us; the launch traced here: 55.4 us
  waiting for transfers between devices  23.4 us (42%)
  Pallas kernels  16.2 us (29%)
  starting transfers between devices  8.49 us (15%)
  local copies, waits for them, and re-layouts  7.35 us (13%)
    ppermute x2, waiting for transfers between devices, body(): high = lax.ppermute(backward, 'surf', back)  16.3 us
    pallas_call x7, Pallas kernels, call(): pl.pallas_call(kernel, out_shape=[jax.ShapeDtypeStruct(shape, jnp.float32...  16.2 us
    ppermute x2, starting transfers between devices, body(): low = lax.ppermute(forward, 'surf', ahead)  8.05 us
    unnamed x18, local copies, waits for them, and re-layouts  7.35 us
    ppermute x1, waiting for transfers between devices, body(): other_ends = lax.ppermute(ends, 'normal', swap)  3.8 us
    ppermute x1, waiting for transfers between devices, body(): other_end = lax.ppermute(end, 'normal', swap)  2.87 us
  transfers between devices with their start and end apart: 7, of which 6 were waited for; matrix products, arithmetic and copies ran while one was open for 0% of the time, Pallas kernels for 13%

profile of v1, /device:TPU:127, one launch (start us, length us, event | category | flops | bytes accessed | tf_op | source)
XLA Modules:
  0.0 55.4 jit_solution(16001580555958447909)
XLA Ops:
  0.0 0.0 copy-start
  0.0 1.2 %copy-done = f32[128,16,128]{2,1,0:T(8,128)S(1)} copy-done((f32[128,16,128]{2,1,0:T(8,128)S(1)}, f32[128,16,128]{2,1,0:T(8,128)}, u32[]{:S(2)}) %copy-start) | copy-done | bytes 1048600
  1.2 0.0 copy-start.2
  1.2 1.2 %copy-done.2 = bf16[256,16,128]{2,1,0:T(8,128)(2,1)S(1)} copy-done((bf16[256,16,128]{2,1,0:T(8,128)(2,1)S(1)}, bf16[256,16,128]{2,1,0:T(8,128)(2,1)}, u32[]{:S(2)}) %copy-start.2) | copy-done | bytes 1048600
  2.5 0.0 copy-start.3
  2.5 0.8 %copy-done.3 = bf16[128,256]{1,0:T(8,128)(2,1)S(1)} copy-done((bf16[128,256]{1,0:T(8,128)(2,1)S(1)}, bf16[128,256]{1,0:T(8,128)(2,1)}, u32[]{:S(2)}) %copy-start.3) | copy-done | bytes 65560
  3.3 0.0 copy-start.4
  3.3 0.8 %copy-done.4 = bf16[128,256]{1,0:T(8,128)(2,1)S(1)} copy-done((bf16[128,256]{1,0:T(8,128)(2,1)S(1)}, bf16[128,256]{1,0:T(8,128)(2,1)}, u32[]{:S(2)}) %copy-start.4) | copy-done | bytes 65560
  4.1 0.0 copy-start.7
  4.1 0.7 %copy-done.7 = s32[128]{0:T(128)S(1)} copy-done((s32[128]{0:T(128)S(1)}, s32[128]{0:T(128)}, u32[]{:S(2)}) %copy-start.7) | copy-done | bytes 536
  4.8 0.0 copy-start.8
  4.8 0.7 %copy-done.8 = f32[128]{0:T(128)S(1)} copy-done((f32[128]{0:T(128)S(1)}, f32[128]{0:T(128)}, u32[]{:S(2)}) %copy-start.8) | copy-done | bytes 536
  5.4 1.3 %shard_map.73 = (f32[16,128,128]{2,1,0:T(8,128)S(1)}, f32[16,128,128]{2,1,0:T(8,128)S(1)}, f32[2,4,128,128]{3,2,1,0:T(8,128)S(1)}, f32[2,4,128,128]{3,2,1,0:T(8,128)S(1)}, f32[128,128]{1,0:T(8,128)S(1)}) custom-call(bf16[256,16,128]{2,1,0:T(8,128)(2,1)S(1)} %copy-done.2, bf16[128,256]{1,0:T(8,128)(2,1)S(1)} %copy-done.3, bf16[128,256]{1,0:T(8,128)(2,1)S(1)} %copy-done.4, ...), custom_call_target="tpu_custom_call" | custom-call | tf_op jit(solution)/shard_map/pallas_call | solution.py:260
  6.7 4.0 %collective-permute-start = (f32[2,4,128,128]{3,2,1,0:T(8,128)S(1)}, f32[2,4,128,128]{3,2,1,0:T(8,128)S(1)}, u32[]{:S(2)}, u32[]{:S(2)}) collective-permute-start(f32[2,4,128,128]{3,2,1,0:T(8,128)S(1)} %get-tuple-element.30), channel_id=1, source_target_pairs={{0,1},{1,2},{2,3},{3,4},{4,5},{5,6},{6,7},{7,8},{8,9},{9,10},{10,1... | collective-permute-start | bytes 1572872 | tf_op jit(solution)/shard_map/ppermute | solution.py:289
  10.7 0.0 collective-permute-start.1
  10.7 0.0 collective-permute-start.2
  10.7 0.0 copy-start.1
  10.7 1.2 %copy-done.1 = f32[128,16,128]{2,1,0:T(8,128)S(1)} copy-done((f32[128,16,128]{2,1,0:T(8,128)S(1)}, f32[128,16,128]{2,1,0:T(8,128)}, u32[]{:S(2)}) %copy-start.1) | copy-done | bytes 1048600
  11.9 0.0 copy-start.5
  11.9 0.7 %copy-done.5 = s32[128,4]{0,1:T(4,128)S(1)} copy-done((s32[128,4]{0,1:T(4,128)S(1)}, s32[128,4]{0,1:T(4,128)}, u32[]{:S(2)}) %copy-start.5) | copy-done | bytes 2072
  12.6 4.3 %shard_map.74 = (f32[16,128,128]{2,1,0:T(8,128)S(1)}, f32[16,128,128]{2,1,0:T(8,128)S(1)}, f32[16,128,128]{2,1,0:T(8,128)S(1)}, f32[4,16,128,128]{3,2,1,0:T(8,128)S(1)}) custom-call(f32[16,128,128]{2,1,0:T(8,128)S(1)} %get-tuple-element.25.kappa_ref, f32[16,128,128]{2,1,0:T(8,128)S(1)} %get-tuple-element.26.emission_ref, f32[2048,128]{1,0:T(8,128)S(1)} %bitcast.6, ...), custom_call_target="tpu_custom_call" | custom-call | tf_op jit(solution)/shard_map/pallas_call | solution.py:260
  16.9 0.0 copy-start.6
  16.9 0.1 collective-permute-done.2.other_edge_ref
  17.1 0.0 collective-permute-done.low_ref
  17.1 8.0 %collective-permute-done.1.high_ref = f32[2,4,128,128]{3,2,1,0:T(8,128)S(1)} collective-permute-done((f32[2,4,128,128]{3,2,1,0:T(8,128)S(1)}, f32[2,4,128,128]{3,2,1,0:T(8,128)S(1)}, u32[]{:S(2)}, u32[]{:S(2)}) %collective-permute-start.1) | collective-permute-done | bytes 524320 | tf_op jit(solution)/shard_map/ppermute | solution.py:290
  25.0 3.5 %shard_map.75 = (f32[4,16,128,128]{3,2,1,0:T(8,128)S(1)}, f32[16,128,128]{2,1,0:T(8,128)S(1)}, f32[16,128,128]{2,1,0:T(8,128)S(1)}, f32[16,128,128]{2,1,0:T(8,128)S(1)}, f32[2,128,128]{2,1,0:T(8,128)S(1)}) custom-call(f32[16,128,128]{2,1,0:T(8,128)S(1)} %get-tuple-element.25.kappa_ref, f32[16,128,128]{2,1,0:T(8,128)S(1)} %get-tuple-element.27.base_ref, ...), custom_call_target="tpu_custom_call" | custom-call | tf_op jit(solution)/shard_map/pallas_call | solution.py:260
  28.5 0.1 collective-permute-start.3
  28.6 3.8 %collective-permute-done.3.other_ref = f32[2,128,128]{2,1,0:T(8,128)S(1)} collective-permute-done((f32[2,128,128]{2,1,0:T(8,128)S(1)}, f32[2,128,128]{2,1,0:T(8,128)S(1)}, u32[]{:S(2)}, u32[]{:S(2)}) %collective-permute-start.3) | collective-permute-done | bytes 131104 | tf_op jit(solution)/shard_map/ppermute | solution.py:300
  32.4 0.5 shard_map.76
  32.9 4.1 %collective-permute-start.4 = (f32[4,128,128]{2,1,0:T(8,128)S(1)}, f32[4,128,128]{2,1,0:T(8,128)S(1)}, u32[]{:S(2)}, u32[]{:S(2)}) collective-permute-start(f32[4,128,128]{2,1,0:T(8,128)S(1)} %get-tuple-element.38), channel_id=1, source_target_pairs={{0,1},{1,2},{2,3},{3,4},{4,5},{5,6},{6,7},{7,8},{8,9},{9,10},{10,1... | collective-permute-start | bytes 786440 | tf_op jit(solution)/shard_map/ppermute | solution.py:304
  36.9 0.0 collective-permute-start.5
  36.9 0.0 copy-done.6
  36.9 3.0 %shard_map.77.rhs_ref = f32[16,128,128]{2,1,0:T(8,128)S(1)} custom-call(f32[16,128,128]{2,1,0:T(8,128)S(1)} %get-tuple-element.36.current_ref, f32[16,128,128]{2,1,0:T(8,128)S(1)} %get-tuple-element.26.emission_ref, f32[4,16,128,128]{3,2,1,0:T(8,128)S(1)} %get-tuple-element.37.couple_ref, s32[4,128]{1,0:T(4,128)S(1)} %bitcast.9), custom_call_target="tpu_custom_call" | custom-call | tf_op jit(solution)/shard_map/pallas_call | solution.py:260
  39.9 0.3 collective-permute-done.4.low_ref
  40.2 8.3 %collective-permute-done.5.high_ref = f32[4,128,128]{2,1,0:T(8,128)S(1)} collective-permute-done((f32[4,128,128]{2,1,0:T(8,128)S(1)}, f32[4,128,128]{2,1,0:T(8,128)S(1)}, u32[]{:S(2)}, u32[]{:S(2)}) %collective-permute-start.5) | collective-permute-done | bytes 262176 | tf_op jit(solution)/shard_map/ppermute | solution.py:305
  48.6 2.3 %shard_map.78 = (f32[16,128,128]{2,1,0:T(8,128)S(1)}, f32[128,128]{1,0:T(8,128)S(1)}) custom-call(f32[16,128,128]{2,1,0:T(8,128)S(1)} %shard_map.77.rhs_ref, f32[4,128,128]{2,1,0:T(8,128)S(1)} %collective-permute-done.4.low_ref, f32[4,128,128]{2,1,0:T(8,128)S(1)} %collective-permute-done.5.high_ref, f32[4,16,128,128]{3,2,1,0:T(8,128)S(1)} %get-tuple-element.40.couple_ref, ...), custom_call_target="tpu_custom_call" | custom-call | tf_op jit(solution)/shard_map/pallas_call | solution.py:260
  50.8 0.3 collective-permute-start.6
  51.2 2.9 %collective-permute-done.6.other_ref = f32[128,128]{1,0:T(8,128)S(1)} collective-permute-done((f32[128,128]{1,0:T(8,128)S(1)}, f32[128,128]{1,0:T(8,128)S(1)}, u32[]{:S(2)}, u32[]{:S(2)}) %collective-permute-start.6) | collective-permute-done | bytes 65568 | tf_op jit(solution)/shard_map/ppermute | solution.py:308
  54.0 1.4 %shard_map.79 = f32[2048,128]{1,0:T(8,128)} custom-call(f32[128,128]{1,0:T(8,128)S(1)} %get-tuple-element.42.end_ref, f32[128,128]{1,0:T(8,128)S(1)} %collective-permute-done.6.other_ref, f32[2,128,128]{2,1,0:T(8,128)S(1)} %get-tuple-element.43.mix_ref, f32[16,128,128]{2,1,0:T(8,128)S(1)} %get-tuple-element.34.carried_ref, ...), custom_call_target="tpu_custom_call" | custom-call | tf_op jit(solution)/shard_map/pallas_call | solution.py:260
Async XLA Ops:
  0.0 1.2 %copy-start = (f32[128,16,128]{2,1,0:T(8,128)S(1)}, f32[128,16,128]{2,1,0:T(8,128)}, u32[]{:S(2)}) copy-start(f32[128,16,128]{2,1,0:T(8,128)} %param.10) | copy-start | bytes 3145732
  1.2 1.2 %copy-start.2 = (bf16[256,16,128]{2,1,0:T(8,128)(2,1)S(1)}, bf16[256,16,128]{2,1,0:T(8,128)(2,1)}, u32[]{:S(2)}) copy-start(bf16[256,16,128]{2,1,0:T(8,128)(2,1)} %pops_ref.1) | copy-start | bytes 3145732
  2.5 0.8 %copy-start.3 = (bf16[128,256]{1,0:T(8,128)(2,1)S(1)}, bf16[128,256]{1,0:T(8,128)(2,1)}, u32[]{:S(2)}) copy-start(bf16[128,256]{1,0:T(8,128)(2,1)} %absorb_ref.1) | copy-start | bytes 196612
  3.3 0.8 %copy-start.4 = (bf16[128,256]{1,0:T(8,128)(2,1)S(1)}, bf16[128,256]{1,0:T(8,128)(2,1)}, u32[]{:S(2)}) copy-start(bf16[128,256]{1,0:T(8,128)(2,1)} %emit_ref.1) | copy-start | bytes 196612
  4.1 0.7 %copy-start.7 = (s32[128]{0:T(128)S(1)}, s32[128]{0:T(128)}, u32[]{:S(2)}) copy-start(s32[128]{0:T(128)} %param.13) | copy-start | bytes 1540
  4.8 0.7 %copy-start.8 = (f32[128]{0:T(128)S(1)}, f32[128]{0:T(128)}, u32[]{:S(2)}) copy-start(f32[128]{0:T(128)} %param.11) | copy-start | bytes 1540
  6.7 10.4 %collective-permute-start = (f32[2,4,128,128]{3,2,1,0:T(8,128)S(1)}, f32[2,4,128,128]{3,2,1,0:T(8,128)S(1)}, u32[]{:S(2)}, u32[]{:S(2)}) collective-permute-start(f32[2,4,128,128]{3,2,1,0:T(8,128)S(1)} %get-tuple-element.30), channel_id=1, source_target_pairs={{0,1},{1,2},{2,3},{3,4},{4,5},{5,6},{6,7},{7,8},{8,9},{9,10},{10,1... | collective-permute-start | bytes 1572872 | tf_op jit(solution)/shard_map/ppermute | solution.py:289
  10.7 14.3 %collective-permute-start.1 = (f32[2,4,128,128]{3,2,1,0:T(8,128)S(1)}, f32[2,4,128,128]{3,2,1,0:T(8,128)S(1)}, u32[]{:S(2)}, u32[]{:S(2)}) collective-permute-start(f32[2,4,128,128]{3,2,1,0:T(8,128)S(1)} %get-tuple-element.31), channel_id=1, source_target_pairs={{1,0},{2,1},{3,2},{4,3},{5,4},{6,5},{7,6},{8,7},{9,8},{10,9},{11,1... | collective-permute-start | bytes 1572872 | tf_op jit(solution)/shard_map/ppermute | solution.py:290
  10.7 6.4 %collective-permute-start.2 = (f32[128,128]{1,0:T(8,128)S(1)}, f32[128,128]{1,0:T(8,128)S(1)}, u32[]{:S(2)}, u32[]{:S(2)}) collective-permute-start(f32[128,128]{1,0:T(8,128)S(1)} %get-tuple-element.32.edge_ref), channel_id=1, source_target_pairs={{0,128},{128,0},{1,129},{129,1},{2,130},{130,2},{3,131},{131,3},{4... | collective-permute-start | bytes 196616 | tf_op jit(solution)/shard_map/ppermute | solution.py:291
  10.7 1.2 %copy-start.1 = (f32[128,16,128]{2,1,0:T(8,128)S(1)}, f32[128,16,128]{2,1,0:T(8,128)}, u32[]{:S(2)}) copy-start(f32[128,16,128]{2,1,0:T(8,128)} %param.10) | copy-start | bytes 3145732
  11.9 0.7 %copy-start.5 = (s32[128,4]{0,1:T(4,128)S(1)}, s32[128,4]{0,1:T(4,128)}, u32[]{:S(2)}) copy-start(s32[128,4]{0,1:T(4,128)} %param.12) | copy-start | bytes 6148
  16.9 20.0 %copy-start.6 = (s32[128,4]{0,1:T(4,128)S(1)}, s32[128,4]{0,1:T(4,128)}, u32[]{:S(2)}) copy-start(s32[128,4]{0,1:T(4,128)} %param.12) | copy-start | bytes 6148
  28.5 3.9 %collective-permute-start.3 = (f32[2,128,128]{2,1,0:T(8,128)S(1)}, f32[2,128,128]{2,1,0:T(8,128)S(1)}, u32[]{:S(2)}, u32[]{:S(2)}) collective-permute-start(f32[2,128,128]{2,1,0:T(8,128)S(1)} %get-tuple-element.33.ends_ref), channel_id=1, source_target_pairs={{0,128},{128,0},{1,129},{129,1},{2,130},{130,2},{3,131},{131,3},{4... | collective-permute-start | bytes 393224 | tf_op jit(solution)/shard_map/ppermute | solution.py:300
  32.9 7.4 %collective-permute-start.4 = (f32[4,128,128]{2,1,0:T(8,128)S(1)}, f32[4,128,128]{2,1,0:T(8,128)S(1)}, u32[]{:S(2)}, u32[]{:S(2)}) collective-permute-start(f32[4,128,128]{2,1,0:T(8,128)S(1)} %get-tuple-element.38), channel_id=1, source_target_pairs={{0,1},{1,2},{2,3},{3,4},{4,5},{5,6},{6,7},{7,8},{8,9},{9,10},{10,1... | collective-permute-start | bytes 786440 | tf_op jit(solution)/shard_map/ppermute | solution.py:304
  36.9 11.6 %collective-permute-start.5 = (f32[4,128,128]{2,1,0:T(8,128)S(1)}, f32[4,128,128]{2,1,0:T(8,128)S(1)}, u32[]{:S(2)}, u32[]{:S(2)}) collective-permute-start(f32[4,128,128]{2,1,0:T(8,128)S(1)} %get-tuple-element.39), channel_id=1, source_target_pairs={{1,0},{2,1},{3,2},{4,3},{5,4},{6,5},{7,6},{8,7},{9,8},{10,9},{11,1... | collective-permute-start | bytes 786440 | tf_op jit(solution)/shard_map/ppermute | solution.py:305
  50.8 3.2 %collective-permute-start.6 = (f32[128,128]{1,0:T(8,128)S(1)}, f32[128,128]{1,0:T(8,128)S(1)}, u32[]{:S(2)}, u32[]{:S(2)}) collective-permute-start(f32[128,128]{1,0:T(8,128)S(1)} %get-tuple-element.42.end_ref), channel_id=1, source_target_pairs={{0,128},{128,0},{1,129},{129,1},{2,130},{130,2},{3,131},{131,3},{4... | collective-permute-start | bytes 196616 | tf_op jit(solution)/shard_map/ppermute | solution.py:308

commit v2 on v1

v2 whole, which is shorter than its diff:
```python
import jax
import jax.numpy as jnp
from jax import lax
from jax.experimental import pallas as pl
from jax.experimental.pallas import tpu as pltpu
from jax.sharding import PartitionSpec as P

HALO = 32
LANES = 128
HALF = 64
SURF_WEIGHT = 0.02
FACE = 2.0 / 3.0
LIMIT = 32 * 1024 * 1024
CHUNK = 32


def inverse(value):
    guess = pl.reciprocal(value, approx=True)
    return guess * (2.0 - value * guess)


def lane_ids(rows):
    return lax.broadcasted_iota(jnp.int32, (rows, LANES), 1)


def gather(value, select):
    high = value.astype(jnp.bfloat16)
    low = (value - high.astype(jnp.float32)).astype(jnp.bfloat16)
    return jnp.dot(jnp.concatenate([high, low], axis=1), select, preferred_element_type=jnp.float32)


def selection(lanes):
    source = lax.broadcasted_iota(jnp.int32, (LANES, LANES), 0)
    parts = [jnp.where(source == lanes[s : s + 1], 1.0, 0.0).astype(jnp.bfloat16) for s in range(4)]
    one = jnp.concatenate(parts, axis=1)
    return jnp.concatenate([one, one], axis=0)


def cut(value, s):
    return value[:, s * LANES : (s + 1) * LANES]


def row_of(position, count):
    block = lax.axis_index("normal")
    return position + block * (count - 1 - 2 * position)


def odd_surf():
    return lax.rem(lax.axis_index("surf"), 2) == 1


def pack_sides(plane_at, rows, far_ref, near_ref):
    groups = far_ref.shape[1]
    slot = lane_ids(groups) // HALO
    odd = odd_surf()
    for part in range(rows // 4):
        four = [plane_at(4 * part + k) for k in range(4)]
        ahead, back = [], []
        for k in range(4):
            turn = (HALO * (k + 1)) % LANES
            ahead.append(pltpu.roll(four[k], turn, 1) if turn else four[k])
            turn = HALO * (k ^ 1)
            back.append(pltpu.roll(four[k], turn, 1) if turn else four[k])
        forward = jnp.where(slot == 0, ahead[0], jnp.where(slot == 1, ahead[1], jnp.where(slot == 2, ahead[2], ahead[3])))
        backward = jnp.where(slot == 0, back[1], jnp.where(slot == 1, back[0], jnp.where(slot == 2, back[3], back[2])))
        far_ref[part] = jnp.where(odd, forward, backward)
        near_ref[part] = jnp.where(odd, backward, forward)


def local_places(neighbours_ref):
    offset = lax.axis_index("surf") * LANES
    found = neighbours_ref[...]
    return found >= 0, found - offset


def spread(table, rows):
    return [jnp.broadcast_to(table[s : s + 1], (rows, LANES)) for s in range(4)]


def edge_lanes(rows):
    lane = lane_ids(rows)
    return (lane < HALO) | (lane >= LANES - HALO)


def own_tables(neighbours_ref):
    valid, local = local_places(neighbours_ref)
    inside = valid & (local >= 0) & (local < LANES)
    return jnp.where(inside, local, -1), jnp.where(inside, SURF_WEIGHT * FACE, 0.0)


def halo_tables(neighbours_ref):
    valid, local = local_places(neighbours_ref)
    low = valid & (local < 0)
    high = valid & (local >= LANES)
    edge = edge_lanes(4)
    weight = jnp.where(low | high, SURF_WEIGHT * FACE, 0.0)
    weight = jnp.where(edge, weight, pltpu.roll(weight, HALF, 1))
    lanes = []
    for k in range(2):
        place = jnp.where(low, local + HALO * (k + 1), jnp.where(high, local - LANES + HALO * (k ^ 1), -LANES))
        lanes.append(jnp.where(edge, place, pltpu.roll(place, HALF, 1) + HALF))
    return lanes, weight


def halo_pair(far, near):
    even = (lane_ids(far.shape[0]) // HALO) % 2 == 0
    first = even != odd_surf()
    return jnp.where(first, far, near), jnp.where(first, near, far)


def start_kernel(pops_hbm, absorb_hbm, emit_hbm, energy_hbm, source_hbm, wall_hbm, kappa_ref, emission_ref, current_ref, far_ref, near_ref, edge_ref, pops_ref, table_ref, lines_ref, source_ref, wall_ref, sems):
    rows, groups, cells = kappa_ref.shape
    levels = pops_ref.shape[0]
    pieces = 4
    first, later = [], []
    step = levels // pieces
    for piece in range(pieces):
        here = pl.ds(piece * step, step)
        first.append(pltpu.make_async_copy(pops_hbm.at[here], pops_ref.at[here], sems.at[piece]))
    first.append(pltpu.make_async_copy(absorb_hbm, table_ref.at[pl.ds(0, groups)], sems.at[pieces]))
    first.append(pltpu.make_async_copy(emit_hbm, table_ref.at[pl.ds(groups, groups)], sems.at[pieces + 1]))
    later.append(pltpu.make_async_copy(source_hbm, source_ref, sems.at[pieces + 2]))
    later.append(pltpu.make_async_copy(wall_hbm, wall_ref, sems.at[pieces + 3]))
    step = groups * rows // pieces
    for piece in range(pieces):
        here = pl.ds(piece * step, step)
        later.append(pltpu.make_async_copy(energy_hbm.at[here], lines_ref.at[here], sems.at[pieces + 4 + piece]))
    for copy in first + later:
        copy.start()
    for copy in first:
        copy.wait()
    table = table_ref[...]
    turned = jnp.swapaxes(pops_ref[...], 0, 1)
    for pair in range(rows // 2):
        both = jnp.concatenate([turned[2 * pair], turned[2 * pair + 1]], axis=1)
        product = jnp.dot(table, both, preferred_element_type=jnp.float32)
        for k in range(2):
            row = row_of(2 * pair + k, rows)
            kappa_ref[row] = product[:groups, k * cells : (k + 1) * cells]
            emission_ref[row] = product[groups:, k * cells : (k + 1) * cells]
    for copy in later:
        copy.wait()

    @pl.when(lax.axis_index("normal") == 0)
    def _():
        kind = wall_ref[...]
        weight = jnp.where(kind == 0, 0.5, jnp.where(kind == 1, 0.25, 0.0))
        source = jnp.broadcast_to(source_ref[...], (groups, groups)).T
        emission_ref[0] = emission_ref[0] + source * weight

    pack_sides(lambda r: kappa_ref[r], rows, far_ref.at[0], near_ref.at[0])
    edge_ref[...] = kappa_ref[rows - 1]
    for r in range(rows):
        current_ref[r] = lines_ref[pl.ds(row_of(r, rows), groups, stride=rows), :]
    pack_sides(lambda r: current_ref[r], rows, far_ref.at[1], near_ref.at[1])


def own_kernel(kappa_ref, emission_ref, current_ref, neighbours_ref, wall_ref, base_ref, face_ref, couple_ref, paired_ref, rhs_ref, select_ref):
    rows, groups, cells = kappa_ref.shape
    lanes, weight = own_tables(neighbours_ref)
    select = selection(lanes)
    weight = spread(weight, groups)
    kind = wall_ref[...]
    share = jnp.where(kind == 0, 0.5, jnp.where(kind == 1, 0.25, 0.0))
    boundary = jnp.where(lax.axis_index("normal") == 0, share, 0.5)

    @pl.loop(0, rows // 4)
    def _(quad):
        here = pl.ds(quad * 4, 4)
        planes = jnp.concatenate([kappa_ref[here], current_ref[here]], axis=0).reshape(8 * groups, cells)
        found = gather(planes, select)
        for k in range(4):
            r = quad * 4 + k
            kappa = kappa_ref[r]
            total = kappa + jnp.where(r == 0, boundary, 0.0) if k == 0 else kappa
            rhs = emission_ref[r]
            near_kappa = found[k * groups : (k + 1) * groups]
            near_current = found[(4 + k) * groups : (5 + k) * groups]
            for s in range(4):
                couple = weight[s] * inverse(kappa + cut(near_kappa, s))
                couple_ref[s, r] = couple
                total = total + couple
                rhs = rhs + couple * cut(near_current, s)
            base_ref[r] = total
            rhs_ref[r] = rhs
            face_ref[r] = FACE * inverse(kappa_ref[jnp.maximum(r - 1, 0)] + kappa)

    edge = edge_lanes(groups)
    for pair in range(rows // 2):
        quad, k = divmod(pair, 2)
        paired_ref[pair] = jnp.where(edge, kappa_ref[4 * quad + k], pltpu.roll(kappa_ref[4 * quad + k + 2], HALF, 1))
    lanes, weight = halo_tables(neighbours_ref)
    for k in range(2):
        select_ref[k] = selection(lanes[k])


def first_kernel(base_ref, face_ref, rhs_ref, paired_ref, edge_ref, other_edge_ref, far_ref, near_ref, neighbours_ref, select_ref, couple_ref, pivot_ref, carried_ref, solved_ref, ends_ref, meeting_ref, found_ref):
    rows, groups, cells = base_ref.shape
    meeting_ref[...] = FACE * inverse(edge_ref[...] + other_edge_ref[...])
    lanes, weight = halo_tables(neighbours_ref)
    weight = spread(weight, CHUNK)
    quads = rows // 4
    far = far_ref[...].reshape(2 * quads * groups, cells)
    near = near_ref[...].reshape(2 * quads * groups, cells)
    halo = halo_pair(far, near)
    for k in range(2):
        found_ref[k] = gather(halo[k], select_ref[k])
    edge = edge_lanes(CHUNK)

    @pl.loop(0, groups // CHUNK)
    def _(part):
        start = pl.multiple_of(part * CHUNK, CHUNK)
        here = pl.ds(start, CHUNK)
        schur = None
        carried = None
        solved = None
        for quad in range(quads):
            sums, terms = [], []
            for k in range(2):
                pair = 2 * quad + k
                kappa = paired_ref[pair, here, :]
                near_kappa = found_ref[k, pl.ds(quad * groups + start, CHUNK), :]
                near_current = found_ref[k, pl.ds((quads + quad) * groups + start, CHUNK), :]
                total = None
                for s in range(4):
                    couple = weight[s] * inverse(kappa + cut(near_kappa, s))
                    couple_ref[s, pair, here, :] = couple
                    term = couple * cut(near_current, s)
                    total = couple if s == 0 else total + couple
                    extra = term if s == 0 else extra + term
                sums.append(total)
                terms.append(extra)
            for k in range(4):
                r = 4 * quad + k
                extra = sums[k] if k < 2 else pltpu.roll(sums[k - 2], HALF, 1)
                base = base_ref[r, here, :] + jnp.where(edge, extra, 0.0)
                extra = terms[k] if k < 2 else pltpu.roll(terms[k - 2], HALF, 1)
                rhs = rhs_ref[r, here, :] + jnp.where(edge, extra, 0.0)
                if r == 0:
                    schur = base
                else:
                    schur = base + schur * carried
                    rhs = rhs + face_ref[r, here, :] * solved
                if r == rows - 1:
                    ends_ref[0, here, :] = schur
                    ends_ref[1, here, :] = rhs
                else:
                    after = face_ref[r + 1, here, :]
                    pivot = inverse(schur + after)
                    carried = after * pivot
                    solved = rhs * pivot
                    pivot_ref[r, here, :] = pivot
                    carried_ref[r, here, :] = carried
                    solved_ref[r, here, :] = solved


def again_kernel(rhs_ref, far_ref, near_ref, couple_ref, select_ref, pivot_ref, face_ref, solved_ref, end_ref, found_ref):
    rows, groups, cells = rhs_ref.shape
    quads = rows // 4
    halo = halo_pair(far_ref[...].reshape(quads * groups, cells), near_ref[...].reshape(quads * groups, cells))
    for k in range(2):
        found_ref[k] = gather(halo[k], select_ref[k])
    edge = edge_lanes(CHUNK)

    @pl.loop(0, groups // CHUNK)
    def _(part):
        start = pl.multiple_of(part * CHUNK, CHUNK)
        here = pl.ds(start, CHUNK)
        solved = None
        for quad in range(quads):
            terms = []
            for k in range(2):
                near_current = found_ref[k, pl.ds(quad * groups + start, CHUNK), :]
                total = None
                for s in range(4):
                    term = couple_ref[s, 2 * quad + k, here, :] * cut(near_current, s)
                    total = term if s == 0 else total + term
                terms.append(total)
            for k in range(4):
                r = 4 * quad + k
                extra = terms[k] if k < 2 else pltpu.roll(terms[k - 2], HALF, 1)
                rhs = rhs_ref[r, here, :] + jnp.where(edge, extra, 0.0)
                if r > 0:
                    rhs = rhs + face_ref[r, here, :] * solved
                if r == rows - 1:
                    end_ref[here, :] = rhs
                else:
                    solved = rhs * pivot_ref[r, here, :]
                    solved_ref[r, here, :] = solved


def meet_kernel(ends_ref, other_ref, meeting_ref, carried_ref, solved_ref, current_ref, far_ref, near_ref, mix_ref):
    rows, groups, cells = current_ref.shape
    face = meeting_ref[...]
    own, other = ends_ref[0], other_ref[0]
    scale = inverse(own * other + face * (own + other))
    mine = (other + face) * scale
    theirs = face * scale
    mix_ref[0] = mine
    mix_ref[1] = theirs
    value = mine * ends_ref[1] + theirs * other_ref[1]
    current_ref[rows - 1] = value
    for r in range(rows - 2, -1, -1):
        value = solved_ref[r] + carried_ref[r] * value
        current_ref[r] = value
    pack_sides(lambda r: current_ref[r], rows, far_ref, near_ref)


def own_again_kernel(current_ref, emission_ref, couple_ref, neighbours_ref, rhs_ref):
    rows, groups, cells = current_ref.shape
    lanes, weight = own_tables(neighbours_ref)
    select = selection(lanes)

    @pl.loop(0, rows // 4)
    def _(quad):
        found = gather(current_ref[pl.ds(quad * 4, 4)].reshape(4 * groups, cells), select)
        for k in range(4):
            r = quad * 4 + k
            rhs = emission_ref[r]
            for s in range(4):
                rhs = rhs + couple_ref[s, r] * cut(found[k * groups : (k + 1) * groups], s)
            rhs_ref[r] = rhs


def last_kernel(end_ref, other_ref, mix_ref, carried_ref, solved_ref, out_hbm, lines_ref, sems):
    rows, groups, cells = carried_ref.shape
    copies = []
    for part in range(groups // CHUNK):
        start = part * CHUNK
        here = pl.ds(start, CHUNK)
        value = mix_ref[0, here, :] * end_ref[here, :] + mix_ref[1, here, :] * other_ref[here, :]
        lines_ref[pl.ds(start * rows + row_of(rows - 1, rows), CHUNK, stride=rows), :] = value
        for r in range(rows - 2, -1, -1):
            value = solved_ref[r, here, :] + carried_ref[r, here, :] * value
            lines_ref[pl.ds(start * rows + row_of(r, rows), CHUNK, stride=rows), :] = value
        there = pl.ds(start * rows, CHUNK * rows)
        copies.append(pltpu.make_async_copy(lines_ref.at[there], out_hbm.at[there], sems.at[part]))
        copies[-1].start()
    for copy in copies:
        copy.wait()


VMEM = pl.BlockSpec(memory_space=pltpu.VMEM)
HBM = pl.BlockSpec(memory_space=pltpu.HBM)


def call(kernel, outs, *args, space=VMEM, out_space=VMEM, scratch=()):
    return pl.pallas_call(
        kernel,
        out_shape=[jax.ShapeDtypeStruct(out, jnp.float32) if isinstance(out, tuple) else out for out in outs],
        in_specs=[space] * len(args),
        out_specs=[out_space] * len(outs),
        scratch_shapes=list(scratch),
        compiler_params=pltpu.CompilerParams(vmem_limit_bytes=LIMIT),
    )(*args)


def body(populations, absorb_table, emit_table, energy, wall_source, neighbours, wall_type):
    levels, rows, cells = populations.shape
    groups = absorb_table.shape[0]
    whole = (rows, groups, cells)
    plane = (groups, cells)
    packed = (rows // 4, groups, cells)
    pairs = (rows // 2, groups, cells)
    count = lax.axis_size("surf")
    far = [(i, (i + 1) % count if i % 2 else (i - 1) % count) for i in range(count)]
    near = [(i, i ^ 1) for i in range(count)]
    swap = [(0, 1), (1, 0)]
    lines = energy.reshape(groups * rows, cells)
    places = neighbours.T
    walls = wall_type.reshape(1, cells)
    sources = wall_source.reshape(1, groups)

    def halo(far_side, near_side):
        near_side = lax.ppermute(near_side, "surf", near)
        return lax.ppermute(far_side, "surf", far), near_side

    inputs = (populations, absorb_table, emit_table, lines, sources, walls)
    kappa, emission, current, far_side, near_side, edge = call(
        start_kernel,
        [whole, whole, whole, (2,) + packed, (2,) + packed, plane],
        *[pltpu.with_memory_space_constraint(value, pltpu.HBM) for value in inputs],
        space=HBM,
        scratch=[
            pltpu.VMEM(populations.shape, populations.dtype),
            pltpu.VMEM((2 * groups, levels), absorb_table.dtype),
            pltpu.VMEM(lines.shape, jnp.float32),
            pltpu.VMEM((1, groups), jnp.float32),
            pltpu.VMEM((1, cells), jnp.int32),
            pltpu.SemaphoreType.DMA((12,)),
        ],
    )
    far_side, near_side = halo(far_side, near_side)
    other_edge = lax.ppermute(edge, "normal", swap)
    base, face, own_couple, paired, rhs, select = call(
        own_kernel,
        [whole, whole, (4,) + whole, pairs, whole, jax.ShapeDtypeStruct((2, 2 * LANES, 4 * LANES), jnp.bfloat16)],
        kappa, emission, current, places, walls,
    )
    halo_couple, pivot, carried, solved, ends, meeting = call(
        first_kernel,
        [(4,) + pairs, whole, whole, whole, (2,) + plane, plane],
        base, face, rhs, paired, edge, other_edge, far_side, near_side, places, select,
        scratch=[pltpu.VMEM((2, 2 * packed[0] * groups, 4 * LANES), jnp.float32)],
    )
    other_ends = lax.ppermute(ends, "normal", swap)
    current, far_side, near_side, mix = call(
        meet_kernel, [whole, packed, packed, (2,) + plane], ends, other_ends, meeting, carried, solved
    )
    far_side, near_side = halo(far_side, near_side)
    (rhs,) = call(own_again_kernel, [whole], current, emission, own_couple, places)
    solved, end = call(
        again_kernel, [whole, plane], rhs, far_side, near_side, halo_couple, select, pivot, face,
        scratch=[pltpu.VMEM((2, packed[0] * groups, 4 * LANES), jnp.float32)],
    )
    other_end = lax.ppermute(end, "normal", swap)
    (out,) = call(
        last_kernel, [lines.shape], end, other_end, mix, carried, solved,
        out_space=HBM,
        scratch=[pltpu.VMEM(lines.shape, jnp.float32), pltpu.SemaphoreType.DMA((groups // CHUNK,))],
    )
    return out.reshape(groups, rows, cells)


def solution(mesh):
    return jax.shard_map(
        body,
        mesh=mesh,
        in_specs=(
            P(None, "normal", "surf"),
            P(),
            P(),
            P(None, "normal", "surf"),
            P(),
            P("surf", None),
            P("surf"),
        ),
        out_specs=P(None, "normal", "surf"),
        check_vma=False,
    )
```

time: 55.8 us -> 46.5 us (0.83)
  the two profiles are of different devices: /device:TPU:127 before, /device:TPU:2 now
where the time goes in v2:
time: 46.5 us; the launch traced here: 46.4 us
  starting transfers between devices  18.6 us (40%)
  waiting for transfers between devices  14.8 us (32%)
  Pallas kernels  11.6 us (25%)
  local copies, waits for them, and re-layouts  1.34 us (3%)
    ppermute x2, starting transfers between devices, halo(): return (lax.ppermute(far_side, 'surf', far), near_side)  14.6 us
    pallas_call x7, Pallas kernels, call(): pl.pallas_call(kernel, out_shape=[jax.ShapeDtypeStruct(out, jnp.float32)...  11.6 us
    ppermute x2, waiting for transfers between devices, halo(): return (lax.ppermute(far_side, 'surf', far), near_side)  6.35 us
    ppermute x1, waiting for transfers between devices, body(): other_ends = lax.ppermute(ends, 'normal', swap)  4.68 us
    ppermute x1, waiting for transfers between devices, body(): other_end = lax.ppermute(end, 'normal', swap)  3.5 us
    ppermute x1, starting transfers between devices, body(): other_ends = lax.ppermute(ends, 'normal', swap)  1.62 us
    ppermute x1, starting transfers between devices, body(): other_edge = lax.ppermute(edge, 'normal', swap)  1.53 us
    unnamed x4, local copies, waits for them, and re-layouts  1.34 us
  transfers between devices with their start and end apart: 7, of which 5 were waited for; matrix products, arithmetic and copies ran while one was open for 0% of the time, Pallas kernels for 9%

profile of v2, /device:TPU:2, one launch (start us, length us, event | category | flops | bytes accessed | tf_op | source)
XLA Modules:
  0.0 46.4 jit_solution(16388492015272862724)
XLA Ops:
  0.0 2.8 %shard_map.73 = (f32[16,128,128]{2,1,0:T(8,128)S(1)}, f32[16,128,128]{2,1,0:T(8,128)S(1)}, f32[16,128,128]{2,1,0:T(8,128)S(1)}, f32[2,4,128,128]{3,2,1,0:T(8,128...) custom-call(bf16[256,16,128]{2,1,0:T(8,128)(2,1)} %pops_hbm.1, bf16[128,256]{1,0:T(8,128)(2,1)} %absorb_hbm.1, ...), custom_call_target="tpu_custom_call" | custom-call | tf_op jit(solution)/shard_map/pallas_call | solution.py:348
  2.8 9.4 %collective-permute-start.1 = (f32[2,4,128,128]{3,2,1,0:T(8,128)S(1)}, f32[2,4,128,128]{3,2,1,0:T(8,128)S(1)}, u32[]{:S(2)}, u32[]{:S(2)}) collective-permute-start(f32[2,4,128,128]{3,2,1,0:T(8,128)S(1)} %get-tuple-element.37), channel_id=1, source_target_pairs={{0,127},{1,2},{2,1},{3,4},{4,3},{5,6},{6,5},{7,8},{8,7},{9,10},{10... | collective-permute-start | bytes 1572872 | tf_op jit(solution)/shard_map/ppermute | solution.py:376
  12.2 0.0 collective-permute-start.2
  12.2 1.5 %collective-permute-start = (f32[128,128]{1,0:T(8,128)S(1)}, f32[128,128]{1,0:T(8,128)S(1)}, u32[]{:S(2)}, u32[]{:S(2)}) collective-permute-start(f32[128,128]{1,0:T(8,128)S(1)} %get-tuple-element.36.edge_ref), channel_id=1, source_target_pairs={{0,128},{128,0},{1,129},{129,1},{2,130},{130,2},{3,131},{131,3},{4... | collective-permute-start | bytes 196616 | tf_op jit(solution)/shard_map/ppermute | solution.py:394
  13.7 0.0 copy-start
  13.7 0.7 %copy-done = s32[128,4]{0,1:T(4,128)S(1)} copy-done((s32[128,4]{0,1:T(4,128)S(1)}, s32[128,4]{0,1:T(4,128)}, u32[]{:S(2)}) %copy-start) | copy-done | bytes 2072
  14.4 0.0 copy-start.1
  14.4 0.7 %copy-done.1 = s32[128]{0:T(128)S(1)} copy-done((s32[128]{0:T(128)S(1)}, s32[128]{0:T(128)}, u32[]{:S(2)}) %copy-start.1) | copy-done | bytes 536
  15.1 2.7 %shard_map.74 = (f32[16,128,128]{2,1,0:T(8,128)S(1)}, f32[16,128,128]{2,1,0:T(8,128)S(1)}, f32[4,16,128,128]{3,2,1,0:T(8,128)S(1)}, f32[8,128,128]{2,1,0:T(8,128...) custom-call(f32[16,128,128]{2,1,0:T(8,128)S(1)} %get-tuple-element.29.kappa_ref, ...), custom_call_target="tpu_custom_call" | custom-call | tf_op jit(solution)/shard_map/pallas_call | solution.py:348
  17.8 0.3 collective-permute-done.other_edge_ref
  18.1 1.1 %collective-permute-done.1.far_ref = f32[2,4,128,128]{3,2,1,0:T(8,128)S(1)} collective-permute-done((f32[2,4,128,128]{3,2,1,0:T(8,128)S(1)}, f32[2,4,128,128]{3,2,1,0:T(8,128)S(1)}, u32[]{:S(2)}, u32[]{:S(2)}) %collective-permute-start.1) | collective-permute-done | bytes 524320 | tf_op jit(solution)/shard_map/ppermute | solution.py:376
  19.2 0.0 collective-permute-done.2.near_ref
  19.2 2.1 %shard_map.75 = (f32[4,8,128,128]{3,2,1,0:T(8,128)S(1)}, f32[16,128,128]{2,1,0:T(8,128)S(1)}, f32[16,128,128]{2,1,0:T(8,128)S(1)}, f32[16,128,128]{2,1,0:T(8,128...) custom-call(f32[16,128,128]{2,1,0:T(8,128)S(1)} %get-tuple-element.32.base_ref, ...), custom_call_target="tpu_custom_call" | custom-call | tf_op jit(solution)/shard_map/pallas_call | solution.py:348
  21.3 1.6 %collective-permute-start.3 = (f32[2,128,128]{2,1,0:T(8,128)S(1)}, f32[2,128,128]{2,1,0:T(8,128)S(1)}, u32[]{:S(2)}, u32[]{:S(2)}) collective-permute-start(f32[2,128,128]{2,1,0:T(8,128)S(1)} %get-tuple-element.40.ends_ref), channel_id=1, source_target_pairs={{0,128},{128,0},{1,129},{129,1},{2,130},{130,2},{3,131},{131,3},{4... | collective-permute-start | bytes 393224 | tf_op jit(solution)/shard_map/ppermute | solution.py:406
  22.9 4.7 %collective-permute-done.3.other_ref = f32[2,128,128]{2,1,0:T(8,128)S(1)} collective-permute-done((f32[2,128,128]{2,1,0:T(8,128)S(1)}, f32[2,128,128]{2,1,0:T(8,128)S(1)}, u32[]{:S(2)}, u32[]{:S(2)}) %collective-permute-start.3) | collective-permute-done | bytes 131104 | tf_op jit(solution)/shard_map/ppermute | solution.py:406
  27.6 0.5 shard_map.76
  28.0 5.2 %collective-permute-start.4 = (f32[4,128,128]{2,1,0:T(8,128)S(1)}, f32[4,128,128]{2,1,0:T(8,128)S(1)}, u32[]{:S(2)}, u32[]{:S(2)}) collective-permute-start(f32[4,128,128]{2,1,0:T(8,128)S(1)} %get-tuple-element.46), channel_id=1, source_target_pairs={{0,127},{1,2},{2,1},{3,4},{4,3},{5,6},{6,5},{7,8},{8,7},{9,10},{10... | collective-permute-start | bytes 786440 | tf_op jit(solution)/shard_map/ppermute | solution.py:376
  33.2 0.0 collective-permute-start.5
  33.2 1.3 %shard_map.77.rhs_ref = f32[16,128,128]{2,1,0:T(8,128)S(1)} custom-call(f32[16,128,128]{2,1,0:T(8,128)S(1)} %get-tuple-element.44.current_ref, f32[16,128,128]{2,1,0:T(8,128)S(1)} %get-tuple-element.30.emission_ref, f32[4,16,128,128]{3,2,1,0:T(8,128)S(1)} %get-tuple-element.45.couple_ref, s32[4,128]{1,0:T(4,128)S(1)} %bitcast.7), custom_call_target="tpu_custom_call" | custom-call | tf_op jit(solution)/shard_map/pallas_call | solution.py:348
  34.5 5.2 %collective-permute-done.4.far_ref = f32[4,128,128]{2,1,0:T(8,128)S(1)} collective-permute-done((f32[4,128,128]{2,1,0:T(8,128)S(1)}, f32[4,128,128]{2,1,0:T(8,128)S(1)}, u32[]{:S(2)}, u32[]{:S(2)}) %collective-permute-start.4) | collective-permute-done | bytes 262176 | tf_op jit(solution)/shard_map/ppermute | solution.py:376
  39.8 0.0 collective-permute-done.5.near_ref
  39.8 1.1 %shard_map.78 = (f32[16,128,128]{2,1,0:T(8,128)S(1)}, f32[128,128]{1,0:T(8,128)S(1)}) custom-call(f32[16,128,128]{2,1,0:T(8,128)S(1)} %shard_map.77.rhs_ref, f32[4,128,128]{2,1,0:T(8,128)S(1)} %collective-permute-done.4.far_ref, f32[4,128,128]{2,1,0:T(8,128)S(1)} %collective-permute-done.5.near_ref, f32[4,8,128,128]{3,2,1,0:T(8,128)S(1)} %get-tuple-element.48.couple_ref, ...), custom_call_target="tpu_custom_call" | custom-call | tf_op jit(solution)/shard_map/pallas_call | solution.py:348
  40.8 0.9 %collective-permute-start.6 = (f32[128,128]{1,0:T(8,128)S(1)}, f32[128,128]{1,0:T(8,128)S(1)}, u32[]{:S(2)}, u32[]{:S(2)}) collective-permute-start(f32[128,128]{1,0:T(8,128)S(1)} %get-tuple-element.50.end_ref), channel_id=1, source_target_pairs={{0,128},{128,0},{1,129},{129,1},{2,130},{130,2},{3,131},{131,3},{4... | collective-permute-start | bytes 196616 | tf_op jit(solution)/shard_map/ppermute | solution.py:416
  41.7 3.5 %collective-permute-done.6.other_ref = f32[128,128]{1,0:T(8,128)S(1)} collective-permute-done((f32[128,128]{1,0:T(8,128)S(1)}, f32[128,128]{1,0:T(8,128)S(1)}, u32[]{:S(2)}, u32[]{:S(2)}) %collective-permute-start.6) | collective-permute-done | bytes 65568 | tf_op jit(solution)/shard_map/ppermute | solution.py:416
  45.2 1.2 %shard_map.79 = f32[2048,128]{1,0:T(8,128)} custom-call(f32[128,128]{1,0:T(8,128)S(1)} %get-tuple-element.50.end_ref, f32[128,128]{1,0:T(8,128)S(1)} %collective-permute-done.6.other_ref, f32[2,128,128]{2,1,0:T(8,128)S(1)} %get-tuple-element.51.mix_ref, f32[16,128,128]{2,1,0:T(8,128)S(1)} %get-tuple-element.42.carried_ref, ...), custom_call_target="tpu_custom_call" | custom-call | tf_op jit(solution)/shard_map/pallas_call | solution.py:348
Async XLA Ops:
  2.8 16.4 %collective-permute-start.1 = (f32[2,4,128,128]{3,2,1,0:T(8,128)S(1)}, f32[2,4,128,128]{3,2,1,0:T(8,128)S(1)}, u32[]{:S(2)}, u32[]{:S(2)}) collective-permute-start(f32[2,4,128,128]{3,2,1,0:T(8,128)S(1)} %get-tuple-element.37), channel_id=1, source_target_pairs={{0,127},{1,2},{2,1},{3,4},{4,3},{5,6},{6,5},{7,8},{8,7},{9,10},{10... | collective-permute-start | bytes 1572872 | tf_op jit(solution)/shard_map/ppermute | solution.py:376
  12.2 7.0 %collective-permute-start.2 = (f32[2,4,128,128]{3,2,1,0:T(8,128)S(1)}, f32[2,4,128,128]{3,2,1,0:T(8,128)S(1)}, u32[]{:S(2)}, u32[]{:S(2)}) collective-permute-start(f32[2,4,128,128]{3,2,1,0:T(8,128)S(1)} %get-tuple-element.38), channel_id=1, source_target_pairs={{0,1},{1,0},{2,3},{3,2},{4,5},{5,4},{6,7},{7,6},{8,9},{9,8},{10,11... | collective-permute-start | bytes 1572872 | tf_op jit(solution)/shard_map/ppermute | solution.py:375
  12.2 5.9 %collective-permute-start = (f32[128,128]{1,0:T(8,128)S(1)}, f32[128,128]{1,0:T(8,128)S(1)}, u32[]{:S(2)}, u32[]{:S(2)}) collective-permute-start(f32[128,128]{1,0:T(8,128)S(1)} %get-tuple-element.36.edge_ref), channel_id=1, source_target_pairs={{0,128},{128,0},{1,129},{129,1},{2,130},{130,2},{3,131},{131,3},{4... | collective-permute-start | bytes 196616 | tf_op jit(solution)/shard_map/ppermute | solution.py:394
  13.7 0.7 %copy-start = (s32[128,4]{0,1:T(4,128)S(1)}, s32[128,4]{0,1:T(4,128)}, u32[]{:S(2)}) copy-start(s32[128,4]{0,1:T(4,128)} %param.12) | copy-start | bytes 6148
  14.4 0.7 %copy-start.1 = (s32[128]{0:T(128)S(1)}, s32[128]{0:T(128)}, u32[]{:S(2)}) copy-start(s32[128]{0:T(128)} %param.13) | copy-start | bytes 1540
  21.3 6.3 %collective-permute-start.3 = (f32[2,128,128]{2,1,0:T(8,128)S(1)}, f32[2,128,128]{2,1,0:T(8,128)S(1)}, u32[]{:S(2)}, u32[]{:S(2)}) collective-permute-start(f32[2,128,128]{2,1,0:T(8,128)S(1)} %get-tuple-element.40.ends_ref), channel_id=1, source_target_pairs={{0,128},{128,0},{1,129},{129,1},{2,130},{130,2},{3,131},{131,3},{4... | collective-permute-start | bytes 393224 | tf_op jit(solution)/shard_map/ppermute | solution.py:406
  28.0 11.7 %collective-permute-start.4 = (f32[4,128,128]{2,1,0:T(8,128)S(1)}, f32[4,128,128]{2,1,0:T(8,128)S(1)}, u32[]{:S(2)}, u32[]{:S(2)}) collective-permute-start(f32[4,128,128]{2,1,0:T(8,128)S(1)} %get-tuple-element.46), channel_id=1, source_target_pairs={{0,127},{1,2},{2,1},{3,4},{4,3},{5,6},{6,5},{7,8},{8,7},{9,10},{10... | collective-permute-start | bytes 786440 | tf_op jit(solution)/shard_map/ppermute | solution.py:376
  33.2 6.5 %collective-permute-start.5 = (f32[4,128,128]{2,1,0:T(8,128)S(1)}, f32[4,128,128]{2,1,0:T(8,128)S(1)}, u32[]{:S(2)}, u32[]{:S(2)}) collective-permute-start(f32[4,128,128]{2,1,0:T(8,128)S(1)} %get-tuple-element.47), channel_id=1, source_target_pairs={{0,1},{1,0},{2,3},{3,2},{4,5},{5,4},{6,7},{7,6},{8,9},{9,8},{10,11... | collective-permute-start | bytes 786440 | tf_op jit(solution)/shard_map/ppermute | solution.py:375
  40.8 4.4 %collective-permute-start.6 = (f32[128,128]{1,0:T(8,128)S(1)}, f32[128,128]{1,0:T(8,128)S(1)}, u32[]{:S(2)}, u32[]{:S(2)}) collective-permute-start(f32[128,128]{1,0:T(8,128)S(1)} %get-tuple-element.50.end_ref), channel_id=1, source_target_pairs={{0,128},{128,0},{1,129},{129,1},{2,130},{130,2},{3,131},{131,3},{4... | collective-permute-start | bytes 196616 | tf_op jit(solution)/shard_map/ppermute | solution.py:416

commit v3 on v2

v3 whole, which is shorter than its diff:
```python
import jax
import jax.numpy as jnp
from jax import lax
from jax.experimental import pallas as pl
from jax.experimental.pallas import tpu as pltpu
from jax.sharding import PartitionSpec as P

HALO = 32
LANES = 128
HALF = 64
SURF_WEIGHT = 0.02
FACE = 2.0 / 3.0
LIMIT = 32 * 1024 * 1024
CHUNK = 64


def inverse(value):
    guess = pl.reciprocal(value, approx=True)
    return guess * (2.0 - value * guess)


def lane_ids(rows):
    return lax.broadcasted_iota(jnp.int32, (rows, LANES), 1)


def gather(value, select):
    high = value.astype(jnp.bfloat16)
    low = (value - high.astype(jnp.float32)).astype(jnp.bfloat16)
    return jnp.dot(jnp.concatenate([high, low], axis=1), select, preferred_element_type=jnp.float32)


def selection(lanes):
    source = lax.broadcasted_iota(jnp.int32, (LANES, LANES), 0)
    parts = [jnp.where(source == lanes[s : s + 1], 1.0, 0.0).astype(jnp.bfloat16) for s in range(4)]
    one = jnp.concatenate(parts, axis=1)
    return jnp.concatenate([one, one], axis=0)


def cut(value, s):
    return value[:, s * LANES : (s + 1) * LANES]


def row_of(position, count):
    block = lax.axis_index("normal")
    return position + block * (count - 1 - 2 * position)


def odd_surf():
    return lax.rem(lax.axis_index("surf"), 2)


def pack(plane, high):
    slot = lane_ids(HALO) // HALO
    packed = None
    for k in range(4):
        turned = pltpu.roll(plane[k * HALO : (k + 1) * HALO], HALO * lax.rem(k + high, 4), 1)
        packed = turned if k == 0 else jnp.where(slot == k, turned, packed)
    return packed


def local_places(neighbours_ref):
    offset = lax.axis_index("surf") * LANES
    found = neighbours_ref[...]
    return found >= 0, found - offset


def spread(table, rows):
    return [jnp.broadcast_to(table[s : s + 1], (rows, LANES)) for s in range(4)]


def own_tables(neighbours_ref):
    valid, local = local_places(neighbours_ref)
    inside = valid & (local >= 0) & (local < LANES)
    return jnp.where(inside, local, -1), jnp.where(inside, SURF_WEIGHT * FACE, 0.0)


def side_tables(neighbours_ref, high):
    valid, local = local_places(neighbours_ref)
    slot = lane_ids(4) // HALO
    place = local + (HALO - high * (LANES + HALO))
    here = slot == 3 * high
    beyond = valid & here & (place >= 0) & (place < HALO)
    place = jnp.where(beyond, place, -LANES)
    weight = jnp.where(beyond, SURF_WEIGHT * FACE, 0.0)

    def repeat(value):
        value = jnp.where(here, value, 0)
        return value + pltpu.roll(value, HALO, 1) + pltpu.roll(value, 2 * HALO, 1) + pltpu.roll(value, 3 * HALO, 1)

    return repeat(place) + HALO * slot, repeat(weight)


def unpack(value, high, quarters=range(4)):
    here = lane_ids(HALO) // HALO == 3 * high
    return jnp.concatenate(
        [jnp.where(here, pltpu.roll(value, HALO * lax.rem(4 - k - high, 4), 1), 0.0) for k in quarters], axis=0
    )


def kappa_kernel(pops_hbm, absorb_hbm, emit_hbm, lines_hbm, places_hbm, walls_hbm, sources_hbm, kappa_ref, turned_ref, far_ref, edge_ref, emit_ref, lines_ref, places_ref, walls_ref, sources_ref, pops_ref, table_ref, sems):
    rows, groups, cells = kappa_ref.shape
    levels = pops_ref.shape[0]
    pieces = 4
    step = levels // pieces
    pairs = []
    for piece in range(pieces):
        here = pl.ds(piece * step, step)
        pairs.append((pops_hbm.at[here], pops_ref.at[here]))
    pairs.append((absorb_hbm, table_ref))
    step = groups * rows // pieces
    for piece in range(pieces):
        there = pl.ds(piece * step, step)
        pairs.append((lines_hbm.at[there], lines_ref.at[there]))
    pairs += [(emit_hbm, emit_ref), (places_hbm, places_ref), (walls_hbm, walls_ref), (sources_hbm, sources_ref)]
    copies = [pltpu.make_async_copy(pair[0], pair[1], sems.at[i]) for i, pair in enumerate(pairs)]
    for copy in copies:
        copy.start()
    step = levels // pieces
    for piece in range(pieces):
        copies[piece].wait()
        here = pl.ds(piece * step, step)
        turned_ref[:, here, :] = jnp.swapaxes(pops_ref[here], 0, 1)
    copies[pieces].wait()
    table = table_ref[...]
    for pair in range(rows // 2):
        both = jnp.concatenate([turned_ref[2 * pair], turned_ref[2 * pair + 1]], axis=1)
        product = jnp.dot(table, both, preferred_element_type=jnp.float32)
        for k in range(2):
            kappa_ref[row_of(2 * pair + k, rows)] = product[:, k * cells : (k + 1) * cells]
    odd = odd_surf()
    for r in range(rows):
        far_ref[0, r] = pack(kappa_ref[r], odd)
    edge_ref[...] = kappa_ref[rows - 1]
    for copy in copies[pieces + 1 :]:
        copy.wait()
    for r in range(rows):
        far_ref[1, r] = pack(lines_ref[pl.ds(row_of(r, rows), groups, stride=rows), :], odd)


def near_kernel(lines_ref, kappa_ref, current_ref, near_kappa_ref, *half_refs):
    rows, groups, cells = current_ref.shape
    low_near = 1 - odd_surf()
    for r in range(rows):
        current = lines_ref[pl.ds(row_of(r, rows), groups, stride=rows), :]
        current_ref[r] = current
        side = pack(kappa_ref[r], low_near)
        near_kappa_ref[r] = side
        half_refs[r // 8][r % 8] = side
        half_refs[2 + r // 8][r % 8] = pack(current, low_near)


def own_kernel(kappa_ref, current_ref, near_kappa_0, near_kappa_1, near_current_0, near_current_1, mine_ref, turned_ref, emit_ref, source_ref, neighbours_ref, wall_ref, base_ref, face_ref, emission_ref, rhs_ref, couple_ref, near_couple_ref, select_ref, weight_ref, beside_ref):
    rows, groups, cells = kappa_ref.shape
    high = odd_surf()
    low_near = 1 - high
    lanes, weight = side_tables(neighbours_ref, high)
    select_ref[2] = selection(lanes)
    weight_ref[...] = weight
    lanes, weight = own_tables(neighbours_ref)
    select_ref[0] = selection(lanes)
    weight = spread(weight, groups)
    lanes, near_weight = side_tables(neighbours_ref, low_near)
    select_ref[1] = selection(lanes)
    near_weight = spread(near_weight, HALO)
    halves = [near_kappa_0[...], near_kappa_1[...], near_current_0[...], near_current_1[...]]
    halves = jnp.concatenate(halves, axis=0).reshape(2 * rows * HALO, cells)
    beside_ref[...] = gather(halves, select_ref[1]).reshape(beside_ref.shape)
    kind = wall_ref[...]
    share = jnp.where(kind == 0, 0.5, jnp.where(kind == 1, 0.25, 0.0))
    at_wall = lax.axis_index("normal") == 0
    boundary = jnp.where(at_wall, share, 0.5)
    source = jnp.broadcast_to(source_ref[...], (groups, groups)).T * jnp.where(at_wall, share, 0.0)
    table = emit_ref[...]
    for pair in range(rows // 2):
        both = jnp.concatenate([turned_ref[2 * pair], turned_ref[2 * pair + 1]], axis=1)
        product = jnp.dot(table, both, preferred_element_type=jnp.float32)
        for k in range(2):
            emission_ref[row_of(2 * pair + k, rows)] = product[:, k * cells : (k + 1) * cells]
    emission_ref[0] = emission_ref[0] + source

    @pl.loop(0, rows // 4)
    def _(quad):
        here = pl.ds(quad * 4, 4)
        planes = jnp.concatenate([kappa_ref[here], current_ref[here]], axis=0).reshape(8 * groups, cells)
        found = gather(planes, select_ref[0])
        for k in range(4):
            r = quad * 4 + k
            kappa = mine_ref[r]
            for s in range(4):
                couple = near_weight[s] * inverse(kappa + cut(beside_ref[0, r], s))
                near_couple_ref[s, r] = couple
                term = couple * cut(beside_ref[1, r], s)
                near_total = couple if s == 0 else near_total + couple
                near_term = term if s == 0 else near_term + term
            kappa = kappa_ref[r]
            total = kappa + unpack(near_total, low_near)
            if k == 0:
                total = total + jnp.where(r == 0, boundary, 0.0)
            rhs = emission_ref[r] + unpack(near_term, low_near)
            for s in range(4):
                couple = weight[s] * inverse(kappa + cut(found[k * groups : (k + 1) * groups], s))
                couple_ref[s, r] = couple
                total = total + couple
                rhs = rhs + couple * cut(found[(4 + k) * groups : (5 + k) * groups], s)
            base_ref[r] = total
            rhs_ref[r] = rhs
            face_ref[r] = FACE * inverse(kappa_ref[jnp.maximum(r - 1, 0)] + kappa)


def own_again_kernel(current_ref, near_ref, emission_ref, couple_ref, near_couple_ref, select_ref, rhs_ref, beside_ref):
    rows, groups, cells = current_ref.shape
    low_near = 1 - odd_surf()
    beside_ref[...] = gather(near_ref[low_near].reshape(rows * HALO, cells), select_ref[1]).reshape(beside_ref.shape)

    @pl.loop(0, rows // 4)
    def _(quad):
        found = gather(current_ref[pl.ds(quad * 4, 4)].reshape(4 * groups, cells), select_ref[0])
        for k in range(4):
            r = quad * 4 + k
            for s in range(4):
                term = near_couple_ref[s, r] * cut(beside_ref[r], s)
                near_term = term if s == 0 else near_term + term
            rhs = emission_ref[r] + unpack(near_term, low_near)
            for s in range(4):
                rhs = rhs + couple_ref[s, r] * cut(found[k * groups : (k + 1) * groups], s)
            rhs_ref[r] = rhs


def halo_terms(halo_ref, couple_ref, select_ref, found_ref, total_ref):
    rows = total_ref.shape[0]
    found_ref[...] = gather(halo_ref[...].reshape(rows * HALO, LANES), select_ref[2]).reshape(found_ref.shape)
    for r in range(rows):
        total = None
        for s in range(4):
            term = couple_ref[s, r] * cut(found_ref[r], s)
            total = term if s == 0 else total + term
        total_ref[r] = total


def first_kernel(base_ref, face_ref, rhs_ref, mine_ref, far_ref, select_ref, weight_ref, edge_ref, other_edge_ref, couple_ref, pivot_ref, carried_ref, solved_ref, ends_ref, meeting_ref, found_ref, total_ref, term_ref):
    rows, groups, cells = base_ref.shape
    meeting_ref[...] = FACE * inverse(edge_ref[...] + other_edge_ref[...])
    high = odd_surf()
    found_ref[...] = gather(far_ref[...].reshape(2 * rows * HALO, cells), select_ref[2]).reshape(found_ref.shape)
    weight = spread(weight_ref[...], HALO)
    for r in range(rows):
        kappa = mine_ref[0, r]
        for s in range(4):
            couple = weight[s] * inverse(kappa + cut(found_ref[r], s))
            couple_ref[s, r] = couple
            term = couple * cut(found_ref[rows + r], s)
            total = couple if s == 0 else total + couple
            terms = term if s == 0 else terms + term
        total_ref[r] = total
        term_ref[r] = terms

    @pl.loop(0, groups // CHUNK)
    def _(part):
        here = pl.ds(pl.multiple_of(part * CHUNK, CHUNK), CHUNK)
        quarters = [part * (CHUNK // HALO) + k for k in range(CHUNK // HALO)]
        schur = None
        carried = None
        solved = None
        for r in range(rows):
            base = base_ref[r, here, :] + unpack(total_ref[r], high, quarters)
            rhs = rhs_ref[r, here, :] + unpack(term_ref[r], high, quarters)
            if r == 0:
                schur = base
            else:
                schur = base + schur * carried
                rhs = rhs + face_ref[r, here, :] * solved
            if r == rows - 1:
                ends_ref[0, here, :] = schur
                ends_ref[1, here, :] = rhs
            else:
                after = face_ref[r + 1, here, :]
                pivot = inverse(schur + after)
                carried = after * pivot
                solved = rhs * pivot
                pivot_ref[r, here, :] = pivot
                carried_ref[r, here, :] = carried
                solved_ref[r, here, :] = solved


def meet_kernel(ends_ref, other_ref, meeting_ref, carried_ref, solved_ref, current_ref, far_ref, mix_ref):
    rows, groups, cells = current_ref.shape
    odd = odd_surf()
    face = meeting_ref[...]
    own, other = ends_ref[0], other_ref[0]
    scale = inverse(own * other + face * (own + other))
    mine = (other + face) * scale
    theirs = face * scale
    mix_ref[0] = mine
    mix_ref[1] = theirs
    value = mine * ends_ref[1] + theirs * other_ref[1]
    current_ref[rows - 1] = value
    far_ref[rows - 1] = pack(value, odd)
    for r in range(rows - 2, -1, -1):
        value = solved_ref[r] + carried_ref[r] * value
        current_ref[r] = value
        far_ref[r] = pack(value, odd)


def near_again_kernel(current_ref, near_ref):
    low_near = 1 - odd_surf()
    for r in range(current_ref.shape[0]):
        near_ref[r] = pack(current_ref[r], low_near)


def again_kernel(rhs_ref, far_ref, couple_ref, select_ref, pivot_ref, face_ref, solved_ref, end_ref, found_ref, total_ref):
    rows, groups, cells = rhs_ref.shape
    high = odd_surf()
    halo_terms(far_ref, couple_ref, select_ref, found_ref, total_ref)

    @pl.loop(0, groups // CHUNK)
    def _(part):
        here = pl.ds(pl.multiple_of(part * CHUNK, CHUNK), CHUNK)
        quarters = [part * (CHUNK // HALO) + k for k in range(CHUNK // HALO)]
        solved = None
        for r in range(rows):
            rhs = rhs_ref[r, here, :] + unpack(total_ref[r], high, quarters)
            if r > 0:
                rhs = rhs + face_ref[r, here, :] * solved
            if r == rows - 1:
                end_ref[here, :] = rhs
            else:
                solved = rhs * pivot_ref[r, here, :]
                solved_ref[r, here, :] = solved


def last_kernel(end_ref, other_ref, mix_ref, carried_ref, solved_ref, out_hbm, lines_ref, sems):
    rows, groups, cells = carried_ref.shape
    copies = []
    step = groups // 4
    for part in range(4):
        start = part * step
        here = pl.ds(start, step)
        value = mix_ref[0, here, :] * end_ref[here, :] + mix_ref[1, here, :] * other_ref[here, :]
        lines_ref[pl.ds(start * rows + row_of(rows - 1, rows), step, stride=rows), :] = value
        for r in range(rows - 2, -1, -1):
            value = solved_ref[r, here, :] + carried_ref[r, here, :] * value
            lines_ref[pl.ds(start * rows + row_of(r, rows), step, stride=rows), :] = value
        there = pl.ds(start * rows, step * rows)
        copies.append(pltpu.make_async_copy(lines_ref.at[there], out_hbm.at[there], sems.at[part]))
        copies[-1].start()
    for copy in copies:
        copy.wait()


VMEM = pl.BlockSpec(memory_space=pltpu.VMEM)
HBM = pl.BlockSpec(memory_space=pltpu.HBM)


def call(kernel, outs, *args, space=VMEM, out_space=VMEM, scratch=()):
    return pl.pallas_call(
        kernel,
        out_shape=[jax.ShapeDtypeStruct(out, jnp.float32) if isinstance(out, tuple) else out for out in outs],
        in_specs=[space] * len(args),
        out_specs=[out_space] * len(outs),
        scratch_shapes=list(scratch),
        compiler_params=pltpu.CompilerParams(vmem_limit_bytes=LIMIT),
    )(*args)


def like(value):
    return jax.ShapeDtypeStruct(value.shape, value.dtype)


def in_hbm(*values):
    return [pltpu.with_memory_space_constraint(value, pltpu.HBM) for value in values]


def far_pairs(count):
    pairs = []
    for block in range(2):
        for i in range(count):
            if i in (0, count - 1):
                pairs.append((block * count + i, (1 - block) * count + count - 1 - i))
            else:
                pairs.append((block * count + i, block * count + (i + 1 if i % 2 else i - 1)))
    return pairs


def body(populations, absorb_table, emit_table, energy, wall_source, neighbours, wall_type):
    levels, rows, cells = populations.shape
    groups = absorb_table.shape[0]
    whole = (rows, groups, cells)
    plane = (groups, cells)
    side = (rows, HALO, cells)
    found = pltpu.VMEM((rows, HALO, 4 * LANES), jnp.float32)
    found_both = pltpu.VMEM((2 * rows, HALO, 4 * LANES), jnp.float32)
    sums = pltpu.VMEM(side, jnp.float32)
    count = lax.axis_size("surf")
    far = far_pairs(count)
    near = [[i, i + 1] for i in range(0, count, 2)]
    swap = [(0, 1), (1, 0)]
    lines = energy.reshape(groups * rows, cells)
    places = neighbours.T
    walls = wall_type.reshape(1, cells)
    sources = wall_source.reshape(1, groups)

    kappa, turned, mine, edge, emit, lines, places, walls, sources = call(
        kappa_kernel,
        [
            whole, jax.ShapeDtypeStruct((rows, levels, cells), populations.dtype), (2,) + side, plane,
            like(emit_table), like(lines), like(places), like(walls), like(sources),
        ],
        *in_hbm(populations, absorb_table, emit_table, lines, places, walls, sources),
        space=HBM,
        scratch=[
            pltpu.VMEM(populations.shape, populations.dtype),
            pltpu.VMEM(absorb_table.shape, absorb_table.dtype),
            pltpu.SemaphoreType.DMA((13,)),
        ],
    )
    far_both = lax.ppermute(mine, ("normal", "surf"), far)
    other_edge = lax.ppermute(edge, "normal", swap)
    current, near_kappa, *halves = call(near_kernel, [whole, side] + [(rows // 2, HALO, cells)] * 4, lines, kappa)
    halves = [lax.ppermute(half, "surf", [(i, i ^ 1) for i in range(count)]) for half in halves]
    base, face, emission, rhs, own_couple, near_couple, select, weight = call(
        own_kernel,
        [
            whole, whole, whole, whole, (4,) + whole, (4,) + side,
            jax.ShapeDtypeStruct((3, 2 * LANES, 4 * LANES), jnp.bfloat16), (4, LANES),
        ],
        kappa, current, *halves, near_kappa, turned, emit, sources, places, walls,
        scratch=[pltpu.VMEM((2, rows, HALO, 4 * LANES), jnp.float32)],
    )
    far_couple, pivot, carried, solved, ends, meeting = call(
        first_kernel, [(4,) + side, whole, whole, whole, (2,) + plane, plane],
        base, face, rhs, mine, far_both, select, weight, edge, other_edge,
        scratch=[found_both, sums, sums],
    )
    other_ends = lax.ppermute(ends, "normal", swap)
    current, far_mine, mix = call(
        meet_kernel, [whole, side, (2,) + plane], ends, other_ends, meeting, carried, solved
    )
    far_current = lax.ppermute(far_mine, ("normal", "surf"), far)
    (near_mine,) = call(near_again_kernel, [side], current)
    beside = lax.all_gather(near_mine, "surf", axis_index_groups=near)
    (rhs,) = call(
        own_again_kernel, [whole], current, beside, emission, own_couple, near_couple, select, scratch=[found]
    )
    solved, end = call(
        again_kernel, [whole, plane], rhs, far_current, far_couple, select, pivot, face, scratch=[found, sums]
    )
    other_end = lax.ppermute(end, "normal", swap)
    (out,) = call(
        last_kernel, [lines.shape], end, other_end, mix, carried, solved,
        out_space=HBM,
        scratch=[pltpu.VMEM(lines.shape, jnp.float32), pltpu.SemaphoreType.DMA((4,))],
    )
    return out.reshape(groups, rows, cells)


def solution(mesh):
    return jax.shard_map(
        body,
        mesh=mesh,
        in_specs=(
            P(None, "normal", "surf"),
            P(),
            P(),
            P(None, "normal", "surf"),
            P(),
            P("surf", None),
            P("surf"),
        ),
        out_specs=P(None, "normal", "surf"),
        check_vma=False,
    )
```

time: 46.5 us -> 45.1 us (0.970)
  blocking collectives: 0 us -> 2.18 us
  waiting for transfers between devices: 14.8 us -> 12.8 us
  local copies, waits for them, and re-layouts: 1.34 us -> 0 us
  starting transfers between devices: 18.6 us -> 17.9 us
    all_gather x0 -> x1, blocking collectives: none -> 2.18 us  [body(): beside = lax.all_gather(near_mine, 'surf', axis_index_groups=near)]
    ppermute x4 -> x6, waiting for transfers between devices: 6.35 us -> 4.82 us  [the longest x1 2.3 us: body(): far_current = lax.ppermute(far_mine, ('normal', 'surf'), far)]
    unnamed x4 -> x0, local copies, waits for them, and re-layouts: 1.34 us -> none
    ppermute x1, starting transfers between devices: 1.62 us -> 0.68 us  [body(): other_ends = lax.ppermute(ends, 'normal', swap)]
    pallas_call x7 -> x9, Pallas kernels: 11.6 us -> 12 us  [call(): pl.pallas_call(kernel, out_shape=[jax.ShapeDtypeStruct(out, jnp.float32)...]
    ppermute x4 -> x6, starting transfers between devices: 14.6 us -> 14.6 us  [the longest x1 8.76 us: body(): far_both = lax.ppermute(mine, ('normal', 'surf'), far)]
  transfers between devices with their start and end apart: 7 -> 9, of which waited for: 5 -> 5; matrix products, arithmetic and copies ran while one was open for 0% -> 0% of each run, Pallas kernels for 9% -> 13%
where the time goes in v3:
time: 45.1 us; the launch traced here: 44.9 us
  starting transfers between devices  17.9 us (40%)
  waiting for transfers between devices  12.8 us (28%)
  Pallas kernels  12 us (27%)
  blocking collectives  2.18 us (5%)
    pallas_call x9, Pallas kernels, call(): pl.pallas_call(kernel, out_shape=[jax.ShapeDtypeStruct(out, jnp.float32)...  12 us
    ppermute x1, starting transfers between devices, body(): far_both = lax.ppermute(mine, ('normal', 'surf'), far)  8.76 us
    ppermute x1, starting transfers between devices, body(): far_current = lax.ppermute(far_mine, ('normal', 'surf'), far)  4.78 us
    ppermute x1, waiting for transfers between devices, body(): other_ends = lax.ppermute(ends, 'normal', swap)  4.37 us
    ppermute x1, waiting for transfers between devices, body(): other_end = lax.ppermute(end, 'normal', swap)  3.56 us
    ppermute x1, waiting for transfers between devices, body(): far_current = lax.ppermute(far_mine, ('normal', 'surf'), far)  2.3 us
    ppermute x1, waiting for transfers between devices, body(): far_both = lax.ppermute(mine, ('normal', 'surf'), far)  2.19 us
    all_gather x1, blocking collectives, body(): beside = lax.all_gather(near_mine, 'surf', axis_index_groups=near)  2.18 us
  transfers between devices with their start and end apart: 9, of which 5 were waited for; matrix products, arithmetic and copies ran while one was open for 0% of the time, Pallas kernels for 13%

profile of v3, /device:TPU:2, one launch (start us, length us, event | category | flops | bytes accessed | tf_op | source)
XLA Modules:
  0.0 44.9 jit_solution(299688617941509789)
XLA Ops:
  0.0 2.5 %shard_map.73 = (f32[16,128,128]{2,1,0:T(8,128)S(1)}, bf16[16,256,128]{2,1,0:T(8,128)(2,1)S(1)}, f32[2,16,32,128]{3,2,1,0:T(8,128)S(1)}, f32[128,128]{1,0:T(8,12...) custom-call(bf16[256,16,128]{2,1,0:T(8,128)(2,1)} %pops_hbm.1, ...), custom_call_target="tpu_custom_call" | custom-call | tf_op jit(solution)/shard_map/pallas_call | solution.py:355
  2.5 8.8 %collective-permute-start.4 = (f32[2,16,32,128]{3,2,1,0:T(8,128)S(1)}, f32[2,16,32,128]{3,2,1,0:T(8,128)S(1)}, u32[]{:S(2)}, u32[]{:S(2)}) collective-permute-start(f32[2,16,32,128]{3,2,1,0:T(8,128)S(1)} %get-tuple-element.55.mine_ref), channel_id=1, source_target_pairs={{0,255},{1,2},{2,1},{3,4},{4,3},{5,6},{6,5},{7,8},{8,7},{9,10},{10... | collective-permute-start | bytes 1572872 | tf_op jit(solution)/shard_map/ppermute | solution.py:416
  11.3 0.7 %shard_map.74 = (f32[16,128,128]{2,1,0:T(8,128)S(1)}, f32[16,32,128]{2,1,0:T(8,128)S(1)}, f32[8,32,128]{2,1,0:T(8,128)S(1)}, f32[8,32,128]{2,1,0:T(8,128)S(1)}, ...) custom-call(f32[2048,128]{1,0:T(8,128)S(1)} %get-tuple-element.40.lines_ref, ...), custom_call_target="tpu_custom_call" | custom-call | tf_op jit(solution)/shard_map/pallas_call | solution.py:355
  12.0 0.1 collective-permute-start
  12.1 0.5 %collective-permute-start.1 = (f32[8,32,128]{2,1,0:T(8,128)S(1)}, f32[8,32,128]{2,1,0:T(8,128)S(1)}, u32[]{:S(2)}, u32[]{:S(2)}) collective-permute-start(f32[8,32,128]{2,1,0:T(8,128)S(1)} %get-tuple-element.43), channel_id=1, source_target_pairs={{0,1},{1,0},{2,3},{3,2},{4,5},{5,4},{6,7},{7,6},{8,9},{9,8},{10,11... | collective-permute-start | bytes 393224 | tf_op jit(solution)/shard_map/ppermute | solution.py:419
  12.6 0.1 collective-permute-start.2
  12.7 0.4 collective-permute-start.3
  13.1 0.3 collective-permute-done.near_kappa_0
  13.4 1.8 %collective-permute-start.5 = (f32[128,128]{1,0:T(8,128)S(1)}, f32[128,128]{1,0:T(8,128)S(1)}, u32[]{:S(2)}, u32[]{:S(2)}) collective-permute-start(f32[128,128]{1,0:T(8,128)S(1)} %get-tuple-element.58.edge_ref), channel_id=1, source_target_pairs={{0,128},{128,0},{1,129},{129,1},{2,130},{130,2},{3,131},{131,3},{4... | collective-permute-start | bytes 196616 | tf_op jit(solution)/shard_map/ppermute | solution.py:417
  15.3 0.0 collective-permute-done.1.near_kappa_1
  15.3 0.0 collective-permute-done.2.near_current_0
  15.3 0.0 collective-permute-done.3.near_current_1
  15.3 3.3 %shard_map.75 = (f32[16,128,128]{2,1,0:T(8,128)S(1)}, f32[16,128,128]{2,1,0:T(8,128)S(1)}, f32[16,128,128]{2,1,0:T(8,128)S(1)}, f32[16,128,128]{2,1,0:T(8,128)S(...) custom-call(f32[16,128,128]{2,1,0:T(8,128)S(1)} %get-tuple-element.3, ...), custom_call_target="tpu_custom_call" | custom-call | tf_op jit(solution)/shard_map/pallas_call | solution.py:355
  18.6 0.0 collective-permute-done.5.other_edge_ref
  18.6 2.2 %collective-permute-done.4.far_ref = f32[2,16,32,128]{3,2,1,0:T(8,128)S(1)} collective-permute-done((f32[2,16,32,128]{3,2,1,0:T(8,128)S(1)}, f32[2,16,32,128]{3,2,1,0:T(8,128)S(1)}, u32[]{:S(2)}, u32[]{:S(2)}) %collective-permute-start.4) | collective-permute-done | bytes 524320 | tf_op jit(solution)/shard_map/ppermute | solution.py:416
  20.8 1.3 %shard_map.76 = (f32[4,16,32,128]{3,2,1,0:T(8,128)S(1)}, f32[16,128,128]{2,1,0:T(8,128)S(1)}, f32[16,128,128]{2,1,0:T(8,128)S(1)}, f32[16,128,128]{2,1,0:T(8,128...) custom-call(f32[16,128,128]{2,1,0:T(8,128)S(1)} %get-tuple-element.52.base_ref, ...), custom_call_target="tpu_custom_call" | custom-call | tf_op jit(solution)/shard_map/pallas_call | solution.py:355
  22.1 0.7 %collective-permute-start.6 = (f32[2,128,128]{2,1,0:T(8,128)S(1)}, f32[2,128,128]{2,1,0:T(8,128)S(1)}, u32[]{:S(2)}, u32[]{:S(2)}) collective-permute-start(f32[2,128,128]{2,1,0:T(8,128)S(1)} %get-tuple-element.59.ends_ref), channel_id=1, source_target_pairs={{0,128},{128,0},{1,129},{129,1},{2,130},{130,2},{3,131},{131,3},{4... | collective-permute-start | bytes 393224 | tf_op jit(solution)/shard_map/ppermute | solution.py:434
  22.7 4.4 %collective-permute-done.6.other_ref = f32[2,128,128]{2,1,0:T(8,128)S(1)} collective-permute-done((f32[2,128,128]{2,1,0:T(8,128)S(1)}, f32[2,128,128]{2,1,0:T(8,128)S(1)}, u32[]{:S(2)}, u32[]{:S(2)}) %collective-permute-start.6) | collective-permute-done | bytes 131104 | tf_op jit(solution)/shard_map/ppermute | solution.py:434
  27.1 0.4 shard_map.77
  27.5 4.8 %collective-permute-start.7 = (f32[16,32,128]{2,1,0:T(8,128)S(1)}, f32[16,32,128]{2,1,0:T(8,128)S(1)}, u32[]{:S(2)}, u32[]{:S(2)}) collective-permute-start(f32[16,32,128]{2,1,0:T(8,128)S(1)} %get-tuple-element.67), channel_id=1, source_target_pairs={{0,255},{1,2},{2,1},{3,4},{4,3},{5,6},{6,5},{7,8},{8,7},{9,10},{10... | collective-permute-start | bytes 786440 | tf_op jit(solution)/shard_map/ppermute | solution.py:438
  32.3 0.3 shard_map.78
  32.6 2.2 %all-gather = f32[32,32,128]{2,1,0:T(8,128)S(1)} all-gather(f32[16,32,128]{2,1,0:T(8,128)S(1)} %shard_map.78), channel_id=2, replica_groups={{0,1},{2,3},{4,5},{6,7},{8,9},{10,11},{12,13},{14,15},{16,17},{18,19},{..., dimensions={0}, use_global_device_ids=true | all-gather | bytes 786432 | tf_op jit(solution)/shard_map/all_gather | solution.py:440
  34.8 1.6 %shard_map.79.rhs_ref = f32[16,128,128]{2,1,0:T(8,128)S(1)} custom-call(f32[16,128,128]{2,1,0:T(8,128)S(1)} %get-tuple-element.63.current_ref, f32[2,16,32,128]{3,2,1,0:T(8,128)S(1)} %bitcast.6, f32[16,128,128]{2,1,0:T(8,128)S(1)} %get-tuple-element.64.emission_ref, f32[4,16,128,128]{3,2,1,0:T(8,128)S(1)} %get-tuple-element.65.couple_ref, ...), custom_call_target="tpu_custom_call" | custom-call | tf_op jit(solution)/shard_map/pallas_call | solution.py:355
  36.4 2.3 %collective-permute-done.7.far_ref = f32[16,32,128]{2,1,0:T(8,128)S(1)} collective-permute-done((f32[16,32,128]{2,1,0:T(8,128)S(1)}, f32[16,32,128]{2,1,0:T(8,128)S(1)}, u32[]{:S(2)}, u32[]{:S(2)}) %collective-permute-start.7) | collective-permute-done | bytes 262176 | tf_op jit(solution)/shard_map/ppermute | solution.py:438
  38.7 0.7 %shard_map.80 = (f32[16,128,128]{2,1,0:T(8,128)S(1)}, f32[128,128]{1,0:T(8,128)S(1)}) custom-call(f32[16,128,128]{2,1,0:T(8,128)S(1)} %shard_map.79.rhs_ref, f32[16,32,128]{2,1,0:T(8,128)S(1)} %collective-permute-done.7.far_ref, f32[4,16,32,128]{3,2,1,0:T(8,128)S(1)} %get-tuple-element.68.couple_ref, bf16[3,256,512]{2,1,0:T(8,128)(2,1)S(1)} %get-tuple-element.56.select_ref, ...), custom_call_target="tpu_custom_call" | custom-call | tf_op jit(solution)/shard_map/pallas_call | solution.py:355
  39.5 0.8 %collective-permute-start.8 = (f32[128,128]{1,0:T(8,128)S(1)}, f32[128,128]{1,0:T(8,128)S(1)}, u32[]{:S(2)}, u32[]{:S(2)}) collective-permute-start(f32[128,128]{1,0:T(8,128)S(1)} %get-tuple-element.70.end_ref), channel_id=1, source_target_pairs={{0,128},{128,0},{1,129},{129,1},{2,130},{130,2},{3,131},{131,3},{4... | collective-permute-start | bytes 196616 | tf_op jit(solution)/shard_map/ppermute | solution.py:447
  40.2 3.6 %collective-permute-done.8.other_ref = f32[128,128]{1,0:T(8,128)S(1)} collective-permute-done((f32[128,128]{1,0:T(8,128)S(1)}, f32[128,128]{1,0:T(8,128)S(1)}, u32[]{:S(2)}, u32[]{:S(2)}) %collective-permute-start.8) | collective-permute-done | bytes 65568 | tf_op jit(solution)/shard_map/ppermute | solution.py:447
  43.8 1.1 %shard_map.81 = f32[2048,128]{1,0:T(8,128)} custom-call(f32[128,128]{1,0:T(8,128)S(1)} %get-tuple-element.70.end_ref, f32[128,128]{1,0:T(8,128)S(1)} %collective-permute-done.8.other_ref, f32[2,128,128]{2,1,0:T(8,128)S(1)} %get-tuple-element.71.mix_ref, f32[16,128,128]{2,1,0:T(8,128)S(1)} %get-tuple-element.61.carried_ref, ...), custom_call_target="tpu_custom_call" | custom-call | tf_op jit(solution)/shard_map/pallas_call | solution.py:355
Async XLA Ops:
  2.5 18.3 %collective-permute-start.4 = (f32[2,16,32,128]{3,2,1,0:T(8,128)S(1)}, f32[2,16,32,128]{3,2,1,0:T(8,128)S(1)}, u32[]{:S(2)}, u32[]{:S(2)}) collective-permute-start(f32[2,16,32,128]{3,2,1,0:T(8,128)S(1)} %get-tuple-element.55.mine_ref), channel_id=1, source_target_pairs={{0,255},{1,2},{2,1},{3,4},{4,3},{5,6},{6,5},{7,8},{8,7},{9,10},{10... | collective-permute-start | bytes 1572872 | tf_op jit(solution)/shard_map/ppermute | solution.py:416
  12.0 1.4 %collective-permute-start = (f32[8,32,128]{2,1,0:T(8,128)S(1)}, f32[8,32,128]{2,1,0:T(8,128)S(1)}, u32[]{:S(2)}, u32[]{:S(2)}) collective-permute-start(f32[8,32,128]{2,1,0:T(8,128)S(1)} %get-tuple-element.42), channel_id=1, source_target_pairs={{0,1},{1,0},{2,3},{3,2},{4,5},{5,4},{6,7},{7,6},{8,9},{9,8},{10,11... | collective-permute-start | bytes 393224 | tf_op jit(solution)/shard_map/ppermute | solution.py:419
  12.1 3.2 %collective-permute-start.1 = (f32[8,32,128]{2,1,0:T(8,128)S(1)}, f32[8,32,128]{2,1,0:T(8,128)S(1)}, u32[]{:S(2)}, u32[]{:S(2)}) collective-permute-start(f32[8,32,128]{2,1,0:T(8,128)S(1)} %get-tuple-element.43), channel_id=1, source_target_pairs={{0,1},{1,0},{2,3},{3,2},{4,5},{5,4},{6,7},{7,6},{8,9},{9,8},{10,11... | collective-permute-start | bytes 393224 | tf_op jit(solution)/shard_map/ppermute | solution.py:419
  12.6 2.7 %collective-permute-start.2 = (f32[8,32,128]{2,1,0:T(8,128)S(1)}, f32[8,32,128]{2,1,0:T(8,128)S(1)}, u32[]{:S(2)}, u32[]{:S(2)}) collective-permute-start(f32[8,32,128]{2,1,0:T(8,128)S(1)} %get-tuple-element.44), channel_id=1, source_target_pairs={{0,1},{1,0},{2,3},{3,2},{4,5},{5,4},{6,7},{7,6},{8,9},{9,8},{10,11... | collective-permute-start | bytes 393224 | tf_op jit(solution)/shard_map/ppermute | solution.py:419
  12.7 2.6 %collective-permute-start.3 = (f32[8,32,128]{2,1,0:T(8,128)S(1)}, f32[8,32,128]{2,1,0:T(8,128)S(1)}, u32[]{:S(2)}, u32[]{:S(2)}) collective-permute-start(f32[8,32,128]{2,1,0:T(8,128)S(1)} %get-tuple-element.45), channel_id=1, source_target_pairs={{0,1},{1,0},{2,3},{3,2},{4,5},{5,4},{6,7},{7,6},{8,9},{9,8},{10,11... | collective-permute-start | bytes 393224 | tf_op jit(solution)/shard_map/ppermute | solution.py:419
  13.4 5.2 %collective-permute-start.5 = (f32[128,128]{1,0:T(8,128)S(1)}, f32[128,128]{1,0:T(8,128)S(1)}, u32[]{:S(2)}, u32[]{:S(2)}) collective-permute-start(f32[128,128]{1,0:T(8,128)S(1)} %get-tuple-element.58.edge_ref), channel_id=1, source_target_pairs={{0,128},{128,0},{1,129},{129,1},{2,130},{130,2},{3,131},{131,3},{4... | collective-permute-start | bytes 196616 | tf_op jit(solution)/shard_map/ppermute | solution.py:417
  22.1 5.1 %collective-permute-start.6 = (f32[2,128,128]{2,1,0:T(8,128)S(1)}, f32[2,128,128]{2,1,0:T(8,128)S(1)}, u32[]{:S(2)}, u32[]{:S(2)}) collective-permute-start(f32[2,128,128]{2,1,0:T(8,128)S(1)} %get-tuple-element.59.ends_ref), channel_id=1, source_target_pairs={{0,128},{128,0},{1,129},{129,1},{2,130},{130,2},{3,131},{131,3},{4... | collective-permute-start | bytes 393224 | tf_op jit(solution)/shard_map/ppermute | solution.py:434
  27.5 11.2 %collective-permute-start.7 = (f32[16,32,128]{2,1,0:T(8,128)S(1)}, f32[16,32,128]{2,1,0:T(8,128)S(1)}, u32[]{:S(2)}, u32[]{:S(2)}) collective-permute-start(f32[16,32,128]{2,1,0:T(8,128)S(1)} %get-tuple-element.67), channel_id=1, source_target_pairs={{0,255},{1,2},{2,1},{3,4},{4,3},{5,6},{6,5},{7,8},{8,7},{9,10},{10... | collective-permute-start | bytes 786440 | tf_op jit(solution)/shard_map/ppermute | solution.py:438
  39.5 4.4 %collective-permute-start.8 = (f32[128,128]{1,0:T(8,128)S(1)}, f32[128,128]{1,0:T(8,128)S(1)}, u32[]{:S(2)}, u32[]{:S(2)}) collective-permute-start(f32[128,128]{1,0:T(8,128)S(1)} %get-tuple-element.70.end_ref), channel_id=1, source_target_pairs={{0,128},{128,0},{1,129},{129,1},{2,130},{130,2},{3,131},{131,3},{4... | collective-permute-start | bytes 196616 | tf_op jit(solution)/shard_map/ppermute | solution.py:447

commit v4 on v3

v4 whole, which is shorter than its diff:
```python
import functools

import jax
import jax.numpy as jnp
from jax import lax
from jax.experimental import pallas as pl
from jax.experimental.pallas import tpu as pltpu
from jax.sharding import PartitionSpec as P

HALO = 32
LANES = 128
HALF = 64
SURF_WEIGHT = 0.02
FACE = 2.0 / 3.0
LIMIT = 32 * 1024 * 1024
ACROSS = (False, True, False, False)


def inverse(value):
    guess = pl.reciprocal(value, approx=True)
    return guess * (2.0 - value * guess)


def lane_ids(rows):
    return lax.broadcasted_iota(jnp.int32, (rows, LANES), 1)


def gather(value, select):
    high = value.astype(jnp.bfloat16)
    low = (value - high.astype(jnp.float32)).astype(jnp.bfloat16)
    return jnp.dot(jnp.concatenate([high, low], axis=1), select, preferred_element_type=jnp.float32)


def selection(lanes):
    source = lax.broadcasted_iota(jnp.int32, (LANES, LANES), 0)
    parts = [jnp.where(source == lanes[s : s + 1], 1.0, 0.0).astype(jnp.bfloat16) for s in range(4)]
    one = jnp.concatenate(parts, axis=1)
    return jnp.concatenate([one, one], axis=0)


def cut(value, s):
    return value[:, s * LANES : (s + 1) * LANES]


def row_of(position, count):
    block = lax.axis_index("normal")
    return position + block * (count - 1 - 2 * position)


def odd_surf():
    return lax.rem(lax.axis_index("surf"), 2)


def pack(plane, high):
    size = plane.shape[0] // 4
    slot = lane_ids(size) // HALO
    packed = None
    for k in range(4):
        turned = pltpu.roll(plane[k * size : (k + 1) * size], HALO * lax.rem(k + high, 4), 1)
        packed = turned if k == 0 else jnp.where(slot == k, turned, packed)
    return packed


def local_places(neighbours_ref):
    offset = lax.axis_index("surf") * LANES
    found = neighbours_ref[...]
    return found >= 0, found - offset


def spread(table, rows):
    return [jnp.broadcast_to(table[s : s + 1], (rows, LANES)) for s in range(4)]


def own_tables(neighbours_ref):
    valid, local = local_places(neighbours_ref)
    inside = valid & (local >= 0) & (local < LANES)
    return jnp.where(inside, local, -1), jnp.where(inside, SURF_WEIGHT * FACE, 0.0)


def side_tables(neighbours_ref, high):
    valid, local = local_places(neighbours_ref)
    slot = lane_ids(4) // HALO
    place = local + (HALO - high * (LANES + HALO))
    here = slot == 3 * high
    beyond = valid & here & (place >= 0) & (place < HALO)
    place = jnp.where(beyond, place, -LANES)
    weight = jnp.where(beyond, SURF_WEIGHT * FACE, 0.0)

    def repeat(value):
        value = jnp.where(here, value, 0)
        return value + pltpu.roll(value, HALO, 1) + pltpu.roll(value, 2 * HALO, 1) + pltpu.roll(value, 3 * HALO, 1)

    return repeat(place) + HALO * slot, repeat(weight)


def unpack(value, high):
    here = lane_ids(value.shape[0]) // HALO == 3 * high
    return jnp.concatenate(
        [jnp.where(here, pltpu.roll(value, HALO * lax.rem(4 - k - high, 4), 1), 0.0) for k in range(4)], axis=0
    )


def kappa_kernel(pops_hbm, absorb_hbm, emit_hbm, lines_hbm, places_hbm, walls_hbm, sources_hbm, kappa_ref, turned_ref, far_0, far_1, emit_ref, lines_ref, places_ref, walls_ref, sources_ref, pops_ref, table_ref, sems):
    rows, groups, cells = kappa_ref.shape
    levels = pops_ref.shape[0]
    pieces = 4
    step = levels // pieces
    pairs = []
    for piece in range(pieces):
        here = pl.ds(piece * step, step)
        pairs.append((pops_hbm.at[here], pops_ref.at[here]))
    pairs.append((absorb_hbm, table_ref))
    step = groups * rows // pieces
    for piece in range(pieces):
        there = pl.ds(piece * step, step)
        pairs.append((lines_hbm.at[there], lines_ref.at[there]))
    pairs += [(emit_hbm, emit_ref), (places_hbm, places_ref), (walls_hbm, walls_ref), (sources_hbm, sources_ref)]
    copies = [pltpu.make_async_copy(pair[0], pair[1], sems.at[i]) for i, pair in enumerate(pairs)]
    for copy in copies:
        copy.start()
    step = levels // pieces
    for piece in range(pieces):
        copies[piece].wait()
        here = pl.ds(piece * step, step)
        turned_ref[:, here, :] = jnp.swapaxes(pops_ref[here], 0, 1)
    copies[pieces].wait()
    table = table_ref[...]
    for pair in range(rows // 2):
        both = jnp.concatenate([turned_ref[2 * pair], turned_ref[2 * pair + 1]], axis=1)
        product = jnp.dot(table, both, preferred_element_type=jnp.float32)
        for k in range(2):
            kappa_ref[row_of(2 * pair + k, rows)] = product[:, k * cells : (k + 1) * cells]
    odd = odd_surf()
    half = groups // 2
    for r in range(rows):
        far_0[0, r] = pack(kappa_ref[r, :half], odd)
        far_1[0, r] = pack(kappa_ref[r, half:], odd)
    for copy in copies[pieces + 1 :]:
        copy.wait()
    for r in range(rows):
        far_0[1, r] = pack(lines_ref[pl.ds(row_of(r, rows), half, stride=rows), :], odd)
        far_1[1, r] = pack(lines_ref[pl.ds(half * rows + row_of(r, rows), half, stride=rows), :], odd)


def near_kernel(lines_ref, kappa_ref, neighbours_ref, current_ref, near_0, near_1, select_ref, weight_ref):
    rows, groups, cells = current_ref.shape
    half = groups // 2
    high = odd_surf()
    low_near = 1 - high
    for r in range(rows):
        current = lines_ref[pl.ds(row_of(r, rows), groups, stride=rows), :]
        current_ref[r] = current
        kappa = kappa_ref[r]
        near_0[0, r] = pack(kappa[:half], low_near)
        near_0[1, r] = pack(current[:half], low_near)
        near_1[0, r] = pack(kappa[half:], low_near)
        near_1[1, r] = pack(current[half:], low_near)
    lanes, weight = own_tables(neighbours_ref)
    select_ref[0] = selection(lanes)
    weight_ref[0] = weight
    lanes, weight = side_tables(neighbours_ref, low_near)
    select_ref[1] = selection(lanes)
    weight_ref[1] = weight
    lanes, weight = side_tables(neighbours_ref, high)
    select_ref[2] = selection(lanes)
    weight_ref[2] = weight


def own_kernel(kappa_ref, current_ref, turned_ref, emit_ref, source_ref, wall_ref, select_ref, weight_ref, base_ref, face_ref, emission_ref, rhs_ref, couple_ref):
    rows, groups, cells = kappa_ref.shape
    weight = spread(weight_ref[0], groups)
    kind = wall_ref[...]
    share = jnp.where(kind == 0, 0.5, jnp.where(kind == 1, 0.25, 0.0))
    at_wall = lax.axis_index("normal") == 0
    boundary = jnp.where(at_wall, share, 0.5)
    source = jnp.broadcast_to(source_ref[...], (groups, groups)).T * jnp.where(at_wall, share, 0.0)
    table = emit_ref[...]
    for pair in range(rows // 2):
        both = jnp.concatenate([turned_ref[2 * pair], turned_ref[2 * pair + 1]], axis=1)
        product = jnp.dot(table, both, preferred_element_type=jnp.float32)
        for k in range(2):
            emission_ref[row_of(2 * pair + k, rows)] = product[:, k * cells : (k + 1) * cells]
    emission_ref[0] = emission_ref[0] + source

    @pl.loop(0, rows // 4)
    def _(quad):
        here = pl.ds(quad * 4, 4)
        planes = jnp.concatenate([kappa_ref[here], current_ref[here]], axis=0).reshape(8 * groups, cells)
        found = gather(planes, select_ref[0])
        for k in range(4):
            r = quad * 4 + k
            kappa = kappa_ref[r]
            total = kappa + jnp.where(r == 0, boundary, 0.0) if k == 0 else kappa
            rhs = emission_ref[r]
            for s in range(4):
                couple = weight[s] * inverse(kappa + cut(found[k * groups : (k + 1) * groups], s))
                couple_ref[s, r] = couple
                total = total + couple
                rhs = rhs + couple * cut(found[(4 + k) * groups : (5 + k) * groups], s)
            base_ref[r] = total
            rhs_ref[r] = rhs
            face_ref[r] = FACE * inverse(kappa_ref[jnp.maximum(r - 1, 0)] + kappa)


def own_again_kernel(current_0, current_1, emission_ref, couple_ref, select_ref, rhs_ref):
    rows, groups, cells = emission_ref.shape

    @pl.loop(0, rows // 4)
    def _(quad):
        here = pl.ds(quad * 4, 4)
        planes = jnp.concatenate([current_0[here], current_1[here]], axis=1).reshape(4 * groups, cells)
        found = gather(planes, select_ref[0])
        for k in range(4):
            r = quad * 4 + k
            rhs = emission_ref[r]
            for s in range(4):
                rhs = rhs + couple_ref[s, r] * cut(found[k * groups : (k + 1) * groups], s)
            rhs_ref[r] = rhs


def find_sides(far, near, select_ref, found_ref):
    found_ref[0] = gather(far, select_ref[2]).reshape(found_ref.shape[1:])
    found_ref[1] = gather(near, select_ref[1]).reshape(found_ref.shape[1:])


def first_kernel(start, kappa_ref, base_ref, face_ref, rhs_ref, mine_ref, far_ref, near_mine_ref, near_ref, select_ref, weight_ref, *refs):
    couple_ref, pivot_ref, carried_ref, solved_ref, ends_ref, found_ref = refs[-6:]
    rows, groups, cells = pivot_ref.shape
    size = groups // 4
    here = pl.ds(start, groups)
    ends_ref[2] = kappa_ref[rows - 1, here]
    high = odd_surf()
    find_sides(far_ref[...].reshape(2 * rows * size, cells), near_ref[...].reshape(2 * rows * size, cells), select_ref, found_ref)
    weights = [spread(weight_ref[2], size), spread(weight_ref[1], size)]
    schur = None
    carried = None
    solved = None
    for r in range(rows):
        base = base_ref[r, here, :]
        rhs = rhs_ref[r, here, :]
        for side in range(2):
            kappa = (near_mine_ref if side else mine_ref)[0, r]
            for s in range(4):
                couple = weights[side][s] * inverse(kappa + cut(found_ref[side, r], s))
                couple_ref[side, s, r] = couple
                term = couple * cut(found_ref[side, rows + r], s)
                total = couple if s == 0 else total + couple
                terms = term if s == 0 else terms + term
            base = base + unpack(total, 1 - high if side else high)
            rhs = rhs + unpack(terms, 1 - high if side else high)
        if r == 0:
            schur = base
        else:
            schur = base + schur * carried
            rhs = rhs + face_ref[r, here, :] * solved
        if r == rows - 1:
            ends_ref[0] = schur
            ends_ref[1] = rhs
        else:
            after = face_ref[r + 1, here, :]
            pivot = inverse(schur + after)
            carried = after * pivot
            solved = rhs * pivot
            pivot_ref[r] = pivot
            carried_ref[r] = carried
            solved_ref[r] = solved


def meet_kernel(ends_ref, other_ref, carried_ref, solved_ref, current_ref, far_ref, near_ref, mix_ref):
    rows, groups, cells = current_ref.shape
    odd = odd_surf()
    face = FACE * inverse(ends_ref[2] + other_ref[2])
    own, other = ends_ref[0], other_ref[0]
    scale = inverse(own * other + face * (own + other))
    mine = (other + face) * scale
    theirs = face * scale
    mix_ref[0] = mine
    mix_ref[1] = theirs
    value = mine * ends_ref[1] + theirs * other_ref[1]
    current_ref[rows - 1] = value
    far_ref[rows - 1] = pack(value, odd)
    near_ref[rows - 1] = pack(value, 1 - odd)
    for r in range(rows - 2, -1, -1):
        value = solved_ref[r] + carried_ref[r] * value
        current_ref[r] = value
        far_ref[r] = pack(value, odd)
        near_ref[r] = pack(value, 1 - odd)


def again_kernel(start, rhs_ref, far_ref, near_ref, couple_ref, select_ref, pivot_ref, face_ref, *refs):
    solved_ref, end_ref, found_ref = refs[-3:]
    rows, groups, cells = pivot_ref.shape
    size = groups // 4
    here = pl.ds(start, groups)
    high = odd_surf()
    find_sides(far_ref[...].reshape(rows * size, cells), near_ref[...].reshape(rows * size, cells), select_ref, found_ref)
    solved = None
    for r in range(rows):
        rhs = rhs_ref[r, here, :]
        for side in range(2):
            for s in range(4):
                term = couple_ref[side, s, r] * cut(found_ref[side, r], s)
                terms = term if s == 0 else terms + term
            rhs = rhs + unpack(terms, 1 - high if side else high)
        if r > 0:
            rhs = rhs + face_ref[r, here, :] * solved
        if r == rows - 1:
            end_ref[...] = rhs
        else:
            solved = rhs * pivot_ref[r]
            solved_ref[r] = solved


def last_kernel(*refs):
    halves, (out_hbm, lines_ref, sems) = (refs[5:10], refs[:5]), refs[10:]
    copies = []
    start = 0
    for end_ref, other_ref, mix_ref, carried_ref, solved_ref in halves:
        rows, groups, cells = carried_ref.shape
        step = groups // 2
        for part in range(2):
            here = pl.ds(part * step, step)
            value = mix_ref[0, here, :] * end_ref[here, :] + mix_ref[1, here, :] * other_ref[here, :]
            lines_ref[pl.ds(start * rows + row_of(rows - 1, rows), step, stride=rows), :] = value
            for r in range(rows - 2, -1, -1):
                value = solved_ref[r, here, :] + carried_ref[r, here, :] * value
                lines_ref[pl.ds(start * rows + row_of(r, rows), step, stride=rows), :] = value
            there = pl.ds(start * rows, step * rows)
            copies.append(pltpu.make_async_copy(lines_ref.at[there], out_hbm.at[there], sems.at[len(copies)]))
            copies[-1].start()
            start = start + step
    for copy in copies:
        copy.wait()


VMEM = pl.BlockSpec(memory_space=pltpu.VMEM)
HBM = pl.BlockSpec(memory_space=pltpu.HBM)


def call(kernel, outs, *args, space=VMEM, out_space=VMEM, scratch=()):
    return pl.pallas_call(
        kernel,
        out_shape=[jax.ShapeDtypeStruct(out, jnp.float32) if isinstance(out, tuple) else out for out in outs],
        in_specs=[space] * len(args),
        out_specs=[out_space] * len(outs),
        scratch_shapes=list(scratch),
        compiler_params=pltpu.CompilerParams(vmem_limit_bytes=LIMIT),
    )(*args)


def like(value):
    return jax.ShapeDtypeStruct(value.shape, value.dtype)


def in_hbm(*values):
    return [pltpu.with_memory_space_constraint(value, pltpu.HBM) for value in values]


def far_pairs(count, across):
    pairs = []
    for block in range(2):
        for i in range(count):
            if i in (0, count - 1):
                other = count - 1 - i if across else i
                pairs.append((block * count + i, (1 - block) * count + other))
            else:
                pairs.append((block * count + i, block * count + (i + 1 if i % 2 else i - 1)))
    return pairs


def body(populations, absorb_table, emit_table, energy, wall_source, neighbours, wall_type):
    levels, rows, cells = populations.shape
    groups = absorb_table.shape[0]
    whole = (rows, groups, cells)
    plane = (groups, cells)
    side = (rows, HALO, cells)
    half = groups // 2
    half_whole = (rows, half, cells)
    half_side = (rows, HALO // 2, cells)
    found_half = pltpu.VMEM((2, rows, HALO // 2, 4 * LANES), jnp.float32)
    found_both = pltpu.VMEM((2, 2 * rows, HALO // 2, 4 * LANES), jnp.float32)
    count = lax.axis_size("surf")
    far = [far_pairs(count, across) for across in ACROSS]
    near = [(i, i ^ 1) for i in range(count)]
    swap = [(0, 1), (1, 0)]
    lines = energy.reshape(groups * rows, cells)
    places = neighbours.T
    walls = wall_type.reshape(1, cells)
    sources = wall_source.reshape(1, groups)

    kappa, turned, mine_0, mine_1, emit, lines, places, walls, sources = call(
        kappa_kernel,
        [
            whole, jax.ShapeDtypeStruct((rows, levels, cells), populations.dtype), (2,) + half_side, (2,) + half_side,
            like(emit_table), like(lines), like(places), like(walls), like(sources),
        ],
        *in_hbm(populations, absorb_table, emit_table, lines, places, walls, sources),
        space=HBM,
        scratch=[
            pltpu.VMEM(populations.shape, populations.dtype),
            pltpu.VMEM(absorb_table.shape, absorb_table.dtype),
            pltpu.SemaphoreType.DMA((13,)),
        ],
    )
    mine = (mine_0, mine_1)
    far_both = [lax.ppermute(mine[i], ("normal", "surf"), far[i]) for i in range(2)]
    current, *near_mine, select, weight = call(
        near_kernel,
        [
            whole, (2,) + half_side, (2,) + half_side,
            jax.ShapeDtypeStruct((3, 2 * LANES, 4 * LANES), jnp.bfloat16), (3, 4, LANES),
        ],
        lines, kappa, places,
    )
    near_both = [lax.ppermute(value, "surf", near) for value in near_mine]
    base, face, emission, rhs, own_couple = call(
        own_kernel, [whole, whole, whole, whole, (4,) + whole],
        kappa, current, turned, emit, sources, walls, select, weight,
    )
    firsts, others, meets = [], [], []
    for i in range(2):
        firsts.append(call(
            functools.partial(first_kernel, i * half),
            [(2, 4) + half_side, half_whole, half_whole, half_whole, (3, half, cells)],
            kappa, base, face, rhs, mine[i], far_both[i], near_mine[i], near_both[i], select, weight,
            *[done[4] for done in firsts],
            scratch=[found_both],
        ))
        others.append(lax.ppermute(firsts[i][4], "normal", swap))
    for i in range(2):
        couple, pivot, carried, solved, ends = firsts[i]
        meets.append(call(
            meet_kernel, [half_whole, half_side, half_side, (2, half, cells)], ends, others[i], carried, solved
        ))
    far_current = [lax.ppermute(meets[i][1], ("normal", "surf"), far[2 + i]) for i in range(2)]
    near_current = [lax.ppermute(meet[2], "surf", near) for meet in meets]
    (rhs,) = call(own_again_kernel, [whole], meets[0][0], meets[1][0], emission, own_couple, select)
    parts = []
    for i in range(2):
        couple, pivot, carried, solved, ends = firsts[i]
        solved, end = call(
            functools.partial(again_kernel, i * half), [half_whole, (half, cells)],
            rhs, far_current[i], near_current[i], couple, select, pivot, face, *parts[:1],
            scratch=[found_half],
        )
        parts += [end, lax.ppermute(end, "normal", swap), meets[i][3], carried, solved]
    (out,) = call(
        last_kernel, [lines.shape], *parts[5:], *parts[:5],
        out_space=HBM,
        scratch=[pltpu.VMEM(lines.shape, jnp.float32), pltpu.SemaphoreType.DMA((4,))],
    )
    return out.reshape(groups, rows, cells)


def solution(mesh):
    return jax.shard_map(
        body,
        mesh=mesh,
        in_specs=(
            P(None, "normal", "surf"),
            P(),
            P(),
            P(None, "normal", "surf"),
            P(),
            P("surf", None),
            P("surf"),
        ),
        out_specs=P(None, "normal", "surf"),
        check_vma=False,
    )
```

time: 45.1 us -> 43 us (0.953)
  the two profiles are of different devices: /device:TPU:2 before, /device:TPU:128 now
where the time goes in v4:
time: 43 us; the launch traced here: 42.7 us
  starting transfers between devices  19.7 us (46%)
  Pallas kernels  12.1 us (28%)
  waiting for transfers between devices  10.7 us (25%)
    pallas_call x11, Pallas kernels, call(): pl.pallas_call(kernel, out_shape=[jax.ShapeDtypeStruct(out, jnp.float32)...  12.1 us
    ppermute x2, starting transfers between devices, body(): lax.ppermute(meets[i][1], ('normal', 'surf'), far[2 + i])  7.64 us
    ppermute x2, starting transfers between devices, body(): lax.ppermute(mine[i], ('normal', 'surf'), far[i])  7.64 us
    ppermute x2, waiting for transfers between devices, body(): lax.ppermute(meets[i][1], ('normal', 'surf'), far[2 + i])  5.08 us
    ppermute x2, waiting for transfers between devices, body(): lax.ppermute(mine[i], ('normal', 'surf'), far[i])  3.36 us
    ppermute x2, waiting for transfers between devices, body(): lax.ppermute(end, 'normal', swap)  2.24 us
    ppermute x2, starting transfers between devices, body(): others.append(lax.ppermute(firsts[i][4], 'normal', swap))  2.21 us
    ppermute x2, starting transfers between devices, body(): lax.ppermute(end, 'normal', swap)  2.11 us
  transfers between devices with their start and end apart: 12, of which 6 were waited for; matrix products, arithmetic and copies ran while one was open for 0% of the time, Pallas kernels for 19%

profile of v4, /device:TPU:128, one launch (start us, length us, event | category | flops | bytes accessed | tf_op | source)
XLA Modules:
  0.0 42.7 jit_solution(8628835179018047735)
XLA Ops:
  0.0 2.5 %shard_map.73 = (f32[16,128,128]{2,1,0:T(8,128)S(1)}, bf16[16,256,128]{2,1,0:T(8,128)(2,1)S(1)}, f32[2,16,16,128]{3,2,1,0:T(8,128)S(1)}, f32[2,16,16,128]{3,2,1,...) custom-call(bf16[256,16,128]{2,1,0:T(8,128)(2,1)} %pops_hbm.1, ...), custom_call_target="tpu_custom_call" | custom-call | tf_op jit(solution)/shard_map/pallas_call | solution.py:341
  2.5 4.5 %collective-permute-start = (f32[2,16,16,128]{3,2,1,0:T(8,128)S(1)}, f32[2,16,16,128]{3,2,1,0:T(8,128)S(1)}, u32[]{:S(2)}, u32[]{:S(2)}) collective-permute-start(f32[2,16,16,128]{3,2,1,0:T(8,128)S(1)} %get-tuple-element.59.mine_ref), channel_id=1, source_target_pairs={{0,128},{1,2},{2,1},{3,4},{4,3},{5,6},{6,5},{7,8},{8,7},{9,10},{10... | collective-permute-start | bytes 786440 | tf_op jit(solution)/shard_map/ppermute | solution.py:406
  7.1 0.8 %shard_map.74 = (f32[16,128,128]{2,1,0:T(8,128)S(1)}, f32[2,16,16,128]{3,2,1,0:T(8,128)S(1)}, f32[2,16,16,128]{3,2,1,0:T(8,128)S(1)}, bf16[3,256,512]{2,1,0:T(8,128)(2,1)S(1)}, f32[3,4,128]{2,1,0:T(4,128)S(1)}) custom-call(f32[2048,128]{1,0:T(8,128)S(1)} %get-tuple-element.47.lines_ref, f32[16,128,128]{2,1,0:T(8,128)S(1)} %get-tuple-element.46.kappa_ref, ...), custom_call_target="tpu_custom_call" | custom-call | tf_op jit(solution)/shard_map/pallas_call | solution.py:341
  7.8 0.1 collective-permute-start.1
  7.9 3.1 %collective-permute-start.3 = (f32[2,16,16,128]{3,2,1,0:T(8,128)S(1)}, f32[2,16,16,128]{3,2,1,0:T(8,128)S(1)}, u32[]{:S(2)}, u32[]{:S(2)}) collective-permute-start(f32[2,16,16,128]{3,2,1,0:T(8,128)S(1)} %get-tuple-element.65.mine_ref), channel_id=1, source_target_pairs={{0,255},{1,2},{2,1},{3,4},{4,3},{5,6},{6,5},{7,8},{8,7},{9,10},{10... | collective-permute-start | bytes 786440 | tf_op jit(solution)/shard_map/ppermute | solution.py:406
  11.0 0.0 collective-permute-start.4
  11.0 2.7 %shard_map.75 = (f32[16,128,128]{2,1,0:T(8,128)S(1)}, f32[16,128,128]{2,1,0:T(8,128)S(1)}, f32[16,128,128]{2,1,0:T(8,128)S(1)}, f32[16,128,128]{2,1,0:T(8,128)S(1)}, f32[4,16,128,128]{3,2,1,0:T(8,128)S(1)}) custom-call(f32[16,128,128]{2,1,0:T(8,128)S(1)} %get-tuple-element.46.kappa_ref, f32[16,128,128]{2,1,0:T(8,128)S(1)} %get-tuple-element.49.current_ref, ...), custom_call_target="tpu_custom_call" | custom-call | tf_op jit(solution)/shard_map/pallas_call | solution.py:341
  13.7 0.5 %collective-permute-done.far_ref = f32[2,16,16,128]{3,2,1,0:T(8,128)S(1)} collective-permute-done((f32[2,16,16,128]{3,2,1,0:T(8,128)S(1)}, f32[2,16,16,128]{3,2,1,0:T(8,128)S(1)}, u32[]{:S(2)}, u32[]{:S(2)}) %collective-permute-start) | collective-permute-done | bytes 262176 | tf_op jit(solution)/shard_map/ppermute | solution.py:406
  14.2 0.0 collective-permute-done.1.near_ref
  14.2 1.0 %shard_map.76 = (f32[2,4,16,16,128]{4,3,2,1,0:T(8,128)S(1)}, f32[16,64,128]{2,1,0:T(8,128)S(1)}, f32[16,64,128]{2,1,0:T(8,128)S(1)}, f32[16,64,128]{2,1,0:T(8,128)S(1)}, f32[3,64,128]{2,1,0:T(8,128)S(1)}) custom-call(f32[16,128,128]{2,1,0:T(8,128)S(1)} %get-tuple-element.46.kappa_ref, f32[16,128,128]{2,1,0:T(8,128)S(1)} %get-tuple-element.56.base_ref, ...), custom_call_target="tpu_custom_call" | custom-call | tf_op jit(solution)/shard_map/pallas_call | solution.py:341
  15.2 1.6 %collective-permute-start.2 = (f32[3,64,128]{2,1,0:T(8,128)S(1)}, f32[3,64,128]{2,1,0:T(8,128)S(1)}, u32[]{:S(2)}, u32[]{:S(2)}) collective-permute-start(f32[3,64,128]{2,1,0:T(8,128)S(1)} %get-tuple-element.61.ends_ref.refs_0_), channel_id=1, source_target_pairs={{0,128},{128,0},{1,129},{129,1},{2,130},{130,2},{3,131},{131,3},{4... | collective-permute-start | bytes 294920 | tf_op jit(solution)/shard_map/ppermute | solution.py:429
  16.8 2.9 %collective-permute-done.3.far_ref = f32[2,16,16,128]{3,2,1,0:T(8,128)S(1)} collective-permute-done((f32[2,16,16,128]{3,2,1,0:T(8,128)S(1)}, f32[2,16,16,128]{3,2,1,0:T(8,128)S(1)}, u32[]{:S(2)}, u32[]{:S(2)}) %collective-permute-start.3) | collective-permute-done | bytes 262176 | tf_op jit(solution)/shard_map/ppermute | solution.py:406
  19.7 0.0 collective-permute-done.4.near_ref
  19.7 1.0 %shard_map.78 = (f32[2,4,16,16,128]{4,3,2,1,0:T(8,128)S(1)}, f32[16,64,128]{2,1,0:T(8,128)S(1)}, f32[16,64,128]{2,1,0:T(8,128)S(1)}, f32[16,64,128]{2,1,0:T(8,128)S(1)}, f32[3,64,128]{2,1,0:T(8,128)S(1)}) custom-call(f32[16,128,128]{2,1,0:T(8,128)S(1)} %get-tuple-element.46.kappa_ref, f32[16,128,128]{2,1,0:T(8,128)S(1)} %get-tuple-element.56.base_ref, ...), custom_call_target="tpu_custom_call" | custom-call | tf_op jit(solution)/shard_map/pallas_call | solution.py:341
  20.6 0.6 %collective-permute-start.5 = (f32[3,64,128]{2,1,0:T(8,128)S(1)}, f32[3,64,128]{2,1,0:T(8,128)S(1)}, u32[]{:S(2)}, u32[]{:S(2)}) collective-permute-start(f32[3,64,128]{2,1,0:T(8,128)S(1)} %get-tuple-element.67.ends_ref), channel_id=1, source_target_pairs={{0,128},{128,0},{1,129},{129,1},{2,130},{130,2},{3,131},{131,3},{4... | collective-permute-start | bytes 294920 | tf_op jit(solution)/shard_map/ppermute | solution.py:429
  21.3 0.0 collective-permute-done.2.other_ref
  21.3 0.4 shard_map.77
  21.6 4.3 %collective-permute-start.8 = (f32[16,16,128]{2,1,0:T(8,128)S(1)}, f32[16,16,128]{2,1,0:T(8,128)S(1)}, u32[]{:S(2)}, u32[]{:S(2)}) collective-permute-start(f32[16,16,128]{2,1,0:T(8,128)S(1)} %get-tuple-element.77), channel_id=1, source_target_pairs={{0,128},{1,2},{2,1},{3,4},{4,3},{5,6},{6,5},{7,8},{8,7},{9,10},{10... | collective-permute-start | bytes 393224 | tf_op jit(solution)/shard_map/ppermute | solution.py:435
  26.0 0.0 collective-permute-start.9
  26.0 0.0 collective-permute-done.5.other_ref
  26.0 0.4 shard_map.79
  26.3 3.3 %collective-permute-start.6 = (f32[16,16,128]{2,1,0:T(8,128)S(1)}, f32[16,16,128]{2,1,0:T(8,128)S(1)}, u32[]{:S(2)}, u32[]{:S(2)}) collective-permute-start(f32[16,16,128]{2,1,0:T(8,128)S(1)} %get-tuple-element.73), channel_id=1, source_target_pairs={{0,128},{1,2},{2,1},{3,4},{4,3},{5,6},{6,5},{7,8},{8,7},{9,10},{10... | collective-permute-start | bytes 393224 | tf_op jit(solution)/shard_map/ppermute | solution.py:435
  29.7 0.0 collective-permute-start.7
  29.7 1.2 %shard_map.80.rhs_ref = f32[16,128,128]{2,1,0:T(8,128)S(1)} custom-call(f32[16,64,128]{2,1,0:T(8,128)S(1)} %get-tuple-element.64.current_0, f32[16,64,128]{2,1,0:T(8,128)S(1)} %get-tuple-element.70.current_1, f32[16,128,128]{2,1,0:T(8,128)S(1)} %get-tuple-element.71.emission_ref, f32[4,16,128,128]{3,2,1,0:T(8,128)S(1)} %get-tuple-element.72.couple_ref, ...), custom_call_target="tpu_custom_call" | custom-call | tf_op jit(solution)/shard_map/pallas_call | solution.py:341
  30.9 0.9 %collective-permute-done.8.far_ref = f32[16,16,128]{2,1,0:T(8,128)S(1)} collective-permute-done((f32[16,16,128]{2,1,0:T(8,128)S(1)}, f32[16,16,128]{2,1,0:T(8,128)S(1)}, u32[]{:S(2)}, u32[]{:S(2)}) %collective-permute-start.8) | collective-permute-done | bytes 131104 | tf_op jit(solution)/shard_map/ppermute | solution.py:435
  31.8 0.0 collective-permute-done.9.near_ref
  31.8 0.5 %shard_map.81 = (f32[16,64,128]{2,1,0:T(8,128)S(1)}, f32[64,128]{1,0:T(8,128)S(1)}) custom-call(f32[16,128,128]{2,1,0:T(8,128)S(1)} %shard_map.80.rhs_ref, f32[16,16,128]{2,1,0:T(8,128)S(1)} %collective-permute-done.8.far_ref, f32[16,16,128]{2,1,0:T(8,128)S(1)} %collective-permute-done.9.near_ref, f32[2,4,16,16,128]{4,3,2,1,0:T(8,128)S(1)} %get-tuple-element.79.couple_ref, ...), custom_call_target="tpu_custom_call" | custom-call | tf_op jit(solution)/shard_map/pallas_call | solution.py:341
  32.4 4.1 %collective-permute-done.6.far_ref = f32[16,16,128]{2,1,0:T(8,128)S(1)} collective-permute-done((f32[16,16,128]{2,1,0:T(8,128)S(1)}, f32[16,16,128]{2,1,0:T(8,128)S(1)}, u32[]{:S(2)}, u32[]{:S(2)}) %collective-permute-start.6) | collective-permute-done | bytes 131104 | tf_op jit(solution)/shard_map/ppermute | solution.py:435
  36.5 0.0 collective-permute-done.7.near_ref
  36.5 0.5 %shard_map.82 = (f32[16,64,128]{2,1,0:T(8,128)S(1)}, f32[64,128]{1,0:T(8,128)S(1)}) custom-call(f32[16,128,128]{2,1,0:T(8,128)S(1)} %shard_map.80.rhs_ref, f32[16,16,128]{2,1,0:T(8,128)S(1)} %collective-permute-done.6.far_ref, f32[16,16,128]{2,1,0:T(8,128)S(1)} %collective-permute-done.7.near_ref, f32[2,4,16,16,128]{4,3,2,1,0:T(8,128)S(1)} %get-tuple-element.75.couple_ref, ...), custom_call_target="tpu_custom_call" | custom-call | tf_op jit(solution)/shard_map/pallas_call | solution.py:341
  37.1 0.1 collective-permute-start.10
  37.2 2.0 %collective-permute-start.11 = (f32[64,128]{1,0:T(8,128)S(1)}, f32[64,128]{1,0:T(8,128)S(1)}, u32[]{:S(2)}, u32[]{:S(2)}) collective-permute-start(f32[64,128]{1,0:T(8,128)S(1)} %get-tuple-element.81.refs_0_.refs_5_), channel_id=1, source_target_pairs={{0,128},{128,0},{1,129},{129,1},{2,130},{130,2},{3,131},{131,3},{4... | collective-permute-start | bytes 98312 | tf_op jit(solution)/shard_map/ppermute | solution.py:446
  39.2 1.9 %collective-permute-done.10.refs_1_ = f32[64,128]{1,0:T(8,128)S(1)} collective-permute-done((f32[64,128]{1,0:T(8,128)S(1)}, f32[64,128]{1,0:T(8,128)S(1)}, u32[]{:S(2)}, u32[]{:S(2)}) %collective-permute-start.10) | collective-permute-done | bytes 32800 | tf_op jit(solution)/shard_map/ppermute | solution.py:446
  41.1 0.4 collective-permute-done.11.refs_6_
  41.4 1.1 %shard_map.83 = f32[2048,128]{1,0:T(8,128)} custom-call(f32[64,128]{1,0:T(8,128)S(1)} %get-tuple-element.82.refs_0_, f32[64,128]{1,0:T(8,128)S(1)} %collective-permute-done.10.refs_1_, f32[2,64,128]{2,1,0:T(8,128)S(1)} %get-tuple-element.83.refs_2_, f32[16,64,128]{2,1,0:T(8,128)S(1)} %get-tuple-element.68.carried_ref.refs_3_, ...), custom_call_target="tpu_custom_call" | custom-call | tf_op jit(solution)/shard_map/pallas_call | solution.py:341
Async XLA Ops:
  2.5 11.7 %collective-permute-start = (f32[2,16,16,128]{3,2,1,0:T(8,128)S(1)}, f32[2,16,16,128]{3,2,1,0:T(8,128)S(1)}, u32[]{:S(2)}, u32[]{:S(2)}) collective-permute-start(f32[2,16,16,128]{3,2,1,0:T(8,128)S(1)} %get-tuple-element.59.mine_ref), channel_id=1, source_target_pairs={{0,128},{1,2},{2,1},{3,4},{4,3},{5,6},{6,5},{7,8},{8,7},{9,10},{10... | collective-permute-start | bytes 786440 | tf_op jit(solution)/shard_map/ppermute | solution.py:406
  7.8 6.4 %collective-permute-start.1 = (f32[2,16,16,128]{3,2,1,0:T(8,128)S(1)}, f32[2,16,16,128]{3,2,1,0:T(8,128)S(1)}, u32[]{:S(2)}, u32[]{:S(2)}) collective-permute-start(f32[2,16,16,128]{3,2,1,0:T(8,128)S(1)} %get-tuple-element.60.near_mine_ref), channel_id=1, source_target_pairs={{0,1},{1,0},{2,3},{3,2},{4,5},{5,4},{6,7},{7,6},{8,9},{9,8},{10,11... | collective-permute-start | bytes 786440 | tf_op jit(solution)/shard_map/ppermute | solution.py:415
  7.9 11.7 %collective-permute-start.3 = (f32[2,16,16,128]{3,2,1,0:T(8,128)S(1)}, f32[2,16,16,128]{3,2,1,0:T(8,128)S(1)}, u32[]{:S(2)}, u32[]{:S(2)}) collective-permute-start(f32[2,16,16,128]{3,2,1,0:T(8,128)S(1)} %get-tuple-element.65.mine_ref), channel_id=1, source_target_pairs={{0,255},{1,2},{2,1},{3,4},{4,3},{5,6},{6,5},{7,8},{8,7},{9,10},{10... | collective-permute-start | bytes 786440 | tf_op jit(solution)/shard_map/ppermute | solution.py:406
  11.0 8.6 %collective-permute-start.4 = (f32[2,16,16,128]{3,2,1,0:T(8,128)S(1)}, f32[2,16,16,128]{3,2,1,0:T(8,128)S(1)}, u32[]{:S(2)}, u32[]{:S(2)}) collective-permute-start(f32[2,16,16,128]{3,2,1,0:T(8,128)S(1)} %get-tuple-element.66.near_mine_ref), channel_id=1, source_target_pairs={{0,1},{1,0},{2,3},{3,2},{4,5},{5,4},{6,7},{7,6},{8,9},{9,8},{10,11... | collective-permute-start | bytes 786440 | tf_op jit(solution)/shard_map/ppermute | solution.py:415
  15.2 6.1 %collective-permute-start.2 = (f32[3,64,128]{2,1,0:T(8,128)S(1)}, f32[3,64,128]{2,1,0:T(8,128)S(1)}, u32[]{:S(2)}, u32[]{:S(2)}) collective-permute-start(f32[3,64,128]{2,1,0:T(8,128)S(1)} %get-tuple-element.61.ends_ref.refs_0_), channel_id=1, source_target_pairs={{0,128},{128,0},{1,129},{129,1},{2,130},{130,2},{3,131},{131,3},{4... | collective-permute-start | bytes 294920 | tf_op jit(solution)/shard_map/ppermute | solution.py:429
  20.6 5.3 %collective-permute-start.5 = (f32[3,64,128]{2,1,0:T(8,128)S(1)}, f32[3,64,128]{2,1,0:T(8,128)S(1)}, u32[]{:S(2)}, u32[]{:S(2)}) collective-permute-start(f32[3,64,128]{2,1,0:T(8,128)S(1)} %get-tuple-element.67.ends_ref), channel_id=1, source_target_pairs={{0,128},{128,0},{1,129},{129,1},{2,130},{130,2},{3,131},{131,3},{4... | collective-permute-start | bytes 294920 | tf_op jit(solution)/shard_map/ppermute | solution.py:429
  21.6 10.2 %collective-permute-start.8 = (f32[16,16,128]{2,1,0:T(8,128)S(1)}, f32[16,16,128]{2,1,0:T(8,128)S(1)}, u32[]{:S(2)}, u32[]{:S(2)}) collective-permute-start(f32[16,16,128]{2,1,0:T(8,128)S(1)} %get-tuple-element.77), channel_id=1, source_target_pairs={{0,128},{1,2},{2,1},{3,4},{4,3},{5,6},{6,5},{7,8},{8,7},{9,10},{10... | collective-permute-start | bytes 393224 | tf_op jit(solution)/shard_map/ppermute | solution.py:435
  26.0 5.9 %collective-permute-start.9 = (f32[16,16,128]{2,1,0:T(8,128)S(1)}, f32[16,16,128]{2,1,0:T(8,128)S(1)}, u32[]{:S(2)}, u32[]{:S(2)}) collective-permute-start(f32[16,16,128]{2,1,0:T(8,128)S(1)} %get-tuple-element.78), channel_id=1, source_target_pairs={{0,1},{1,0},{2,3},{3,2},{4,5},{5,4},{6,7},{7,6},{8,9},{9,8},{10,11... | collective-permute-start | bytes 393224 | tf_op jit(solution)/shard_map/ppermute | solution.py:436
  26.3 10.2 %collective-permute-start.6 = (f32[16,16,128]{2,1,0:T(8,128)S(1)}, f32[16,16,128]{2,1,0:T(8,128)S(1)}, u32[]{:S(2)}, u32[]{:S(2)}) collective-permute-start(f32[16,16,128]{2,1,0:T(8,128)S(1)} %get-tuple-element.73), channel_id=1, source_target_pairs={{0,128},{1,2},{2,1},{3,4},{4,3},{5,6},{6,5},{7,8},{8,7},{9,10},{10... | collective-permute-start | bytes 393224 | tf_op jit(solution)/shard_map/ppermute | solution.py:435
  29.7 6.9 %collective-permute-start.7 = (f32[16,16,128]{2,1,0:T(8,128)S(1)}, f32[16,16,128]{2,1,0:T(8,128)S(1)}, u32[]{:S(2)}, u32[]{:S(2)}) collective-permute-start(f32[16,16,128]{2,1,0:T(8,128)S(1)} %get-tuple-element.74), channel_id=1, source_target_pairs={{0,1},{1,0},{2,3},{3,2},{4,5},{5,4},{6,7},{7,6},{8,9},{9,8},{10,11... | collective-permute-start | bytes 393224 | tf_op jit(solution)/shard_map/ppermute | solution.py:436
  37.1 4.0 %collective-permute-start.10 = (f32[64,128]{1,0:T(8,128)S(1)}, f32[64,128]{1,0:T(8,128)S(1)}, u32[]{:S(2)}, u32[]{:S(2)}) collective-permute-start(f32[64,128]{1,0:T(8,128)S(1)} %get-tuple-element.82.refs_0_), channel_id=1, source_target_pairs={{0,128},{128,0},{1,129},{129,1},{2,130},{130,2},{3,131},{131,3},{4... | collective-permute-start | bytes 98312 | tf_op jit(solution)/shard_map/ppermute | solution.py:446
  37.2 4.3 %collective-permute-start.11 = (f32[64,128]{1,0:T(8,128)S(1)}, f32[64,128]{1,0:T(8,128)S(1)}, u32[]{:S(2)}, u32[]{:S(2)}) collective-permute-start(f32[64,128]{1,0:T(8,128)S(1)} %get-tuple-element.81.refs_0_.refs_5_), channel_id=1, source_target_pairs={{0,128},{128,0},{1,129},{129,1},{2,130},{130,2},{3,131},{131,3},{4... | collective-permute-start | bytes 98312 | tf_op jit(solution)/shard_map/ppermute | solution.py:446

commit v5 on v4

--- a/solution.py
+++ b/solution.py
@@ -100,7 +100,7 @@
     )
 
 
-def kappa_kernel(pops_hbm, absorb_hbm, emit_hbm, lines_hbm, places_hbm, walls_hbm, sources_hbm, kappa_ref, turned_ref, far_0, far_1, emit_ref, lines_ref, places_ref, walls_ref, sources_ref, pops_ref, table_ref, sems):
+def kappa_kernel(pops_hbm, absorb_hbm, emit_hbm, lines_hbm, places_hbm, walls_hbm, sources_hbm, kappa_ref, turned_ref, far_0, emit_ref, lines_ref, places_ref, walls_ref, sources_ref, pops_ref, table_ref, sems):
     rows, groups, cells = kappa_ref.shape
     levels = pops_ref.shape[0]
     pieces = 4
@@ -134,15 +134,13 @@
     half = groups // 2
     for r in range(rows):
         far_0[0, r] = pack(kappa_ref[r, :half], odd)
-        far_1[0, r] = pack(kappa_ref[r, half:], odd)
     for copy in copies[pieces + 1 :]:
         copy.wait()
     for r in range(rows):
         far_0[1, r] = pack(lines_ref[pl.ds(row_of(r, rows), half, stride=rows), :], odd)
-        far_1[1, r] = pack(lines_ref[pl.ds(half * rows + row_of(r, rows), half, stride=rows), :], odd)
-
-
-def near_kernel(lines_ref, kappa_ref, neighbours_ref, current_ref, near_0, near_1, select_ref, weight_ref):
+
+
+def near_kernel(lines_ref, kappa_ref, neighbours_ref, current_ref, far_1, near_0, near_1, select_ref, weight_ref):
     rows, groups, cells = current_ref.shape
     half = groups // 2
     high = odd_surf()
@@ -151,6 +149,8 @@
         current = lines_ref[pl.ds(row_of(r, rows), groups, stride=rows), :]
         current_ref[r] = current
         kappa = kappa_ref[r]
+        far_1[0, r] = pack(kappa[half:], high)
+        far_1[1, r] = pack(current[half:], high)
         near_0[0, r] = pack(kappa[:half], low_near)
         near_0[1, r] = pack(current[:half], low_near)
         near_1[0, r] = pack(kappa[half:], low_near)
@@ -289,6 +289,9 @@
 
 def again_kernel(start, rhs_ref, far_ref, near_ref, couple_ref, select_ref, pivot_ref, face_ref, *refs):
     solved_ref, end_ref, found_ref = refs[-3:]
+    if len(refs) > 3:
+        end_ref[0] = refs[0][...]
+        end_ref = end_ref.at[1]
     rows, groups, cells = pivot_ref.shape
     size = groups // 4
     here = pl.ds(start, groups)
@@ -312,10 +315,12 @@
 
 
 def last_kernel(*refs):
-    halves, (out_hbm, lines_ref, sems) = (refs[5:10], refs[:5]), refs[10:]
+    ends_ref, others_ref, *halves, out_hbm, lines_ref, sems = refs
     copies = []
     start = 0
-    for end_ref, other_ref, mix_ref, carried_ref, solved_ref in halves:
+    for i in range(2):
+        mix_ref, carried_ref, solved_ref = halves[3 * i : 3 * i + 3]
+        end_ref, other_ref = ends_ref.at[i], others_ref.at[i]
         rows, groups, cells = carried_ref.shape
         step = groups // 2
         for part in range(2):
@@ -388,10 +393,10 @@
     walls = wall_type.reshape(1, cells)
     sources = wall_source.reshape(1, groups)
 
-    kappa, turned, mine_0, mine_1, emit, lines, places, walls, sources = call(
+    kappa, turned, mine_0, emit, lines, places, walls, sources = call(
         kappa_kernel,
         [
-            whole, jax.ShapeDtypeStruct((rows, levels, cells), populations.dtype), (2,) + half_side, (2,) + half_side,
+            whole, jax.ShapeDtypeStruct((rows, levels, cells), populations.dtype), (2,) + half_side,
             like(emit_table), like(lines), like(places), like(walls), like(sources),
         ],
         *in_hbm(populations, absorb_table, emit_table, lines, places, walls, sources),
@@ -402,16 +407,17 @@
             pltpu.SemaphoreType.DMA((13,)),
         ],
     )
-    mine = (mine_0, mine_1)
-    far_both = [lax.ppermute(mine[i], ("normal", "surf"), far[i]) for i in range(2)]
-    current, *near_mine, select, weight = call(
+    far_0 = lax.ppermute(mine_0, ("normal", "surf"), far[0])
+    current, mine_1, *near_mine, select, weight = call(
         near_kernel,
         [
-            whole, (2,) + half_side, (2,) + half_side,
+            whole, (2,) + half_side, (2,) + half_side, (2,) + half_side,
             jax.ShapeDtypeStruct((3, 2 * LANES, 4 * LANES), jnp.bfloat16), (3, 4, LANES),
         ],
         lines, kappa, places,
     )
+    mine = (mine_0, mine_1)
+    far_both = (far_0, lax.ppermute(mine_1, ("normal", "surf"), far[1]))
     near_both = [lax.ppermute(value, "surf", near) for value in near_mine]
     base, face, emission, rhs, own_couple = call(
         own_kernel, [whole, whole, whole, whole, (4,) + whole],
@@ -439,13 +445,14 @@
     for i in range(2):
         couple, pivot, carried, solved, ends = firsts[i]
         solved, end = call(
-            functools.partial(again_kernel, i * half), [half_whole, (half, cells)],
+            functools.partial(again_kernel, i * half), [half_whole, (2, half, cells) if i else (half, cells)],
             rhs, far_current[i], near_current[i], couple, select, pivot, face, *parts[:1],
             scratch=[found_half],
         )
-        parts += [end, lax.ppermute(end, "normal", swap), meets[i][3], carried, solved]
+        parts += [end, meets[i][3], carried, solved]
+    other_ends = lax.ppermute(end, "normal", swap)
     (out,) = call(
-        last_kernel, [lines.shape], *parts[5:], *parts[:5],
+        last_kernel, [lines.shape], end, other_ends, *parts[1:4], *parts[5:],
         out_space=HBM,
         scratch=[pltpu.VMEM(lines.shape, jnp.float32), pltpu.SemaphoreType.DMA((4,))],
     )

time: 43 us -> 42.6 us (level)
  starting transfers between devices: 19.7 us -> 17.7 us
  waiting for transfers between devices: 10.7 us -> 12.7 us
    ppermute x4 -> x3, starting transfers between devices: 9.75 us -> 7.73 us  [the longest x1 4.54 us: body(): far_0 = lax.ppermute(mine_0, ('normal', 'surf'), far[0])]
    ppermute x4 -> x3, waiting for transfers between devices: 5.6 us -> 7.6 us  [the longest x1 4.25 us: body(): other_ends = lax.ppermute(end, 'normal', swap)]
  transfers between devices with their start and end apart: 12 -> 11, of which waited for: 6 -> 5; matrix products, arithmetic and copies ran while one was open for 0% -> 0% of each run, Pallas kernels for 19% -> 19%
where the time goes in v5:
time: 42.6 us; the launch traced here: 42.5 us
  starting transfers between devices  17.7 us (42%)
  waiting for transfers between devices  12.7 us (30%)
  Pallas kernels  12 us (28%)
    pallas_call x11, Pallas kernels, call(): pl.pallas_call(kernel, out_shape=[jax.ShapeDtypeStruct(out, jnp.float32)...  12 us
    ppermute x2, starting transfers between devices, body(): lax.ppermute(meets[i][1], ('normal', 'surf'), far[2 + i])  7.64 us
    ppermute x2, waiting for transfers between devices, body(): lax.ppermute(meets[i][1], ('normal', 'surf'), far[2 + i])  5.08 us
    ppermute x1, starting transfers between devices, body(): far_0 = lax.ppermute(mine_0, ('normal', 'surf'), far[0])  4.54 us
    ppermute x1, waiting for transfers between devices, body(): other_ends = lax.ppermute(end, 'normal', swap)  4.25 us
    ppermute x1, starting transfers between devices, body(): far_both = (far_0, lax.ppermute(mine_1, ('normal', 'surf'), far[1]))  3.1 us
    ppermute x1, waiting for transfers between devices, body(): far_both = (far_0, lax.ppermute(mine_1, ('normal', 'surf'), far[1]))  3.1 us
    ppermute x2, starting transfers between devices, body(): others.append(lax.ppermute(firsts[i][4], 'normal', swap))  2.22 us
  transfers between devices with their start and end apart: 11, of which 5 were waited for; matrix products, arithmetic and copies ran while one was open for 0% of the time, Pallas kernels for 19%

profile of v5, /device:TPU:128, one launch (start us, length us, event | category | flops | bytes accessed | tf_op | source)
XLA Modules:
  0.0 42.5 jit_solution(8268828337274262757)
XLA Ops:
  0.0 2.2 %shard_map.73 = (f32[16,128,128]{2,1,0:T(8,128)S(1)}, bf16[16,256,128]{2,1,0:T(8,128)(2,1)S(1)}, f32[2,16,16,128]{3,2,1,0:T(8,128)S(1)}, bf16[128,256]{1,0:T(8,1...) custom-call(bf16[256,16,128]{2,1,0:T(8,128)(2,1)} %pops_hbm.1, ...), custom_call_target="tpu_custom_call" | custom-call | tf_op jit(solution)/shard_map/pallas_call | solution.py:346
  2.2 4.5 %collective-permute-start = (f32[2,16,16,128]{3,2,1,0:T(8,128)S(1)}, f32[2,16,16,128]{3,2,1,0:T(8,128)S(1)}, u32[]{:S(2)}, u32[]{:S(2)}) collective-permute-start(f32[2,16,16,128]{3,2,1,0:T(8,128)S(1)} %get-tuple-element.59.mine_ref), channel_id=1, source_target_pairs={{0,128},{1,2},{2,1},{3,4},{4,3},{5,6},{6,5},{7,8},{8,7},{9,10},{10... | collective-permute-start | bytes 786440 | tf_op jit(solution)/shard_map/ppermute | solution.py:410
  6.8 1.0 %shard_map.74 = (f32[16,128,128]{2,1,0:T(8,128)S(1)}, f32[2,16,16,128]{3,2,1,0:T(8,128)S(1)}, f32[2,16,16,128]{3,2,1,0:T(8,128)S(1)}, f32[2,16,16,128]{3,2,1,0:T...) custom-call(f32[2048,128]{1,0:T(8,128)S(1)} %get-tuple-element.47.lines_ref, ...), custom_call_target="tpu_custom_call" | custom-call | tf_op jit(solution)/shard_map/pallas_call | solution.py:346
  7.8 0.1 collective-permute-start.1
  7.9 3.1 %collective-permute-start.3 = (f32[2,16,16,128]{3,2,1,0:T(8,128)S(1)}, f32[2,16,16,128]{3,2,1,0:T(8,128)S(1)}, u32[]{:S(2)}, u32[]{:S(2)}) collective-permute-start(f32[2,16,16,128]{3,2,1,0:T(8,128)S(1)} %get-tuple-element.65.mine_ref), channel_id=1, source_target_pairs={{0,255},{1,2},{2,1},{3,4},{4,3},{5,6},{6,5},{7,8},{8,7},{9,10},{10... | collective-permute-start | bytes 786440 | tf_op jit(solution)/shard_map/ppermute | solution.py:420
  11.0 0.0 collective-permute-start.4
  11.0 2.7 %shard_map.75 = (f32[16,128,128]{2,1,0:T(8,128)S(1)}, f32[16,128,128]{2,1,0:T(8,128)S(1)}, f32[16,128,128]{2,1,0:T(8,128)S(1)}, f32[16,128,128]{2,1,0:T(8,128)S(1)}, f32[4,16,128,128]{3,2,1,0:T(8,128)S(1)}) custom-call(f32[16,128,128]{2,1,0:T(8,128)S(1)} %get-tuple-element.46.kappa_ref, f32[16,128,128]{2,1,0:T(8,128)S(1)} %get-tuple-element.49.current_ref, ...), custom_call_target="tpu_custom_call" | custom-call | tf_op jit(solution)/shard_map/pallas_call | solution.py:346
  13.7 0.2 collective-permute-done.far_ref
  13.9 0.0 collective-permute-done.1.near_ref
  13.9 1.0 %shard_map.76 = (f32[2,4,16,16,128]{4,3,2,1,0:T(8,128)S(1)}, f32[16,64,128]{2,1,0:T(8,128)S(1)}, f32[16,64,128]{2,1,0:T(8,128)S(1)}, f32[16,64,128]{2,1,0:T(8,128)S(1)}, f32[3,64,128]{2,1,0:T(8,128)S(1)}) custom-call(f32[16,128,128]{2,1,0:T(8,128)S(1)} %get-tuple-element.46.kappa_ref, f32[16,128,128]{2,1,0:T(8,128)S(1)} %get-tuple-element.56.base_ref, ...), custom_call_target="tpu_custom_call" | custom-call | tf_op jit(solution)/shard_map/pallas_call | solution.py:346
  14.9 1.6 %collective-permute-start.2 = (f32[3,64,128]{2,1,0:T(8,128)S(1)}, f32[3,64,128]{2,1,0:T(8,128)S(1)}, u32[]{:S(2)}, u32[]{:S(2)}) collective-permute-start(f32[3,64,128]{2,1,0:T(8,128)S(1)} %get-tuple-element.61.ends_ref.refs_0_), channel_id=1, source_target_pairs={{0,128},{128,0},{1,129},{129,1},{2,130},{130,2},{3,131},{131,3},{4... | collective-permute-start | bytes 294920 | tf_op jit(solution)/shard_map/ppermute | solution.py:435
  16.5 3.1 %collective-permute-done.3.far_ref = f32[2,16,16,128]{3,2,1,0:T(8,128)S(1)} collective-permute-done((f32[2,16,16,128]{3,2,1,0:T(8,128)S(1)}, f32[2,16,16,128]{3,2,1,0:T(8,128)S(1)}, u32[]{:S(2)}, u32[]{:S(2)}) %collective-permute-start.3) | collective-permute-done | bytes 262176 | tf_op jit(solution)/shard_map/ppermute | solution.py:420
  19.6 0.0 collective-permute-done.4.near_ref
  19.6 1.0 %shard_map.78 = (f32[2,4,16,16,128]{4,3,2,1,0:T(8,128)S(1)}, f32[16,64,128]{2,1,0:T(8,128)S(1)}, f32[16,64,128]{2,1,0:T(8,128)S(1)}, f32[16,64,128]{2,1,0:T(8,128)S(1)}, f32[3,64,128]{2,1,0:T(8,128)S(1)}) custom-call(f32[16,128,128]{2,1,0:T(8,128)S(1)} %get-tuple-element.46.kappa_ref, f32[16,128,128]{2,1,0:T(8,128)S(1)} %get-tuple-element.56.base_ref, ...), custom_call_target="tpu_custom_call" | custom-call | tf_op jit(solution)/shard_map/pallas_call | solution.py:346
  20.6 0.6 %collective-permute-start.5 = (f32[3,64,128]{2,1,0:T(8,128)S(1)}, f32[3,64,128]{2,1,0:T(8,128)S(1)}, u32[]{:S(2)}, u32[]{:S(2)}) collective-permute-start(f32[3,64,128]{2,1,0:T(8,128)S(1)} %get-tuple-element.67.ends_ref), channel_id=1, source_target_pairs={{0,128},{128,0},{1,129},{129,1},{2,130},{130,2},{3,131},{131,3},{4... | collective-permute-start | bytes 294920 | tf_op jit(solution)/shard_map/ppermute | solution.py:435
  21.2 0.0 collective-permute-done.2.other_ref
  21.2 0.4 shard_map.77
  21.6 4.3 %collective-permute-start.8 = (f32[16,16,128]{2,1,0:T(8,128)S(1)}, f32[16,16,128]{2,1,0:T(8,128)S(1)}, u32[]{:S(2)}, u32[]{:S(2)}) collective-permute-start(f32[16,16,128]{2,1,0:T(8,128)S(1)} %get-tuple-element.77), channel_id=1, source_target_pairs={{0,128},{1,2},{2,1},{3,4},{4,3},{5,6},{6,5},{7,8},{8,7},{9,10},{10... | collective-permute-start | bytes 393224 | tf_op jit(solution)/shard_map/ppermute | solution.py:441
  25.9 0.0 collective-permute-start.9
  25.9 0.0 collective-permute-done.5.other_ref
  25.9 0.4 shard_map.79
  26.3 3.3 %collective-permute-start.6 = (f32[16,16,128]{2,1,0:T(8,128)S(1)}, f32[16,16,128]{2,1,0:T(8,128)S(1)}, u32[]{:S(2)}, u32[]{:S(2)}) collective-permute-start(f32[16,16,128]{2,1,0:T(8,128)S(1)} %get-tuple-element.73), channel_id=1, source_target_pairs={{0,128},{1,2},{2,1},{3,4},{4,3},{5,6},{6,5},{7,8},{8,7},{9,10},{10... | collective-permute-start | bytes 393224 | tf_op jit(solution)/shard_map/ppermute | solution.py:441
  29.6 0.0 collective-permute-start.7
  29.6 1.2 %shard_map.80.rhs_ref = f32[16,128,128]{2,1,0:T(8,128)S(1)} custom-call(f32[16,64,128]{2,1,0:T(8,128)S(1)} %get-tuple-element.64.current_0, f32[16,64,128]{2,1,0:T(8,128)S(1)} %get-tuple-element.70.current_1, f32[16,128,128]{2,1,0:T(8,128)S(1)} %get-tuple-element.71.emission_ref, f32[4,16,128,128]{3,2,1,0:T(8,128)S(1)} %get-tuple-element.72.couple_ref, ...), custom_call_target="tpu_custom_call" | custom-call | tf_op jit(solution)/shard_map/pallas_call | solution.py:346
  30.9 0.9 %collective-permute-done.8.far_ref = f32[16,16,128]{2,1,0:T(8,128)S(1)} collective-permute-done((f32[16,16,128]{2,1,0:T(8,128)S(1)}, f32[16,16,128]{2,1,0:T(8,128)S(1)}, u32[]{:S(2)}, u32[]{:S(2)}) %collective-permute-start.8) | collective-permute-done | bytes 131104 | tf_op jit(solution)/shard_map/ppermute | solution.py:441
  31.8 0.0 collective-permute-done.9.near_ref
  31.8 0.5 %shard_map.81 = (f32[16,64,128]{2,1,0:T(8,128)S(1)}, f32[64,128]{1,0:T(8,128)S(1)}) custom-call(f32[16,128,128]{2,1,0:T(8,128)S(1)} %shard_map.80.rhs_ref, f32[16,16,128]{2,1,0:T(8,128)S(1)} %collective-permute-done.8.far_ref, f32[16,16,128]{2,1,0:T(8,128)S(1)} %collective-permute-done.9.near_ref, f32[2,4,16,16,128]{4,3,2,1,0:T(8,128)S(1)} %get-tuple-element.79.couple_ref, ...), custom_call_target="tpu_custom_call" | custom-call | tf_op jit(solution)/shard_map/pallas_call | solution.py:346
  32.3 4.1 %collective-permute-done.6.far_ref = f32[16,16,128]{2,1,0:T(8,128)S(1)} collective-permute-done((f32[16,16,128]{2,1,0:T(8,128)S(1)}, f32[16,16,128]{2,1,0:T(8,128)S(1)}, u32[]{:S(2)}, u32[]{:S(2)}) %collective-permute-start.6) | collective-permute-done | bytes 131104 | tf_op jit(solution)/shard_map/ppermute | solution.py:441
  36.5 0.0 collective-permute-done.7.near_ref
  36.5 0.5 %shard_map.82 = (f32[16,64,128]{2,1,0:T(8,128)S(1)}, f32[2,64,128]{2,1,0:T(8,128)S(1)}) custom-call(f32[16,128,128]{2,1,0:T(8,128)S(1)} %shard_map.80.rhs_ref, f32[16,16,128]{2,1,0:T(8,128)S(1)} %collective-permute-done.6.far_ref, f32[16,16,128]{2,1,0:T(8,128)S(1)} %collective-permute-done.7.near_ref, ...), custom_call_target="tpu_custom_call" | custom-call | tf_op jit(solution)/shard_map/pallas_call | solution.py:346
  37.0 0.1 collective-permute-start.10
  37.1 4.3 %collective-permute-done.10.refs_1_ = f32[2,64,128]{2,1,0:T(8,128)S(1)} collective-permute-done((f32[2,64,128]{2,1,0:T(8,128)S(1)}, f32[2,64,128]{2,1,0:T(8,128)S(1)}, u32[]{:S(2)}, u32[]{:S(2)}) %collective-permute-start.10) | collective-permute-done | bytes 65568 | tf_op jit(solution)/shard_map/ppermute | solution.py:453
  41.4 1.1 %shard_map.83 = f32[2048,128]{1,0:T(8,128)} custom-call(f32[2,64,128]{2,1,0:T(8,128)S(1)} %get-tuple-element.82.refs_0_, f32[2,64,128]{2,1,0:T(8,128)S(1)} %collective-permute-done.10.refs_1_, f32[2,64,128]{2,1,0:T(8,128)S(1)} %get-tuple-element.83.refs_2_, f32[16,64,128]{2,1,0:T(8,128)S(1)} %get-tuple-element.62.carried_ref.refs_3_, ...), custom_call_target="tpu_custom_call" | custom-call | tf_op jit(solution)/shard_map/pallas_call | solution.py:346
Async XLA Ops:
  2.2 11.7 %collective-permute-start = (f32[2,16,16,128]{3,2,1,0:T(8,128)S(1)}, f32[2,16,16,128]{3,2,1,0:T(8,128)S(1)}, u32[]{:S(2)}, u32[]{:S(2)}) collective-permute-start(f32[2,16,16,128]{3,2,1,0:T(8,128)S(1)} %get-tuple-element.59.mine_ref), channel_id=1, source_target_pairs={{0,128},{1,2},{2,1},{3,4},{4,3},{5,6},{6,5},{7,8},{8,7},{9,10},{10... | collective-permute-start | bytes 786440 | tf_op jit(solution)/shard_map/ppermute | solution.py:410
  7.8 6.1 %collective-permute-start.1 = (f32[2,16,16,128]{3,2,1,0:T(8,128)S(1)}, f32[2,16,16,128]{3,2,1,0:T(8,128)S(1)}, u32[]{:S(2)}, u32[]{:S(2)}) collective-permute-start(f32[2,16,16,128]{3,2,1,0:T(8,128)S(1)} %get-tuple-element.60.near_mine_ref), channel_id=1, source_target_pairs={{0,1},{1,0},{2,3},{3,2},{4,5},{5,4},{6,7},{7,6},{8,9},{9,8},{10,11... | collective-permute-start | bytes 786440 | tf_op jit(solution)/shard_map/ppermute | solution.py:421
  7.9 11.7 %collective-permute-start.3 = (f32[2,16,16,128]{3,2,1,0:T(8,128)S(1)}, f32[2,16,16,128]{3,2,1,0:T(8,128)S(1)}, u32[]{:S(2)}, u32[]{:S(2)}) collective-permute-start(f32[2,16,16,128]{3,2,1,0:T(8,128)S(1)} %get-tuple-element.65.mine_ref), channel_id=1, source_target_pairs={{0,255},{1,2},{2,1},{3,4},{4,3},{5,6},{6,5},{7,8},{8,7},{9,10},{10... | collective-permute-start | bytes 786440 | tf_op jit(solution)/shard_map/ppermute | solution.py:420
  11.0 8.6 %collective-permute-start.4 = (f32[2,16,16,128]{3,2,1,0:T(8,128)S(1)}, f32[2,16,16,128]{3,2,1,0:T(8,128)S(1)}, u32[]{:S(2)}, u32[]{:S(2)}) collective-permute-start(f32[2,16,16,128]{3,2,1,0:T(8,128)S(1)} %get-tuple-element.66.near_mine_ref), channel_id=1, source_target_pairs={{0,1},{1,0},{2,3},{3,2},{4,5},{5,4},{6,7},{7,6},{8,9},{9,8},{10,11... | collective-permute-start | bytes 786440 | tf_op jit(solution)/shard_map/ppermute | solution.py:421
  14.9 6.3 %collective-permute-start.2 = (f32[3,64,128]{2,1,0:T(8,128)S(1)}, f32[3,64,128]{2,1,0:T(8,128)S(1)}, u32[]{:S(2)}, u32[]{:S(2)}) collective-permute-start(f32[3,64,128]{2,1,0:T(8,128)S(1)} %get-tuple-element.61.ends_ref.refs_0_), channel_id=1, source_target_pairs={{0,128},{128,0},{1,129},{129,1},{2,130},{130,2},{3,131},{131,3},{4... | collective-permute-start | bytes 294920 | tf_op jit(solution)/shard_map/ppermute | solution.py:435
  20.6 5.3 %collective-permute-start.5 = (f32[3,64,128]{2,1,0:T(8,128)S(1)}, f32[3,64,128]{2,1,0:T(8,128)S(1)}, u32[]{:S(2)}, u32[]{:S(2)}) collective-permute-start(f32[3,64,128]{2,1,0:T(8,128)S(1)} %get-tuple-element.67.ends_ref), channel_id=1, source_target_pairs={{0,128},{128,0},{1,129},{129,1},{2,130},{130,2},{3,131},{131,3},{4... | collective-permute-start | bytes 294920 | tf_op jit(solution)/shard_map/ppermute | solution.py:435
  21.6 10.2 %collective-permute-start.8 = (f32[16,16,128]{2,1,0:T(8,128)S(1)}, f32[16,16,128]{2,1,0:T(8,128)S(1)}, u32[]{:S(2)}, u32[]{:S(2)}) collective-permute-start(f32[16,16,128]{2,1,0:T(8,128)S(1)} %get-tuple-element.77), channel_id=1, source_target_pairs={{0,128},{1,2},{2,1},{3,4},{4,3},{5,6},{6,5},{7,8},{8,7},{9,10},{10... | collective-permute-start | bytes 393224 | tf_op jit(solution)/shard_map/ppermute | solution.py:441
  25.9 5.9 %collective-permute-start.9 = (f32[16,16,128]{2,1,0:T(8,128)S(1)}, f32[16,16,128]{2,1,0:T(8,128)S(1)}, u32[]{:S(2)}, u32[]{:S(2)}) collective-permute-start(f32[16,16,128]{2,1,0:T(8,128)S(1)} %get-tuple-element.78), channel_id=1, source_target_pairs={{0,1},{1,0},{2,3},{3,2},{4,5},{5,4},{6,7},{7,6},{8,9},{9,8},{10,11... | collective-permute-start | bytes 393224 | tf_op jit(solution)/shard_map/ppermute | solution.py:442
  26.3 10.2 %collective-permute-start.6 = (f32[16,16,128]{2,1,0:T(8,128)S(1)}, f32[16,16,128]{2,1,0:T(8,128)S(1)}, u32[]{:S(2)}, u32[]{:S(2)}) collective-permute-start(f32[16,16,128]{2,1,0:T(8,128)S(1)} %get-tuple-element.73), channel_id=1, source_target_pairs={{0,128},{1,2},{2,1},{3,4},{4,3},{5,6},{6,5},{7,8},{8,7},{9,10},{10... | collective-permute-start | bytes 393224 | tf_op jit(solution)/shard_map/ppermute | solution.py:441
  29.6 6.9 %collective-permute-start.7 = (f32[16,16,128]{2,1,0:T(8,128)S(1)}, f32[16,16,128]{2,1,0:T(8,128)S(1)}, u32[]{:S(2)}, u32[]{:S(2)}) collective-permute-start(f32[16,16,128]{2,1,0:T(8,128)S(1)} %get-tuple-element.74), channel_id=1, source_target_pairs={{0,1},{1,0},{2,3},{3,2},{4,5},{5,4},{6,7},{7,6},{8,9},{9,8},{10,11... | collective-permute-start | bytes 393224 | tf_op jit(solution)/shard_map/ppermute | solution.py:442
  37.0 4.4 %collective-permute-start.10 = (f32[2,64,128]{2,1,0:T(8,128)S(1)}, f32[2,64,128]{2,1,0:T(8,128)S(1)}, u32[]{:S(2)}, u32[]{:S(2)}) collective-permute-start(f32[2,64,128]{2,1,0:T(8,128)S(1)} %get-tuple-element.82.refs_0_), channel_id=1, source_target_pairs={{0,128},{128,0},{1,129},{129,1},{2,130},{130,2},{3,131},{131,3},{4... | collective-permute-start | bytes 196616 | tf_op jit(solution)/shard_map/ppermute | solution.py:453

commit v6 on v5

--- a/solution.py
+++ b/solution.py
@@ -228,7 +228,9 @@
     rows, groups, cells = pivot_ref.shape
     size = groups // 4
     here = pl.ds(start, groups)
-    ends_ref[2] = kappa_ref[rows - 1, here]
+    if start == 0:
+        ends_ref[2] = kappa_ref[rows - 1, here]
+        ends_ref[3] = kappa_ref[rows - 1, pl.ds(groups, groups)]
     high = odd_surf()
     find_sides(far_ref[...].reshape(2 * rows * size, cells), near_ref[...].reshape(2 * rows * size, cells), select_ref, found_ref)
     weights = [spread(weight_ref[2], size), spread(weight_ref[1], size)]
@@ -266,10 +268,10 @@
             solved_ref[r] = solved
 
 
-def meet_kernel(ends_ref, other_ref, carried_ref, solved_ref, current_ref, far_ref, near_ref, mix_ref):
+def meet_kernel(edge, ends_ref, other_ref, edges_ref, other_edges_ref, carried_ref, solved_ref, current_ref, far_ref, near_ref, mix_ref):
     rows, groups, cells = current_ref.shape
     odd = odd_surf()
-    face = FACE * inverse(ends_ref[2] + other_ref[2])
+    face = FACE * inverse(edges_ref[edge] + other_edges_ref[edge])
     own, other = ends_ref[0], other_ref[0]
     scale = inverse(own * other + face * (own + other))
     mine = (other + face) * scale
@@ -427,7 +429,7 @@
     for i in range(2):
         firsts.append(call(
             functools.partial(first_kernel, i * half),
-            [(2, 4) + half_side, half_whole, half_whole, half_whole, (3, half, cells)],
+            [(2, 4) + half_side, half_whole, half_whole, half_whole, (2 if i else 4, half, cells)],
             kappa, base, face, rhs, mine[i], far_both[i], near_mine[i], near_both[i], select, weight,
             *[done[4] for done in firsts],
             scratch=[found_both],
@@ -436,7 +438,8 @@
     for i in range(2):
         couple, pivot, carried, solved, ends = firsts[i]
         meets.append(call(
-            meet_kernel, [half_whole, half_side, half_side, (2, half, cells)], ends, others[i], carried, solved
+            functools.partial(meet_kernel, 2 + i), [half_whole, half_side, half_side, (2, half, cells)],
+            ends, others[i], firsts[0][4], others[0], carried, solved,
         ))
     far_current = [lax.ppermute(meets[i][1], ("normal", "surf"), far[2 + i]) for i in range(2)]
     near_current = [lax.ppermute(meet[2], "surf", near) for meet in meets]

time: 42.6 us -> 42.6 us (level)
  transfers between devices with their start and end apart: 11 -> 11, of which waited for: 5 -> 6; matrix products, arithmetic and copies ran while one was open for 0% -> 0% of each run, Pallas kernels for 19% -> 19%
where the time goes in v6:
time: 42.6 us; the launch traced here: 42.5 us
  starting transfers between devices  17.7 us (42%)
  waiting for transfers between devices  12.7 us (30%)
  Pallas kernels  12 us (28%)
    pallas_call x11, Pallas kernels, call(): pl.pallas_call(kernel, out_shape=[jax.ShapeDtypeStruct(out, jnp.float32)...  12 us
    ppermute x2, starting transfers between devices, body(): lax.ppermute(meets[i][1], ('normal', 'surf'), far[2 + i])  7.64 us
    ppermute x2, waiting for transfers between devices, body(): lax.ppermute(meets[i][1], ('normal', 'surf'), far[2 + i])  4.86 us
    ppermute x1, starting transfers between devices, body(): far_0 = lax.ppermute(mine_0, ('normal', 'surf'), far[0])  4.54 us
    ppermute x1, waiting for transfers between devices, body(): other_ends = lax.ppermute(end, 'normal', swap)  4.25 us
    ppermute x1, starting transfers between devices, body(): far_both = (far_0, lax.ppermute(mine_1, ('normal', 'surf'), far[1]))  3.1 us
    ppermute x1, waiting for transfers between devices, body(): far_both = (far_0, lax.ppermute(mine_1, ('normal', 'surf'), far[1]))  3.1 us
    ppermute x2, starting transfers between devices, body(): others.append(lax.ppermute(firsts[i][4], 'normal', swap))  2.22 us
  transfers between devices with their start and end apart: 11, of which 6 were waited for; matrix products, arithmetic and copies ran while one was open for 0% of the time, Pallas kernels for 19%

profile of v6, /device:TPU:128, one launch (start us, length us, event | category | flops | bytes accessed | tf_op | source)
XLA Modules:
  0.0 42.5 jit_solution(3263459264493592828)
XLA Ops:
  0.0 2.2 %shard_map.73 = (f32[16,128,128]{2,1,0:T(8,128)S(1)}, bf16[16,256,128]{2,1,0:T(8,128)(2,1)S(1)}, f32[2,16,16,128]{3,2,1,0:T(8,128)S(1)}, bf16[128,256]{1,0:T(8,1...) custom-call(bf16[256,16,128]{2,1,0:T(8,128)(2,1)} %pops_hbm.1, ...), custom_call_target="tpu_custom_call" | custom-call | tf_op jit(solution)/shard_map/pallas_call | solution.py:348
  2.2 4.5 %collective-permute-start = (f32[2,16,16,128]{3,2,1,0:T(8,128)S(1)}, f32[2,16,16,128]{3,2,1,0:T(8,128)S(1)}, u32[]{:S(2)}, u32[]{:S(2)}) collective-permute-start(f32[2,16,16,128]{3,2,1,0:T(8,128)S(1)} %get-tuple-element.59.mine_ref), channel_id=1, source_target_pairs={{0,128},{1,2},{2,1},{3,4},{4,3},{5,6},{6,5},{7,8},{8,7},{9,10},{10... | collective-permute-start | bytes 786440 | tf_op jit(solution)/shard_map/ppermute | solution.py:412
  6.8 1.0 %shard_map.74 = (f32[16,128,128]{2,1,0:T(8,128)S(1)}, f32[2,16,16,128]{3,2,1,0:T(8,128)S(1)}, f32[2,16,16,128]{3,2,1,0:T(8,128)S(1)}, f32[2,16,16,128]{3,2,1,0:T...) custom-call(f32[2048,128]{1,0:T(8,128)S(1)} %get-tuple-element.47.lines_ref, ...), custom_call_target="tpu_custom_call" | custom-call | tf_op jit(solution)/shard_map/pallas_call | solution.py:348
  7.8 0.1 collective-permute-start.1
  7.9 3.1 %collective-permute-start.3 = (f32[2,16,16,128]{3,2,1,0:T(8,128)S(1)}, f32[2,16,16,128]{3,2,1,0:T(8,128)S(1)}, u32[]{:S(2)}, u32[]{:S(2)}) collective-permute-start(f32[2,16,16,128]{3,2,1,0:T(8,128)S(1)} %get-tuple-element.65.mine_ref), channel_id=1, source_target_pairs={{0,255},{1,2},{2,1},{3,4},{4,3},{5,6},{6,5},{7,8},{8,7},{9,10},{10... | collective-permute-start | bytes 786440 | tf_op jit(solution)/shard_map/ppermute | solution.py:422
  11.0 0.0 collective-permute-start.4
  11.0 2.7 %shard_map.75 = (f32[16,128,128]{2,1,0:T(8,128)S(1)}, f32[16,128,128]{2,1,0:T(8,128)S(1)}, f32[16,128,128]{2,1,0:T(8,128)S(1)}, f32[16,128,128]{2,1,0:T(8,128)S(1)}, f32[4,16,128,128]{3,2,1,0:T(8,128)S(1)}) custom-call(f32[16,128,128]{2,1,0:T(8,128)S(1)} %get-tuple-element.46.kappa_ref, f32[16,128,128]{2,1,0:T(8,128)S(1)} %get-tuple-element.49.current_ref, ...), custom_call_target="tpu_custom_call" | custom-call | tf_op jit(solution)/shard_map/pallas_call | solution.py:348
  13.7 0.3 collective-permute-done.far_ref
  13.9 0.0 collective-permute-done.1.near_ref
  13.9 1.0 %shard_map.76 = (f32[2,4,16,16,128]{4,3,2,1,0:T(8,128)S(1)}, f32[16,64,128]{2,1,0:T(8,128)S(1)}, f32[16,64,128]{2,1,0:T(8,128)S(1)}, f32[16,64,128]{2,1,0:T(8,128)S(1)}, f32[4,64,128]{2,1,0:T(8,128)S(1)}) custom-call(f32[16,128,128]{2,1,0:T(8,128)S(1)} %get-tuple-element.46.kappa_ref, f32[16,128,128]{2,1,0:T(8,128)S(1)} %get-tuple-element.56.base_ref, ...), custom_call_target="tpu_custom_call" | custom-call | tf_op jit(solution)/shard_map/pallas_call | solution.py:348
  14.9 1.6 %collective-permute-start.2 = (f32[4,64,128]{2,1,0:T(8,128)S(1)}, f32[4,64,128]{2,1,0:T(8,128)S(1)}, u32[]{:S(2)}, u32[]{:S(2)}) collective-permute-start(f32[4,64,128]{2,1,0:T(8,128)S(1)} %get-tuple-element.61.ends_ref.edges_ref.refs_0_), channel_id=1, source_target_pairs={{0,128},{128,0},{1,129},{129,1},{2,130},{130,2},{3,131},{131,3},{4... | collective-permute-start | bytes 393224 | tf_op jit(solution)/shard_map/ppermute | solution.py:437
  16.5 3.1 %collective-permute-done.3.far_ref = f32[2,16,16,128]{3,2,1,0:T(8,128)S(1)} collective-permute-done((f32[2,16,16,128]{3,2,1,0:T(8,128)S(1)}, f32[2,16,16,128]{3,2,1,0:T(8,128)S(1)}, u32[]{:S(2)}, u32[]{:S(2)}) %collective-permute-start.3) | collective-permute-done | bytes 262176 | tf_op jit(solution)/shard_map/ppermute | solution.py:422
  19.6 0.0 collective-permute-done.4.near_ref
  19.6 1.0 %shard_map.78 = (f32[2,4,16,16,128]{4,3,2,1,0:T(8,128)S(1)}, f32[16,64,128]{2,1,0:T(8,128)S(1)}, f32[16,64,128]{2,1,0:T(8,128)S(1)}, f32[16,64,128]{2,1,0:T(8,128)S(1)}, f32[2,64,128]{2,1,0:T(8,128)S(1)}) custom-call(f32[16,128,128]{2,1,0:T(8,128)S(1)} %get-tuple-element.46.kappa_ref, f32[16,128,128]{2,1,0:T(8,128)S(1)} %get-tuple-element.56.base_ref, ...), custom_call_target="tpu_custom_call" | custom-call | tf_op jit(solution)/shard_map/pallas_call | solution.py:348
  20.6 0.6 %collective-permute-start.5 = (f32[2,64,128]{2,1,0:T(8,128)S(1)}, f32[2,64,128]{2,1,0:T(8,128)S(1)}, u32[]{:S(2)}, u32[]{:S(2)}) collective-permute-start(f32[2,64,128]{2,1,0:T(8,128)S(1)} %get-tuple-element.67.ends_ref), channel_id=1, source_target_pairs={{0,128},{128,0},{1,129},{129,1},{2,130},{130,2},{3,131},{131,3},{4... | collective-permute-start | bytes 196616 | tf_op jit(solution)/shard_map/ppermute | solution.py:437
  21.2 0.2 collective-permute-done.2.other_ref.other_edges_ref
  21.4 0.4 shard_map.77
  21.8 4.1 %collective-permute-start.8 = (f32[16,16,128]{2,1,0:T(8,128)S(1)}, f32[16,16,128]{2,1,0:T(8,128)S(1)}, u32[]{:S(2)}, u32[]{:S(2)}) collective-permute-start(f32[16,16,128]{2,1,0:T(8,128)S(1)} %get-tuple-element.77), channel_id=1, source_target_pairs={{0,128},{1,2},{2,1},{3,4},{4,3},{5,6},{6,5},{7,8},{8,7},{9,10},{10... | collective-permute-start | bytes 393224 | tf_op jit(solution)/shard_map/ppermute | solution.py:444
  25.9 0.0 collective-permute-start.9
  25.9 0.0 collective-permute-done.5.other_ref
  25.9 0.4 shard_map.79
  26.3 3.5 %collective-permute-start.6 = (f32[16,16,128]{2,1,0:T(8,128)S(1)}, f32[16,16,128]{2,1,0:T(8,128)S(1)}, u32[]{:S(2)}, u32[]{:S(2)}) collective-permute-start(f32[16,16,128]{2,1,0:T(8,128)S(1)} %get-tuple-element.73), channel_id=1, source_target_pairs={{0,128},{1,2},{2,1},{3,4},{4,3},{5,6},{6,5},{7,8},{8,7},{9,10},{10... | collective-permute-start | bytes 393224 | tf_op jit(solution)/shard_map/ppermute | solution.py:444
  29.8 0.0 collective-permute-start.7
  29.9 1.2 %shard_map.80.rhs_ref = f32[16,128,128]{2,1,0:T(8,128)S(1)} custom-call(f32[16,64,128]{2,1,0:T(8,128)S(1)} %get-tuple-element.64.current_0, f32[16,64,128]{2,1,0:T(8,128)S(1)} %get-tuple-element.70.current_1, f32[16,128,128]{2,1,0:T(8,128)S(1)} %get-tuple-element.71.emission_ref, f32[4,16,128,128]{3,2,1,0:T(8,128)S(1)} %get-tuple-element.72.couple_ref, ...), custom_call_target="tpu_custom_call" | custom-call | tf_op jit(solution)/shard_map/pallas_call | solution.py:348
  31.1 0.9 %collective-permute-done.8.far_ref = f32[16,16,128]{2,1,0:T(8,128)S(1)} collective-permute-done((f32[16,16,128]{2,1,0:T(8,128)S(1)}, f32[16,16,128]{2,1,0:T(8,128)S(1)}, u32[]{:S(2)}, u32[]{:S(2)}) %collective-permute-start.8) | collective-permute-done | bytes 131104 | tf_op jit(solution)/shard_map/ppermute | solution.py:444
  32.0 0.0 collective-permute-done.9.near_ref
  32.0 0.5 %shard_map.81 = (f32[16,64,128]{2,1,0:T(8,128)S(1)}, f32[64,128]{1,0:T(8,128)S(1)}) custom-call(f32[16,128,128]{2,1,0:T(8,128)S(1)} %shard_map.80.rhs_ref, f32[16,16,128]{2,1,0:T(8,128)S(1)} %collective-permute-done.8.far_ref, f32[16,16,128]{2,1,0:T(8,128)S(1)} %collective-permute-done.9.near_ref, f32[2,4,16,16,128]{4,3,2,1,0:T(8,128)S(1)} %get-tuple-element.79.couple_ref, ...), custom_call_target="tpu_custom_call" | custom-call | tf_op jit(solution)/shard_map/pallas_call | solution.py:348
  32.6 3.9 %collective-permute-done.6.far_ref = f32[16,16,128]{2,1,0:T(8,128)S(1)} collective-permute-done((f32[16,16,128]{2,1,0:T(8,128)S(1)}, f32[16,16,128]{2,1,0:T(8,128)S(1)}, u32[]{:S(2)}, u32[]{:S(2)}) %collective-permute-start.6) | collective-permute-done | bytes 131104 | tf_op jit(solution)/shard_map/ppermute | solution.py:444
  36.5 0.0 collective-permute-done.7.near_ref
  36.5 0.5 %shard_map.82 = (f32[16,64,128]{2,1,0:T(8,128)S(1)}, f32[2,64,128]{2,1,0:T(8,128)S(1)}) custom-call(f32[16,128,128]{2,1,0:T(8,128)S(1)} %shard_map.80.rhs_ref, f32[16,16,128]{2,1,0:T(8,128)S(1)} %collective-permute-done.6.far_ref, f32[16,16,128]{2,1,0:T(8,128)S(1)} %collective-permute-done.7.near_ref, ...), custom_call_target="tpu_custom_call" | custom-call | tf_op jit(solution)/shard_map/pallas_call | solution.py:348
  37.0 0.1 collective-permute-start.10
  37.1 4.3 %collective-permute-done.10.refs_1_ = f32[2,64,128]{2,1,0:T(8,128)S(1)} collective-permute-done((f32[2,64,128]{2,1,0:T(8,128)S(1)}, f32[2,64,128]{2,1,0:T(8,128)S(1)}, u32[]{:S(2)}, u32[]{:S(2)}) %collective-permute-start.10) | collective-permute-done | bytes 65568 | tf_op jit(solution)/shard_map/ppermute | solution.py:456
  41.4 1.1 %shard_map.83 = f32[2048,128]{1,0:T(8,128)} custom-call(f32[2,64,128]{2,1,0:T(8,128)S(1)} %get-tuple-element.82.refs_0_, f32[2,64,128]{2,1,0:T(8,128)S(1)} %collective-permute-done.10.refs_1_, f32[2,64,128]{2,1,0:T(8,128)S(1)} %get-tuple-element.83.refs_2_, f32[16,64,128]{2,1,0:T(8,128)S(1)} %get-tuple-element.62.carried_ref.refs_3_, ...), custom_call_target="tpu_custom_call" | custom-call | tf_op jit(solution)/shard_map/pallas_call | solution.py:348
Async XLA Ops:
  2.2 11.7 %collective-permute-start = (f32[2,16,16,128]{3,2,1,0:T(8,128)S(1)}, f32[2,16,16,128]{3,2,1,0:T(8,128)S(1)}, u32[]{:S(2)}, u32[]{:S(2)}) collective-permute-start(f32[2,16,16,128]{3,2,1,0:T(8,128)S(1)} %get-tuple-element.59.mine_ref), channel_id=1, source_target_pairs={{0,128},{1,2},{2,1},{3,4},{4,3},{5,6},{6,5},{7,8},{8,7},{9,10},{10... | collective-permute-start | bytes 786440 | tf_op jit(solution)/shard_map/ppermute | solution.py:412
  7.8 6.1 %collective-permute-start.1 = (f32[2,16,16,128]{3,2,1,0:T(8,128)S(1)}, f32[2,16,16,128]{3,2,1,0:T(8,128)S(1)}, u32[]{:S(2)}, u32[]{:S(2)}) collective-permute-start(f32[2,16,16,128]{3,2,1,0:T(8,128)S(1)} %get-tuple-element.60.near_mine_ref), channel_id=1, source_target_pairs={{0,1},{1,0},{2,3},{3,2},{4,5},{5,4},{6,7},{7,6},{8,9},{9,8},{10,11... | collective-permute-start | bytes 786440 | tf_op jit(solution)/shard_map/ppermute | solution.py:423
  7.9 11.7 %collective-permute-start.3 = (f32[2,16,16,128]{3,2,1,0:T(8,128)S(1)}, f32[2,16,16,128]{3,2,1,0:T(8,128)S(1)}, u32[]{:S(2)}, u32[]{:S(2)}) collective-permute-start(f32[2,16,16,128]{3,2,1,0:T(8,128)S(1)} %get-tuple-element.65.mine_ref), channel_id=1, source_target_pairs={{0,255},{1,2},{2,1},{3,4},{4,3},{5,6},{6,5},{7,8},{8,7},{9,10},{10... | collective-permute-start | bytes 786440 | tf_op jit(solution)/shard_map/ppermute | solution.py:422
  11.0 8.6 %collective-permute-start.4 = (f32[2,16,16,128]{3,2,1,0:T(8,128)S(1)}, f32[2,16,16,128]{3,2,1,0:T(8,128)S(1)}, u32[]{:S(2)}, u32[]{:S(2)}) collective-permute-start(f32[2,16,16,128]{3,2,1,0:T(8,128)S(1)} %get-tuple-element.66.near_mine_ref), channel_id=1, source_target_pairs={{0,1},{1,0},{2,3},{3,2},{4,5},{5,4},{6,7},{7,6},{8,9},{9,8},{10,11... | collective-permute-start | bytes 786440 | tf_op jit(solution)/shard_map/ppermute | solution.py:423
  14.9 6.5 %collective-permute-start.2 = (f32[4,64,128]{2,1,0:T(8,128)S(1)}, f32[4,64,128]{2,1,0:T(8,128)S(1)}, u32[]{:S(2)}, u32[]{:S(2)}) collective-permute-start(f32[4,64,128]{2,1,0:T(8,128)S(1)} %get-tuple-element.61.ends_ref.edges_ref.refs_0_), channel_id=1, source_target_pairs={{0,128},{128,0},{1,129},{129,1},{2,130},{130,2},{3,131},{131,3},{4... | collective-permute-start | bytes 393224 | tf_op jit(solution)/shard_map/ppermute | solution.py:437
  20.6 5.3 %collective-permute-start.5 = (f32[2,64,128]{2,1,0:T(8,128)S(1)}, f32[2,64,128]{2,1,0:T(8,128)S(1)}, u32[]{:S(2)}, u32[]{:S(2)}) collective-permute-start(f32[2,64,128]{2,1,0:T(8,128)S(1)} %get-tuple-element.67.ends_ref), channel_id=1, source_target_pairs={{0,128},{128,0},{1,129},{129,1},{2,130},{130,2},{3,131},{131,3},{4... | collective-permute-start | bytes 196616 | tf_op jit(solution)/shard_map/ppermute | solution.py:437
  21.8 10.2 %collective-permute-start.8 = (f32[16,16,128]{2,1,0:T(8,128)S(1)}, f32[16,16,128]{2,1,0:T(8,128)S(1)}, u32[]{:S(2)}, u32[]{:S(2)}) collective-permute-start(f32[16,16,128]{2,1,0:T(8,128)S(1)} %get-tuple-element.77), channel_id=1, source_target_pairs={{0,128},{1,2},{2,1},{3,4},{4,3},{5,6},{6,5},{7,8},{8,7},{9,10},{10... | collective-permute-start | bytes 393224 | tf_op jit(solution)/shard_map/ppermute | solution.py:444
  25.9 6.1 %collective-permute-start.9 = (f32[16,16,128]{2,1,0:T(8,128)S(1)}, f32[16,16,128]{2,1,0:T(8,128)S(1)}, u32[]{:S(2)}, u32[]{:S(2)}) collective-permute-start(f32[16,16,128]{2,1,0:T(8,128)S(1)} %get-tuple-element.78), channel_id=1, source_target_pairs={{0,1},{1,0},{2,3},{3,2},{4,5},{5,4},{6,7},{7,6},{8,9},{9,8},{10,11... | collective-permute-start | bytes 393224 | tf_op jit(solution)/shard_map/ppermute | solution.py:445
  26.3 10.2 %collective-permute-start.6 = (f32[16,16,128]{2,1,0:T(8,128)S(1)}, f32[16,16,128]{2,1,0:T(8,128)S(1)}, u32[]{:S(2)}, u32[]{:S(2)}) collective-permute-start(f32[16,16,128]{2,1,0:T(8,128)S(1)} %get-tuple-element.73), channel_id=1, source_target_pairs={{0,128},{1,2},{2,1},{3,4},{4,3},{5,6},{6,5},{7,8},{8,7},{9,10},{10... | collective-permute-start | bytes 393224 | tf_op jit(solution)/shard_map/ppermute | solution.py:444
  29.8 6.7 %collective-permute-start.7 = (f32[16,16,128]{2,1,0:T(8,128)S(1)}, f32[16,16,128]{2,1,0:T(8,128)S(1)}, u32[]{:S(2)}, u32[]{:S(2)}) collective-permute-start(f32[16,16,128]{2,1,0:T(8,128)S(1)} %get-tuple-element.74), channel_id=1, source_target_pairs={{0,1},{1,0},{2,3},{3,2},{4,5},{5,4},{6,7},{7,6},{8,9},{9,8},{10,11... | collective-permute-start | bytes 393224 | tf_op jit(solution)/shard_map/ppermute | solution.py:445
  37.0 4.4 %collective-permute-start.10 = (f32[2,64,128]{2,1,0:T(8,128)S(1)}, f32[2,64,128]{2,1,0:T(8,128)S(1)}, u32[]{:S(2)}, u32[]{:S(2)}) collective-permute-start(f32[2,64,128]{2,1,0:T(8,128)S(1)} %get-tuple-element.82.refs_0_), channel_id=1, source_target_pairs={{0,128},{128,0},{1,129},{129,1},{2,130},{130,2},{3,131},{131,3},{4... | collective-permute-start | bytes 196616 | tf_op jit(solution)/shard_map/ppermute | solution.py:456

commit v7 on v6

--- a/solution.py
+++ b/solution.py
@@ -324,8 +324,8 @@
         mix_ref, carried_ref, solved_ref = halves[3 * i : 3 * i + 3]
         end_ref, other_ref = ends_ref.at[i], others_ref.at[i]
         rows, groups, cells = carried_ref.shape
-        step = groups // 2
-        for part in range(2):
+        step = groups // 4
+        for part in range(4):
             here = pl.ds(part * step, step)
             value = mix_ref[0, here, :] * end_ref[here, :] + mix_ref[1, here, :] * other_ref[here, :]
             lines_ref[pl.ds(start * rows + row_of(rows - 1, rows), step, stride=rows), :] = value
@@ -457,7 +457,7 @@
     (out,) = call(
         last_kernel, [lines.shape], end, other_ends, *parts[1:4], *parts[5:],
         out_space=HBM,
-        scratch=[pltpu.VMEM(lines.shape, jnp.float32), pltpu.SemaphoreType.DMA((4,))],
+        scratch=[pltpu.VMEM(lines.shape, jnp.float32), pltpu.SemaphoreType.DMA((8,))],
     )
     return out.reshape(groups, rows, cells)
 

time: 42.6 us -> 42.6 us (level)
  no operation moved by 1% of the time
where the time goes in v7:
time: 42.6 us; the launch traced here: 42.5 us
  starting transfers between devices  17.7 us (42%)
  waiting for transfers between devices  12.7 us (30%)
  Pallas kernels  12 us (28%)
    pallas_call x11, Pallas kernels, call(): pl.pallas_call(kernel, out_shape=[jax.ShapeDtypeStruct(out, jnp.float32)...  12 us
    ppermute x2, starting transfers between devices, body(): lax.ppermute(meets[i][1], ('normal', 'surf'), far[2 + i])  7.64 us
    ppermute x2, waiting for transfers between devices, body(): lax.ppermute(meets[i][1], ('normal', 'surf'), far[2 + i])  4.86 us
    ppermute x1, starting transfers between devices, body(): far_0 = lax.ppermute(mine_0, ('normal', 'surf'), far[0])  4.54 us
    ppermute x1, waiting for transfers between devices, body(): other_ends = lax.ppermute(end, 'normal', swap)  4.25 us
    ppermute x1, starting transfers between devices, body(): far_both = (far_0, lax.ppermute(mine_1, ('normal', 'surf'), far[1]))  3.1 us
    ppermute x1, waiting for transfers between devices, body(): far_both = (far_0, lax.ppermute(mine_1, ('normal', 'surf'), far[1]))  3.1 us
    ppermute x2, starting transfers between devices, body(): others.append(lax.ppermute(firsts[i][4], 'normal', swap))  2.22 us
  transfers between devices with their start and end apart: 11, of which 6 were waited for; matrix products, arithmetic and copies ran while one was open for 0% of the time, Pallas kernels for 19%

profile of v7, /device:TPU:128, one launch (start us, length us, event | category | flops | bytes accessed | tf_op | source)
XLA Modules:
  0.0 42.5 jit_solution(12278147268267182117)
XLA Ops:
  0.0 2.2 %shard_map.73 = (f32[16,128,128]{2,1,0:T(8,128)S(1)}, bf16[16,256,128]{2,1,0:T(8,128)(2,1)S(1)}, f32[2,16,16,128]{3,2,1,0:T(8,128)S(1)}, bf16[128,256]{1,0:T(8,1...) custom-call(bf16[256,16,128]{2,1,0:T(8,128)(2,1)} %pops_hbm.1, ...), custom_call_target="tpu_custom_call" | custom-call | tf_op jit(solution)/shard_map/pallas_call | solution.py:348
  2.2 4.5 %collective-permute-start = (f32[2,16,16,128]{3,2,1,0:T(8,128)S(1)}, f32[2,16,16,128]{3,2,1,0:T(8,128)S(1)}, u32[]{:S(2)}, u32[]{:S(2)}) collective-permute-start(f32[2,16,16,128]{3,2,1,0:T(8,128)S(1)} %get-tuple-element.59.mine_ref), channel_id=1, source_target_pairs={{0,128},{1,2},{2,1},{3,4},{4,3},{5,6},{6,5},{7,8},{8,7},{9,10},{10... | collective-permute-start | bytes 786440 | tf_op jit(solution)/shard_map/ppermute | solution.py:412
  6.8 1.0 %shard_map.74 = (f32[16,128,128]{2,1,0:T(8,128)S(1)}, f32[2,16,16,128]{3,2,1,0:T(8,128)S(1)}, f32[2,16,16,128]{3,2,1,0:T(8,128)S(1)}, f32[2,16,16,128]{3,2,1,0:T...) custom-call(f32[2048,128]{1,0:T(8,128)S(1)} %get-tuple-element.47.lines_ref, ...), custom_call_target="tpu_custom_call" | custom-call | tf_op jit(solution)/shard_map/pallas_call | solution.py:348
  7.8 0.1 collective-permute-start.1
  7.9 3.1 %collective-permute-start.3 = (f32[2,16,16,128]{3,2,1,0:T(8,128)S(1)}, f32[2,16,16,128]{3,2,1,0:T(8,128)S(1)}, u32[]{:S(2)}, u32[]{:S(2)}) collective-permute-start(f32[2,16,16,128]{3,2,1,0:T(8,128)S(1)} %get-tuple-element.65.mine_ref), channel_id=1, source_target_pairs={{0,255},{1,2},{2,1},{3,4},{4,3},{5,6},{6,5},{7,8},{8,7},{9,10},{10... | collective-permute-start | bytes 786440 | tf_op jit(solution)/shard_map/ppermute | solution.py:422
  11.0 0.0 collective-permute-start.4
  11.0 2.7 %shard_map.75 = (f32[16,128,128]{2,1,0:T(8,128)S(1)}, f32[16,128,128]{2,1,0:T(8,128)S(1)}, f32[16,128,128]{2,1,0:T(8,128)S(1)}, f32[16,128,128]{2,1,0:T(8,128)S(1)}, f32[4,16,128,128]{3,2,1,0:T(8,128)S(1)}) custom-call(f32[16,128,128]{2,1,0:T(8,128)S(1)} %get-tuple-element.46.kappa_ref, f32[16,128,128]{2,1,0:T(8,128)S(1)} %get-tuple-element.49.current_ref, ...), custom_call_target="tpu_custom_call" | custom-call | tf_op jit(solution)/shard_map/pallas_call | solution.py:348
  13.7 0.3 collective-permute-done.far_ref
  13.9 0.0 collective-permute-done.1.near_ref
  13.9 1.0 %shard_map.76 = (f32[2,4,16,16,128]{4,3,2,1,0:T(8,128)S(1)}, f32[16,64,128]{2,1,0:T(8,128)S(1)}, f32[16,64,128]{2,1,0:T(8,128)S(1)}, f32[16,64,128]{2,1,0:T(8,128)S(1)}, f32[4,64,128]{2,1,0:T(8,128)S(1)}) custom-call(f32[16,128,128]{2,1,0:T(8,128)S(1)} %get-tuple-element.46.kappa_ref, f32[16,128,128]{2,1,0:T(8,128)S(1)} %get-tuple-element.56.base_ref, ...), custom_call_target="tpu_custom_call" | custom-call | tf_op jit(solution)/shard_map/pallas_call | solution.py:348
  14.9 1.6 %collective-permute-start.2 = (f32[4,64,128]{2,1,0:T(8,128)S(1)}, f32[4,64,128]{2,1,0:T(8,128)S(1)}, u32[]{:S(2)}, u32[]{:S(2)}) collective-permute-start(f32[4,64,128]{2,1,0:T(8,128)S(1)} %get-tuple-element.61.ends_ref.edges_ref.refs_0_), channel_id=1, source_target_pairs={{0,128},{128,0},{1,129},{129,1},{2,130},{130,2},{3,131},{131,3},{4... | collective-permute-start | bytes 393224 | tf_op jit(solution)/shard_map/ppermute | solution.py:437
  16.5 3.1 %collective-permute-done.3.far_ref = f32[2,16,16,128]{3,2,1,0:T(8,128)S(1)} collective-permute-done((f32[2,16,16,128]{3,2,1,0:T(8,128)S(1)}, f32[2,16,16,128]{3,2,1,0:T(8,128)S(1)}, u32[]{:S(2)}, u32[]{:S(2)}) %collective-permute-start.3) | collective-permute-done | bytes 262176 | tf_op jit(solution)/shard_map/ppermute | solution.py:422
  19.6 0.0 collective-permute-done.4.near_ref
  19.6 1.0 %shard_map.78 = (f32[2,4,16,16,128]{4,3,2,1,0:T(8,128)S(1)}, f32[16,64,128]{2,1,0:T(8,128)S(1)}, f32[16,64,128]{2,1,0:T(8,128)S(1)}, f32[16,64,128]{2,1,0:T(8,128)S(1)}, f32[2,64,128]{2,1,0:T(8,128)S(1)}) custom-call(f32[16,128,128]{2,1,0:T(8,128)S(1)} %get-tuple-element.46.kappa_ref, f32[16,128,128]{2,1,0:T(8,128)S(1)} %get-tuple-element.56.base_ref, ...), custom_call_target="tpu_custom_call" | custom-call | tf_op jit(solution)/shard_map/pallas_call | solution.py:348
  20.6 0.6 %collective-permute-start.5 = (f32[2,64,128]{2,1,0:T(8,128)S(1)}, f32[2,64,128]{2,1,0:T(8,128)S(1)}, u32[]{:S(2)}, u32[]{:S(2)}) collective-permute-start(f32[2,64,128]{2,1,0:T(8,128)S(1)} %get-tuple-element.67.ends_ref), channel_id=1, source_target_pairs={{0,128},{128,0},{1,129},{129,1},{2,130},{130,2},{3,131},{131,3},{4... | collective-permute-start | bytes 196616 | tf_op jit(solution)/shard_map/ppermute | solution.py:437
  21.2 0.2 collective-permute-done.2.other_ref.other_edges_ref
  21.4 0.4 shard_map.77
  21.8 4.1 %collective-permute-start.8 = (f32[16,16,128]{2,1,0:T(8,128)S(1)}, f32[16,16,128]{2,1,0:T(8,128)S(1)}, u32[]{:S(2)}, u32[]{:S(2)}) collective-permute-start(f32[16,16,128]{2,1,0:T(8,128)S(1)} %get-tuple-element.77), channel_id=1, source_target_pairs={{0,128},{1,2},{2,1},{3,4},{4,3},{5,6},{6,5},{7,8},{8,7},{9,10},{10... | collective-permute-start | bytes 393224 | tf_op jit(solution)/shard_map/ppermute | solution.py:444
  25.9 0.0 collective-permute-start.9
  25.9 0.0 collective-permute-done.5.other_ref
  25.9 0.4 shard_map.79
  26.3 3.5 %collective-permute-start.6 = (f32[16,16,128]{2,1,0:T(8,128)S(1)}, f32[16,16,128]{2,1,0:T(8,128)S(1)}, u32[]{:S(2)}, u32[]{:S(2)}) collective-permute-start(f32[16,16,128]{2,1,0:T(8,128)S(1)} %get-tuple-element.73), channel_id=1, source_target_pairs={{0,128},{1,2},{2,1},{3,4},{4,3},{5,6},{6,5},{7,8},{8,7},{9,10},{10... | collective-permute-start | bytes 393224 | tf_op jit(solution)/shard_map/ppermute | solution.py:444
  29.8 0.0 collective-permute-start.7
  29.9 1.2 %shard_map.80.rhs_ref = f32[16,128,128]{2,1,0:T(8,128)S(1)} custom-call(f32[16,64,128]{2,1,0:T(8,128)S(1)} %get-tuple-element.64.current_0, f32[16,64,128]{2,1,0:T(8,128)S(1)} %get-tuple-element.70.current_1, f32[16,128,128]{2,1,0:T(8,128)S(1)} %get-tuple-element.71.emission_ref, f32[4,16,128,128]{3,2,1,0:T(8,128)S(1)} %get-tuple-element.72.couple_ref, ...), custom_call_target="tpu_custom_call" | custom-call | tf_op jit(solution)/shard_map/pallas_call | solution.py:348
  31.1 0.9 %collective-permute-done.8.far_ref = f32[16,16,128]{2,1,0:T(8,128)S(1)} collective-permute-done((f32[16,16,128]{2,1,0:T(8,128)S(1)}, f32[16,16,128]{2,1,0:T(8,128)S(1)}, u32[]{:S(2)}, u32[]{:S(2)}) %collective-permute-start.8) | collective-permute-done | bytes 131104 | tf_op jit(solution)/shard_map/ppermute | solution.py:444
  32.0 0.0 collective-permute-done.9.near_ref
  32.0 0.5 %shard_map.81 = (f32[16,64,128]{2,1,0:T(8,128)S(1)}, f32[64,128]{1,0:T(8,128)S(1)}) custom-call(f32[16,128,128]{2,1,0:T(8,128)S(1)} %shard_map.80.rhs_ref, f32[16,16,128]{2,1,0:T(8,128)S(1)} %collective-permute-done.8.far_ref, f32[16,16,128]{2,1,0:T(8,128)S(1)} %collective-permute-done.9.near_ref, f32[2,4,16,16,128]{4,3,2,1,0:T(8,128)S(1)} %get-tuple-element.79.couple_ref, ...), custom_call_target="tpu_custom_call" | custom-call | tf_op jit(solution)/shard_map/pallas_call | solution.py:348
  32.6 3.9 %collective-permute-done.6.far_ref = f32[16,16,128]{2,1,0:T(8,128)S(1)} collective-permute-done((f32[16,16,128]{2,1,0:T(8,128)S(1)}, f32[16,16,128]{2,1,0:T(8,128)S(1)}, u32[]{:S(2)}, u32[]{:S(2)}) %collective-permute-start.6) | collective-permute-done | bytes 131104 | tf_op jit(solution)/shard_map/ppermute | solution.py:444
  36.5 0.0 collective-permute-done.7.near_ref
  36.5 0.5 %shard_map.82 = (f32[16,64,128]{2,1,0:T(8,128)S(1)}, f32[2,64,128]{2,1,0:T(8,128)S(1)}) custom-call(f32[16,128,128]{2,1,0:T(8,128)S(1)} %shard_map.80.rhs_ref, f32[16,16,128]{2,1,0:T(8,128)S(1)} %collective-permute-done.6.far_ref, f32[16,16,128]{2,1,0:T(8,128)S(1)} %collective-permute-done.7.near_ref, ...), custom_call_target="tpu_custom_call" | custom-call | tf_op jit(solution)/shard_map/pallas_call | solution.py:348
  37.0 0.1 collective-permute-start.10
  37.1 4.3 %collective-permute-done.10.refs_1_ = f32[2,64,128]{2,1,0:T(8,128)S(1)} collective-permute-done((f32[2,64,128]{2,1,0:T(8,128)S(1)}, f32[2,64,128]{2,1,0:T(8,128)S(1)}, u32[]{:S(2)}, u32[]{:S(2)}) %collective-permute-start.10) | collective-permute-done | bytes 65568 | tf_op jit(solution)/shard_map/ppermute | solution.py:456
  41.4 1.1 %shard_map.83 = f32[2048,128]{1,0:T(8,128)} custom-call(f32[2,64,128]{2,1,0:T(8,128)S(1)} %get-tuple-element.82.refs_0_, f32[2,64,128]{2,1,0:T(8,128)S(1)} %collective-permute-done.10.refs_1_, f32[2,64,128]{2,1,0:T(8,128)S(1)} %get-tuple-element.83.refs_2_, f32[16,64,128]{2,1,0:T(8,128)S(1)} %get-tuple-element.62.carried_ref.refs_3_, ...), custom_call_target="tpu_custom_call" | custom-call | tf_op jit(solution)/shard_map/pallas_call | solution.py:348
Async XLA Ops:
  2.2 11.7 %collective-permute-start = (f32[2,16,16,128]{3,2,1,0:T(8,128)S(1)}, f32[2,16,16,128]{3,2,1,0:T(8,128)S(1)}, u32[]{:S(2)}, u32[]{:S(2)}) collective-permute-start(f32[2,16,16,128]{3,2,1,0:T(8,128)S(1)} %get-tuple-element.59.mine_ref), channel_id=1, source_target_pairs={{0,128},{1,2},{2,1},{3,4},{4,3},{5,6},{6,5},{7,8},{8,7},{9,10},{10... | collective-permute-start | bytes 786440 | tf_op jit(solution)/shard_map/ppermute | solution.py:412
  7.8 6.1 %collective-permute-start.1 = (f32[2,16,16,128]{3,2,1,0:T(8,128)S(1)}, f32[2,16,16,128]{3,2,1,0:T(8,128)S(1)}, u32[]{:S(2)}, u32[]{:S(2)}) collective-permute-start(f32[2,16,16,128]{3,2,1,0:T(8,128)S(1)} %get-tuple-element.60.near_mine_ref), channel_id=1, source_target_pairs={{0,1},{1,0},{2,3},{3,2},{4,5},{5,4},{6,7},{7,6},{8,9},{9,8},{10,11... | collective-permute-start | bytes 786440 | tf_op jit(solution)/shard_map/ppermute | solution.py:423
  7.9 11.7 %collective-permute-start.3 = (f32[2,16,16,128]{3,2,1,0:T(8,128)S(1)}, f32[2,16,16,128]{3,2,1,0:T(8,128)S(1)}, u32[]{:S(2)}, u32[]{:S(2)}) collective-permute-start(f32[2,16,16,128]{3,2,1,0:T(8,128)S(1)} %get-tuple-element.65.mine_ref), channel_id=1, source_target_pairs={{0,255},{1,2},{2,1},{3,4},{4,3},{5,6},{6,5},{7,8},{8,7},{9,10},{10... | collective-permute-start | bytes 786440 | tf_op jit(solution)/shard_map/ppermute | solution.py:422
  11.0 8.6 %collective-permute-start.4 = (f32[2,16,16,128]{3,2,1,0:T(8,128)S(1)}, f32[2,16,16,128]{3,2,1,0:T(8,128)S(1)}, u32[]{:S(2)}, u32[]{:S(2)}) collective-permute-start(f32[2,16,16,128]{3,2,1,0:T(8,128)S(1)} %get-tuple-element.66.near_mine_ref), channel_id=1, source_target_pairs={{0,1},{1,0},{2,3},{3,2},{4,5},{5,4},{6,7},{7,6},{8,9},{9,8},{10,11... | collective-permute-start | bytes 786440 | tf_op jit(solution)/shard_map/ppermute | solution.py:423
  14.9 6.5 %collective-permute-start.2 = (f32[4,64,128]{2,1,0:T(8,128)S(1)}, f32[4,64,128]{2,1,0:T(8,128)S(1)}, u32[]{:S(2)}, u32[]{:S(2)}) collective-permute-start(f32[4,64,128]{2,1,0:T(8,128)S(1)} %get-tuple-element.61.ends_ref.edges_ref.refs_0_), channel_id=1, source_target_pairs={{0,128},{128,0},{1,129},{129,1},{2,130},{130,2},{3,131},{131,3},{4... | collective-permute-start | bytes 393224 | tf_op jit(solution)/shard_map/ppermute | solution.py:437
  20.6 5.3 %collective-permute-start.5 = (f32[2,64,128]{2,1,0:T(8,128)S(1)}, f32[2,64,128]{2,1,0:T(8,128)S(1)}, u32[]{:S(2)}, u32[]{:S(2)}) collective-permute-start(f32[2,64,128]{2,1,0:T(8,128)S(1)} %get-tuple-element.67.ends_ref), channel_id=1, source_target_pairs={{0,128},{128,0},{1,129},{129,1},{2,130},{130,2},{3,131},{131,3},{4... | collective-permute-start | bytes 196616 | tf_op jit(solution)/shard_map/ppermute | solution.py:437
  21.8 10.2 %collective-permute-start.8 = (f32[16,16,128]{2,1,0:T(8,128)S(1)}, f32[16,16,128]{2,1,0:T(8,128)S(1)}, u32[]{:S(2)}, u32[]{:S(2)}) collective-permute-start(f32[16,16,128]{2,1,0:T(8,128)S(1)} %get-tuple-element.77), channel_id=1, source_target_pairs={{0,128},{1,2},{2,1},{3,4},{4,3},{5,6},{6,5},{7,8},{8,7},{9,10},{10... | collective-permute-start | bytes 393224 | tf_op jit(solution)/shard_map/ppermute | solution.py:444
  25.9 6.1 %collective-permute-start.9 = (f32[16,16,128]{2,1,0:T(8,128)S(1)}, f32[16,16,128]{2,1,0:T(8,128)S(1)}, u32[]{:S(2)}, u32[]{:S(2)}) collective-permute-start(f32[16,16,128]{2,1,0:T(8,128)S(1)} %get-tuple-element.78), channel_id=1, source_target_pairs={{0,1},{1,0},{2,3},{3,2},{4,5},{5,4},{6,7},{7,6},{8,9},{9,8},{10,11... | collective-permute-start | bytes 393224 | tf_op jit(solution)/shard_map/ppermute | solution.py:445
  26.3 10.2 %collective-permute-start.6 = (f32[16,16,128]{2,1,0:T(8,128)S(1)}, f32[16,16,128]{2,1,0:T(8,128)S(1)}, u32[]{:S(2)}, u32[]{:S(2)}) collective-permute-start(f32[16,16,128]{2,1,0:T(8,128)S(1)} %get-tuple-element.73), channel_id=1, source_target_pairs={{0,128},{1,2},{2,1},{3,4},{4,3},{5,6},{6,5},{7,8},{8,7},{9,10},{10... | collective-permute-start | bytes 393224 | tf_op jit(solution)/shard_map/ppermute | solution.py:444
  29.8 6.7 %collective-permute-start.7 = (f32[16,16,128]{2,1,0:T(8,128)S(1)}, f32[16,16,128]{2,1,0:T(8,128)S(1)}, u32[]{:S(2)}, u32[]{:S(2)}) collective-permute-start(f32[16,16,128]{2,1,0:T(8,128)S(1)} %get-tuple-element.74), channel_id=1, source_target_pairs={{0,1},{1,0},{2,3},{3,2},{4,5},{5,4},{6,7},{7,6},{8,9},{9,8},{10,11... | collective-permute-start | bytes 393224 | tf_op jit(solution)/shard_map/ppermute | solution.py:445
  37.0 4.4 %collective-permute-start.10 = (f32[2,64,128]{2,1,0:T(8,128)S(1)}, f32[2,64,128]{2,1,0:T(8,128)S(1)}, u32[]{:S(2)}, u32[]{:S(2)}) collective-permute-start(f32[2,64,128]{2,1,0:T(8,128)S(1)} %get-tuple-element.82.refs_0_), channel_id=1, source_target_pairs={{0,128},{128,0},{1,129},{129,1},{2,130},{130,2},{3,131},{131,3},{4... | collective-permute-start | bytes 196616 | tf_op jit(solution)/shard_map/ppermute | solution.py:456
